TPU v7x, 128 devices: a whole 4x4x4 slice. The times are simulated.
128 devices in a mesh: gx: 8 (over y, core), gy: 16 (over x, z).
Axes of the slice: x: 4, y: 4, z: 4, core: 2. Of those that a mesh axis runs over, the one named last changes fastest.
Arguments:
- load: float32 [3, 72, 256, 128], P(None, 'gx', 'gy'), may hold values from -6 to 6
- plastic_flags: int32 [8, 72, 256, 128], P(None, 'gx', 'gy'), may hold values from 0 to 1, as said below
- flow_dir: float32 [6, 72, 256, 128], P(None, 'gx', 'gy'), may hold values from -1 to 1, as said below
- contact_flags: int32 [72, 256], P('gx', 'gy'), may hold values from 0 to 1, as said below
- die_depth: float32 [72, 256], P('gx', 'gy'), may hold values from -0.5 to -0.05
Outputs:
- displacement: float32 [3, 72, 256, 128], P(None, 'gx', 'gy')
- residual: float32 [3, 72, 256, 128], P(None, 'gx', 'gy')
Inputs may be any that keep to these rules, and one draw needn't show every extreme that they name: `plastic_flags`: 0 or 1 for each Gauss point. `contact_flags`: 0 or 1 for each top-face node. `flow_dir`: each element's six entries form a traceless tensor of unit norm, the off-diagonal entries counted twice in the norm.
All inputs are finite; a program needn't handle non-finite values.
Results may differ from a plain program's by a relative error of at most 0.0003.
Values sent between devices are 32-bit elements; how exact they have to be, the bound alone decides.
No kernel may reach another device: no remote copies, remote signals or barrier semaphores. Data moves between devices by JAX's collectives and lax.ppermute only.
A program may use at most 64 MiB of HBM per device.

v0:
```python
import math

import jax
import jax.numpy as jnp
from jax import lax
from jax.sharding import PartitionSpec as P

NEWTON = 2
CG_STEPS = 3


LAME_FIRST = 1.0
SHEAR_MOD = 1.0
PLASTIC_GAIN = 6.0 / 3.1
YIELD_OFFSET = 0.05
CONTACT_STIFF = 4.0
POINT_WEIGHT = 0.125
GAUSS_POINTS = (0.5 - 0.5 / math.sqrt(3.0), 0.5 + 0.5 / math.sqrt(3.0))
FLOW_SLOT = ((0, 3, 5), (3, 1, 4), (5, 4, 2))


def from_behind(value, axis, steps):
    count = lax.axis_size(axis)
    leading, last = (max(0, -steps), min(count, count - steps))
    return lax.ppermute(value, axis, [(source, source + steps) for source in range(leading, last)])


def lower_part(values, dimension):
    return lax.slice_in_dim(values, 0, values.shape[dimension] - 1, axis=dimension)


def upper_part(values, dimension):
    return lax.slice_in_dim(values, 1, values.shape[dimension], axis=dimension)


def blend_at(values, dimension, weight_at):
    return (1.0 - weight_at) * lower_part(values, dimension) + weight_at * upper_part(
        values, dimension
    )


def pad_pair(values, dimension):
    pad_before = [(0, 0)] * values.ndim
    pad_after = [(0, 0)] * values.ndim
    pad_before[dimension] = (1, 0)
    pad_after[dimension] = (0, 1)
    return (jnp.pad(values, pad_after), jnp.pad(values, pad_before))


def blend_back(values, dimension, weight_at):
    first, second = pad_pair(values, dimension)
    return (1.0 - weight_at) * first + weight_at * second


def spread(values, dimension):
    first, second = pad_pair(values, dimension)
    return second - first


def element_forces(node_values, plastic, flow_dir, element_mask, offset):
    slopes = [
        [upper_part(node_values[c], d) - lower_part(node_values[c], d) for d in range(3)]
        for c in range(3)
    ]
    totals = [[0.0, 0.0, 0.0] for c in range(3)]
    for i in range(2):
        for j in range(2):
            for k in range(2):
                point_x = GAUSS_POINTS[i]
                point_y = GAUSS_POINTS[j]
                point_z = GAUSS_POINTS[k]
                gradient = [
                    [
                        blend_at(blend_at(slopes[c][0], 1, point_y), 2, point_z),
                        blend_at(blend_at(slopes[c][1], 0, point_x), 2, point_z),
                        blend_at(blend_at(slopes[c][2], 0, point_x), 1, point_y),
                    ]
                    for c in range(3)
                ]
                strain = [
                    [
                        0.5 * (gradient[c][d] + gradient[d][c]) if c != d else gradient[c][c]
                        for d in range(3)
                    ]
                    for c in range(3)
                ]
                trace_sum = strain[0][0] + strain[1][1] + strain[2][2]
                normal_part = (
                    flow_dir[0] * strain[0][0]
                    + flow_dir[1] * strain[1][1]
                    + flow_dir[2] * strain[2][2]
                )
                normal_part = normal_part + 2.0 * (
                    flow_dir[3] * strain[0][1]
                    + flow_dir[4] * strain[1][2]
                    + flow_dir[5] * strain[2][0]
                )
                return_size = PLASTIC_GAIN * plastic[4 * i + 2 * j + k] * (normal_part - offset)
                scaling = POINT_WEIGHT * element_mask
                stress = [[None] * 3 for c in range(3)]
                for c in range(3):
                    for d in range(c, 3):
                        entry = (
                            2.0 * SHEAR_MOD * strain[c][d] - return_size * flow_dir[FLOW_SLOT[c][d]]
                        )
                        if c == d:
                            entry = entry + LAME_FIRST * trace_sum
                        stress[c][d] = scaling * entry
                        stress[d][c] = stress[c][d]
                for c in range(3):
                    totals[c][0] = totals[c][0] + blend_back(
                        blend_back(stress[c][0], 2, point_z), 1, point_y
                    )
                    totals[c][1] = totals[c][1] + blend_back(
                        blend_back(stress[c][1], 2, point_z), 0, point_x
                    )
                    totals[c][2] = totals[c][2] + blend_back(
                        blend_back(stress[c][2], 1, point_y), 0, point_x
                    )
    return jnp.stack(
        [
            spread(totals[c][0], 0) + spread(totals[c][1], 1) + spread(totals[c][2], 2)
            for c in range(3)
        ]
    )


def add_contact(result, field, active):
    return result.at[2, :, :, -1].add(CONTACT_STIFF * active * field[2, :, :, -1])


def squares_sum(values):
    return lax.psum(jnp.sum(values * values), ("gx", "gy"))


def conjugate(right, operate):
    solution = jnp.zeros_like(right)
    remain = right
    direction = right
    norm_now = squares_sum(remain)
    for step in range(CG_STEPS):
        image = operate(direction)
        alpha = norm_now / lax.psum(jnp.sum(direction * image), ("gx", "gy"))
        solution = solution + alpha * direction
        remain = remain - alpha * image
        if step + 1 < CG_STEPS:
            norm_next = squares_sum(remain)
            direction = remain + norm_next / norm_now * direction
            norm_now = norm_next
    return solution


def body(load, plastic_flags, flow_dir, contact_flags, die_depth):
    rows_x = load.shape[1]
    rows_y = load.shape[2]
    depth = load.shape[3]
    plastic = plastic_flags.astype(jnp.float32)
    active = contact_flags.astype(jnp.float32)

    def send_back(forces_all):
        forces_all = forces_all[:, :, :, 1:]
        from_next_y = from_behind(forces_all[:, :, -1:], "gy", 1)
        merged = forces_all[:, :, :-1]
        merged = jnp.concatenate([merged[:, :, :1] + from_next_y, merged[:, :, 1:]], axis=2)
        from_next_x = from_behind(merged[:, -1:], "gx", 1)
        merged = merged[:, :-1]
        return jnp.concatenate([merged[:, :1] + from_next_x, merged[:, 1:]], axis=1)

    def operate(field):
        plane_x = from_behind(field[:, :1], "gx", -1)
        widened = jnp.concatenate([field, plane_x], axis=1)
        plane_y = from_behind(widened[:, :, :1], "gy", -1)
        widened = jnp.concatenate([widened, plane_y], axis=2)
        widened = jnp.pad(widened, ((0, 0), (0, 0), (0, 0), (1, 0)))
        result = send_back(element_forces(widened, plastic, flow_dir, 1.0, 0.0))
        return add_contact(result, field, active)

    zero_nodes = jnp.zeros((3, rows_x + 1, rows_y + 1, depth + 1), jnp.float32)
    offset_force = send_back(element_forces(zero_nodes, plastic, flow_dir, 1.0, YIELD_OFFSET))
    right_side = (load - offset_force).at[2, :, :, -1].add(CONTACT_STIFF * active * die_depth)
    displacement = jnp.zeros_like(load)
    for newton in range(NEWTON):
        if newton == 0:
            newton_residual = right_side
        else:
            newton_residual = right_side - operate(displacement)
        displacement = displacement + conjugate(newton_residual, operate)
    return (displacement, right_side - operate(displacement))


def solution(mesh):
    in_specs = (
        P(None, "gx", "gy", None),
        P(None, "gx", "gy", None),
        P(None, "gx", "gy", None),
        P("gx", "gy"),
        P("gx", "gy"),
    )
    out_specs = (P(None, "gx", "gy", None), P(None, "gx", "gy", None))
    return jax.shard_map(body, mesh=mesh, in_specs=in_specs, out_specs=out_specs, check_vma=False)
```

profile of v0, /device:TPU:1, one launch (start us, length us, event | category | flops | bytes accessed | tf_op | source)
XLA Modules:
  0.0 941.1 jit_solution(3213593529580090575)
XLA Ops:
  8.4 4.4 collective-permute-start
  13.9 4.6 collective-permute-start.1
  22.5 3.6 collective-permute-done.2
  27.6 3.5 collective-permute-done.3
  42.0 3.5 collective-permute-start.4
  46.6 3.7 collective-permute-start.5
  52.8 70.1 %all-reduce.2619 = (f32[]{:T(128)}, f32[]{:T(128)}) all-reduce(f32[]{:T(128)} %get-tuple-element.139, f32[]{:T(128)} %get-tuple-element.138), channel_id=1, replica_groups=mesh['gx'=8,'gy'=16] {'gx','gy'}, use_global_device_ids=true, to_apply=%region_1.2 | all-reduce | flops 2 | bytes 16 | tf_op jit(solution)/shard_map/psum | solution.py:133
  124.9 62.5 %psum.86 = f32[]{:T(128)} all-reduce(f32[]{:T(128)} %get-tuple-element.566), channel_id=1, replica_groups=mesh['gx'=8,'gy'=16] {'gx','gy'}, use_global_device_ids=true, to_apply=%region_5.6 | all-reduce | flops 1 | bytes 8 | tf_op jit(solution)/shard_map/psum | solution.py:133
  213.2 3.9 collective-permute-start.9
  219.6 67.0 %psum.87 = f32[]{:T(128)} all-reduce(f32[]{:T(128)} %multiply_reduce_fusion.8), channel_id=1, replica_groups=mesh['gx'=8,'gy'=16] {'gx','gy'}, use_global_device_ids=true, to_apply=%region_7.8 | all-reduce | flops 1 | bytes 8 | tf_op jit(solution)/shard_map/psum | solution.py:143
  288.6 62.5 %psum.88 = f32[]{:T(128)} all-reduce(f32[]{:T(128)} %multiply_reduce_fusion.7), channel_id=1, replica_groups=mesh['gx'=8,'gy'=16] {'gx','gy'}, use_global_device_ids=true, to_apply=%region_9.10 | all-reduce | flops 1 | bytes 8 | tf_op jit(solution)/shard_map/psum | solution.py:133
  359.4 3.0 collective-permute-done.11
  376.9 3.9 collective-permute-start.13
  383.3 67.0 %psum.89 = f32[]{:T(128)} all-reduce(f32[]{:T(128)} %multiply_reduce_fusion.6), channel_id=1, replica_groups=mesh['gx'=8,'gy'=16] {'gx','gy'}, use_global_device_ids=true, to_apply=%region_11.12 | all-reduce | flops 1 | bytes 8 | tf_op jit(solution)/shard_map/psum | solution.py:143
  451.7 3.0 collective-permute-start.14
  458.4 3.0 collective-permute-done.15
  474.9 3.6 collective-permute-start.17
  482.3 3.8 collective-permute-done.18
  487.8 3.3 collective-permute-done.19
  501.9 4.1 collective-permute-start.20
  507.1 3.6 collective-permute-start.21
  513.2 69.2 %all-reduce.2618 = (f32[]{:T(128)}, f32[]{:T(128)}) all-reduce(f32[]{:T(128)} %get-tuple-element.137, f32[]{:T(128)} %get-tuple-element.136), channel_id=1, replica_groups=mesh['gx'=8,'gy'=16] {'gx','gy'}, use_global_device_ids=true, to_apply=%region_13.14 | all-reduce | flops 2 | bytes 16 | tf_op jit(solution)/shard_map/psum | solution.py:133
  584.4 63.3 %psum.92 = f32[]{:T(128)} all-reduce(f32[]{:T(128)} %get-tuple-element.324), channel_id=1, replica_groups=mesh['gx'=8,'gy'=16] {'gx','gy'}, use_global_device_ids=true, to_apply=%region_17.18 | all-reduce | flops 1 | bytes 8 | tf_op jit(solution)/shard_map/psum | solution.py:133
  655.7 3.0 collective-permute-done.23
  672.7 3.9 collective-permute-start.25
  679.1 67.0 %psum.93 = f32[]{:T(128)} all-reduce(f32[]{:T(128)} %multiply_reduce_fusion.2), channel_id=1, replica_groups=mesh['gx'=8,'gy'=16] {'gx','gy'}, use_global_device_ids=true, to_apply=%region_19.20 | all-reduce | flops 1 | bytes 8 | tf_op jit(solution)/shard_map/psum | solution.py:143
  748.2 62.5 %psum.94 = f32[]{:T(128)} all-reduce(f32[]{:T(128)} %multiply_reduce_fusion.1), channel_id=1, replica_groups=mesh['gx'=8,'gy'=16] {'gx','gy'}, use_global_device_ids=true, to_apply=%region_21.22 | all-reduce | flops 1 | bytes 8 | tf_op jit(solution)/shard_map/psum | solution.py:133
  818.8 3.0 collective-permute-done.27
  836.4 3.9 collective-permute-start.29
  842.8 67.1 %psum.95 = f32[]{:T(128)} all-reduce(f32[]{:T(128)} %multiply_reduce_fusion), channel_id=1, replica_groups=mesh['gx'=8,'gy'=16] {'gx','gy'}, use_global_device_ids=true, to_apply=%region_23.24 | all-reduce | flops 1 | bytes 8 | tf_op jit(solution)/shard_map/psum | solution.py:143
  911.3 3.0 collective-permute-start.30
  934.6 3.6 collective-permute-start.33
  (1118 shorter events, 182.4 us)
Async XLA Ops:
  8.4 5.2 collective-permute-start
  13.9 5.6 collective-permute-start.1
  20.5 5.6 collective-permute-start.2
  26.1 5.0 collective-permute-start.3
  42.0 4.4 collective-permute-start.4
  46.6 4.7 collective-permute-start.5
  188.8 5.1 collective-permute-start.6
  194.0 4.5 collective-permute-start.7
  209.3 3.7 collective-permute-start.8
  213.2 4.9 collective-permute-start.9
  352.5 5.4 collective-permute-start.10
  358.0 4.5 collective-permute-start.11
  373.2 3.4 collective-permute-start.12
  376.9 4.9 collective-permute-start.13
  451.7 5.1 collective-permute-start.14
  456.9 4.5 collective-permute-start.15
  474.9 4.6 collective-permute-start.17
  480.4 5.7 collective-permute-start.18
  486.1 5.0 collective-permute-start.19
  501.9 4.9 collective-permute-start.20
  507.1 4.6 collective-permute-start.21
  649.1 5.1 collective-permute-start.22
  654.2 4.5 collective-permute-start.23
  669.5 2.9 collective-permute-start.24
  672.7 4.9 collective-permute-start.25
  812.1 5.2 collective-permute-start.26
  817.3 4.5 collective-permute-start.27
  832.6 3.6 collective-permute-start.28
  836.4 4.9 collective-permute-start.29
  911.3 5.1 collective-permute-start.30
  916.5 4.5 collective-permute-start.31
  934.6 4.6 collective-permute-start.33
  (7 other events, 38.6 us)
where the time goes:
time: 952 us; the launch traced here: 941 us
  blocking collectives  658 us (69%)
  other arithmetic  98.9 us (10%)
  starting transfers between devices  92.7 us (10%)
  waiting for transfers between devices  60.3 us (6%)
  between operations  21.3 us (2%)
  local copies, waits for them, and re-layouts  9.68 us (1%)
    psum x6, blocking collectives, squares_sum(): return lax.psum(jnp.sum(values * values), ('gx', 'gy'))  390 us
    psum x4, blocking collectives, conjugate(): alpha = norm_now / lax.psum(jnp.sum(direction * image), ('gx', 'gy'))  268 us
    ppermute x34, starting transfers between devices, from_behind(): lax.ppermute(value, axis, [(source, source + steps) for source in range(l...  92.7 us
    ppermute x34, waiting for transfers between devices, from_behind(): lax.ppermute(value, axis, [(source, source + steps) for source in range(l...  60.3 us
    add x544, other arithmetic, blend_back(): return (1.0 - weight_at) * first + weight_at * second  39.6 us
  transfers between devices with their start and end apart: 34, of which 34 were waited for; matrix products, arithmetic and copies ran while one was open for 0% of the time, Pallas kernels for 0%

commit v1 on v0

v1 whole, which is shorter than its diff:
```python
import math

import jax
import jax.numpy as jnp
from jax import lax
from jax.experimental import pallas as pl
from jax.experimental.pallas import tpu as pltpu
from jax.sharding import PartitionSpec as P

PLASTIC_GAIN = 6.0 / 3.1
YIELD_OFFSET = 0.05
CONTACT_STIFF = 4.0
CG_STEPS = 3
NEWTON = 2
ROOT_THIRD = 1.0 / math.sqrt(3.0)
THIRD = 1.0 / 3.0
SPAN = 10.0

HALO = 3
OX, OY, DZ = 9, 16, 128
WX = OX + 2 * HALO
WE = WX - 1
WY = 24
F32 = jnp.float32

FLOW_SENT = (0, 1, 3, 4, 5)
NEL = 14
CONTACT_AT = 13
ZZ_AT = 14


def lanes():
    return lax.broadcasted_iota(jnp.int32, (8, DZ), 1)


def z_pair(value, first_lane):
    low = jnp.where(first_lane, 0.0, pltpu.roll(value, 1, 1))
    return value + low, value - low


def z_merge(total, slope, last_lane):
    return total + slope + jnp.where(last_lane, 0.0, pltpu.roll(total - slope, DZ - 1, 1))


def to_points(s1, sx, sy, sz, syz, sxz, sxy):
    points = []
    for sign_x in (-1, 1):
        a0 = s1 + sx if sign_x > 0 else s1 - sx
        ay = sy + sxy if sign_x > 0 else sy - sxy
        az = sz + sxz if sign_x > 0 else sz - sxz
        for sign_y in (-1, 1):
            b0 = a0 + ay if sign_y > 0 else a0 - ay
            bz = az + syz if sign_y > 0 else az - syz
            points += [b0 - bz, b0 + bz]
    return points


def from_points(t):
    per_x = []
    for i in range(2):
        e0 = [t[4 * i + 2 * j + 1] + t[4 * i + 2 * j] for j in range(2)]
        ez = [t[4 * i + 2 * j + 1] - t[4 * i + 2 * j] for j in range(2)]
        per_x.append((e0[1] + e0[0], e0[1] - e0[0], ez[1] + ez[0], ez[1] - ez[0]))
    low, high = per_x
    t1, ty, tz, tyz = (high[m] + low[m] for m in range(4))
    tx, txy, txz = (high[m] - low[m] for m in range(3))
    return t1, tx, ty, tz, tyz, txz, txy


def plastic_forces(n, t):
    nxx, nyy, nzz, nxy, nyz, nzx = n
    t1, tx, ty, tz, tyz, txz, txy = t
    tx, ty, tz = tx * ROOT_THIRD, ty * ROOT_THIRD, tz * ROOT_THIRD
    tyz, txz, txy = tyz * THIRD, txz * THIRD, txy * THIRD
    a_xy, a_yz, a_zx = nxy * t1, nyz * t1, nzx * t1
    fx = [nxx * t1, a_xy, a_zx]
    fy = [a_xy, nyy * t1, a_yz]
    fz = [a_zx, a_yz, nzz * t1]
    xy_z, yz_x, zx_y = nxy * tz, nyz * tx, nzx * ty
    fxy = [nxx * ty + nxy * tx, nxy * ty + nyy * tx, zx_y + yz_x]
    fxz = [nxx * tz + nzx * tx, xy_z + yz_x, nzx * tz + nzz * tx]
    fyz = [xy_z + zx_y, nyy * tz + nyz * ty, nyz * tz + nzz * ty]
    fxyz = [
        nxx * tyz + nxy * txz + nzx * txy,
        nxy * tyz + nyy * txz + nyz * txy,
        nzx * tyz + nyz * txz + nzz * txy,
    ]
    return fx, fy, fz, fxy, fxz, fyz, fxyz


def element_core(modes, n, flags):
    ax, ay, az, axy, axz, ayz, axyz = modes
    nxx, nyy, nzz, nxy, nyz, nzx = n
    sh_xy, sh_yz, sh_zx = ax[1] + ay[0], ay[2] + az[1], az[0] + ax[2]
    k_x, k_y, k_z = axy[2] + axz[1], axy[2] + ayz[0], axz[1] + ayz[0]
    s1 = (nxx * ax[0] + nyy * ay[1] + nzz * az[2]) + (nxy * sh_xy + nyz * sh_yz + nzx * sh_zx)
    sx = (nxy * axy[0] + nyy * axy[1]) + (nyz * k_x + nzx * axz[0] + nzz * axz[2])
    sy = (nxx * axy[0] + nxy * axy[1]) + (nzx * k_y + nyz * ayz[1] + nzz * ayz[2])
    sz = (nxx * axz[0] + nxy * k_z) + (nzx * axz[2] + nyy * ayz[1] + nyz * ayz[2])
    syz = nxx * axyz[0] + nxy * axyz[1] + nzx * axyz[2]
    sxz = nxy * axyz[0] + nyy * axyz[1] + nyz * axyz[2]
    sxy = nzx * axyz[0] + nyz * axyz[1] + nzz * axyz[2]
    values = to_points(
        s1, sx * ROOT_THIRD, sy * ROOT_THIRD, sz * ROOT_THIRD, syz * THIRD, sxz * THIRD, sxy * THIRD
    )
    plastic = plastic_forces(n, from_points([value * flag for value, flag in zip(values, flags)]))
    trace = ax[0] + ay[1] + az[2]
    tr_x, tr_y, tr_z = (
        (axy[1] + axz[2]) * THIRD,
        (axy[0] + ayz[2]) * THIRD,
        (axz[0] + ayz[1]) * THIRD,
    )
    mixed = (k_x + ayz[0]) * THIRD
    elastic = (
        [trace + (ax[0] + ax[0]), sh_xy, sh_zx],
        [sh_xy, trace + (ay[1] + ay[1]), sh_yz],
        [sh_zx, sh_yz, trace + (az[2] + az[2])],
        [tr_y + axy[0], tr_x + axy[1], mixed + axy[2] * THIRD],
        [tr_z + axz[0], mixed + axz[1] * THIRD, tr_x + axz[2]],
        [mixed + ayz[0] * THIRD, tr_z + ayz[1], tr_y + ayz[2]],
        [axyz[c] * (5.0 / 9.0) for c in range(3)],
    )
    return [[elastic[m][c] + plastic[m][c] for c in range(3)] for m in range(7)]


def scatter_x(forces, behind):
    fx, fy, fz, fxy, fxz, fyz, fxyz = forces
    node, ahead = [], []
    for c in range(3):
        node += [
            behind[4 * c] - fx[c],
            behind[4 * c + 1] + (fy[c] - fxy[c]),
            behind[4 * c + 2] + (fz[c] - fxz[c]),
            behind[4 * c + 3] + (fyz[c] - fxyz[c]),
        ]
        ahead += [fx[c], fy[c] + fxy[c], fz[c] + fxz[c], fyz[c] + fxyz[c]]
    return node, ahead


def store_y(node, lower_ref, upper_ref, x, row, upper_keep=None):
    for c in range(3):
        ss, sd, ds, dd = node[4 * c : 4 * c + 4]
        lower_ref[2 * c, x, row : row + 8] = ss - sd
        lower_ref[2 * c + 1, x, row : row + 8] = ds - dd
        up_s, up_d = ss + sd, ds + dd
        if upper_keep is not None:
            up_s, up_d = jnp.where(upper_keep, up_s, 0.0), jnp.where(upper_keep, up_d, 0.0)
        upper_ref[2 * c, x, row + 8 : row + 16] = up_s
        upper_ref[2 * c + 1, x, row + 8 : row + 16] = up_d


def merge_yz(lower_ref, upper_ref, c, x, row, last_lane):
    total = lower_ref[2 * c, x, row : row + 8] + upper_ref[2 * c, x, row + 7 : row + 15]
    slope = lower_ref[2 * c + 1, x, row : row + 8] + upper_ref[2 * c + 1, x, row + 7 : row + 15]
    return z_merge(total, slope, last_lane)


def place():
    index_x, index_y = lax.axis_index("gx"), lax.axis_index("gy")
    return (
        index_x == 0,
        index_x == lax.axis_size("gx") - 1,
        index_y == 0,
        index_y == lax.axis_size("gy") - 1,
    )


def ask(flag):
    return jnp.where(flag, 0.0, 1.0).astype(F32)


def offset_kernel(load_ref, flags_ref, flow_ref, contact_ref, die_ref,
                  part_ref, right_ref, left_ref, up_ref, down_ref, lower_ref, upper_ref):
    lane = lanes()
    last_lane = lane == DZ - 1
    zero = jnp.zeros((8, DZ), F32)

    def clear(x, _):
        for m in range(6):
            lower_ref[m, x, 16:24] = zero
            upper_ref[m, x, 0:8] = zero
        return 0

    lax.fori_loop(0, OX + 1, clear, 0)
    for row in (0, 8):

        def element(x, behind):
            flags = [flags_ref[q, x, row : row + 8].astype(F32) * (0.5 * PLASTIC_GAIN * YIELD_OFFSET) for q in range(8)]
            n = [flow_ref[m, x, row : row + 8] for m in range(6)]
            node, ahead = scatter_x(plastic_forces(n, from_points(flags)), behind)
            store_y(node, lower_ref, upper_ref, x, row)
            return ahead

        behind = lax.fori_loop(0, OX, element, [zero] * 12)
        store_y(behind, lower_ref, upper_ref, OX, row)

    def finish(x, _):
        for c in range(3):
            for row in (0, 8, 16):
                part_ref[c, x, row : row + 8] = merge_yz(lower_ref, upper_ref, c, x, row, last_lane) * (-1.0 / 16.0)
        return 0

    lax.fori_loop(0, OX + 1, finish, 0)

    def add_load(x, _):
        for c in range(3):
            for row in (0, 8):
                value = part_ref[c, x, row : row + 8] + load_ref[c, x, row : row + 8]
                if c == 2:
                    value = value + die_ref[x, row : row + 8]
                part_ref[c, x, row : row + 8] = value
        return 0

    lax.fori_loop(0, OX, add_load, 0)

    def field(f, x, rows):
        if f < 8:
            return flags_ref[f, x, rows].astype(F32) * (-PLASTIC_GAIN / 8.0)
        if f < CONTACT_AT:
            return flow_ref[FLOW_SENT[f - 8], x, rows]
        return contact_ref[x, rows]

    whole = slice(0, OY)
    for f in range(NEL):
        for i in range(3):
            right_ref[3 * f + i] = field(f, 6 + i, whole)
        for i in range(2):
            left_ref[2 * f + i] = field(f, i, whole)
    for c in range(3):
        for i in range(4):
            right_ref[42 + 4 * c + i] = part_ref[c, 6 + i, 0:16]
            right_ref[54, 4 * c + i : 4 * c + i + 1] = part_ref[c, 6 + i, 16:17]
        for i in range(3):
            left_ref[28 + 3 * c + i] = part_ref[c, i, 0:16]
            left_ref[37, 3 * c + i : 3 * c + i + 1] = part_ref[c, i, 16:17]

    def slabs(x, _):
        for f in range(NEL):
            up_ref[x, 3 * f : 3 * f + 3] = field(f, x, slice(13, 16))
            down_ref[x, 2 * f : 2 * f + 2] = field(f, x, slice(0, 2))
        return 0

    lax.fori_loop(0, OX, slabs, 0)

    def part_slabs(x, _):
        for c in range(3):
            up_ref[x, 42 + 4 * c : 46 + 4 * c] = part_ref[c, x, 13:17]
            down_ref[x, 28 + 3 * c : 31 + 3 * c] = part_ref[c, x, 0:3]
        return 0

    lax.fori_loop(0, OX + 1, part_slabs, 0)


def three_steps(els_ref, basis, z_ref, lower_ref, upper_ref):
    at_first_x, at_last_x, at_first_y, at_last_y = place()
    lane = lanes()
    first_lane, last_lane = lane == 0, lane == DZ - 1
    rows = lax.broadcasted_iota(jnp.int32, (8, DZ), 0)
    keep_upper = jnp.logical_or(rows >= HALO, jnp.logical_not(at_first_y))
    keep_node = jnp.logical_or(rows < HALO, jnp.logical_not(at_last_y))
    zero = jnp.zeros((8, DZ), F32)

    def clear(x, _):
        for m in range(6):
            z_ref[m, x, 24:32] = zero
            upper_ref[m, x, 0:8] = zero
        return 0

    lax.fori_loop(0, WX, clear, 0)

    def first(x, _):
        for row in (0, 8, 16):
            for c in range(3):
                z_ref[2 * c, x, row : row + 8], z_ref[2 * c + 1, x, row : row + 8] = z_pair(
                    basis[0][c, x, row : row + 8], first_lane
                )
        return 0

    lax.fori_loop(0, WX, first, 0)

    for step in range(1, HALO + 1):
        start = jnp.where(at_first_x, HALO, step - 1)
        end = jnp.where(at_last_x, HALO + OX - 1, WX - 1 - step)
        for row in (0, 8, 16):

            def plane(x):
                values = []
                for m in range(6):
                    low, high = z_ref[m, x, row : row + 8], z_ref[m, x, row + 1 : row + 9]
                    values += [high + low, high - low]
                return values

            def element(x, carry):
                before, behind = carry
                after = plane(x + 1)
                p, q = before, after
                modes = (
                    [q[4 * c] - p[4 * c] for c in range(3)],
                    [q[4 * c + 1] + p[4 * c + 1] for c in range(3)],
                    [q[4 * c + 2] + p[4 * c + 2] for c in range(3)],
                    [q[4 * c + 1] - p[4 * c + 1] for c in range(3)],
                    [q[4 * c + 2] - p[4 * c + 2] for c in range(3)],
                    [q[4 * c + 3] + p[4 * c + 3] for c in range(3)],
                    [q[4 * c + 3] - p[4 * c + 3] for c in range(3)],
                )
                here = [els_ref[f, x, row : row + 8] for f in range(NEL + 1) if f != CONTACT_AT]
                n = (here[8], here[9], here[13], here[10], here[11], here[12])
                node, ahead = scatter_x(element_core(modes, n, here[:8]), behind)
                store_y(node, lower_ref, upper_ref, x, row, keep_upper if row == 0 else None)
                return after, ahead

            lax.fori_loop(start, end + 1, element, (plane(start), [zero] * 12))

        node_start = jnp.where(at_first_x, HALO, step)
        scale = (2.0 if step == 1 else 4.0) / SPAN

        def finish(x, _):
            for row in (0, 8, 16):
                for c in range(3):
                    here = basis[step - 1][c, x, row : row + 8]
                    value = merge_yz(lower_ref, upper_ref, c, x, row, last_lane) * (scale / 16.0)
                    if c == 2:
                        value = value + (els_ref[CONTACT_AT, x, row : row + 8] * scale) * here
                    if step == 1:
                        value = value - here
                    else:
                        value = value - (here + here) - basis[step - 2][c, x, row : row + 8]
                    if row == 16:
                        value = jnp.where(keep_node, value, 0.0)
                    basis[step][c, x, row : row + 8] = value
                    if step < HALO:
                        z_ref[2 * c, x, row : row + 8], z_ref[2 * c + 1, x, row : row + 8] = z_pair(value, first_lane)
            return 0

        lax.fori_loop(node_start, end + 1, finish, 0)


def sum_rows(values):
    return jnp.sum(values, axis=0, keepdims=True)


def first_kernel(flags_ref, flow_ref, contact_ref, part_ref, left_ref, right_ref, down_ref, up_ref, cl_ref, cr_ref,
                 els_ref, own_ref, dots_ref, right_out, left_out, up_out, down_out,
                 b0, b1, b2, b3, z_ref, lower_ref, upper_ref):
    at_first_x, at_last_x, at_first_y, at_last_y = place()
    has_l, has_r, has_d, has_u = ask(at_first_x), ask(at_last_x), ask(at_first_y), ask(at_last_y)
    zero = jnp.zeros((8, DZ), F32)
    low, high = slice(0, 3), slice(19, 21)
    mid = slice(HALO, HALO + OY)

    def clear(x, _):
        for f in range(NEL):
            els_ref[f, x, 16:24] = zero
        return 0

    lax.fori_loop(0, WE, clear, 0)

    def clear_start(x, _):
        for c in range(3):
            for row in (0, 8, 16):
                b0[c, x, row : row + 8] = zero
        return 0

    lax.fori_loop(0, WX, clear_start, 0)

    def own(x, _):
        w = x + HALO
        for f in range(NEL):
            if f < 8:
                value = flags_ref[f, x].astype(F32) * (-PLASTIC_GAIN / 8.0)
            elif f < CONTACT_AT:
                value = flow_ref[FLOW_SENT[f - 8], x]
            else:
                value = contact_ref[x]
            els_ref[f, w, mid] = value
            els_ref[f, w, low] = down_ref[x, 3 * f : 3 * f + 3]
            els_ref[f, w, high] = up_ref[x, 2 * f : 2 * f + 2]
        for c in range(3):
            b0[c, w, mid] = part_ref[c, x, 0:16]
            b0[c, w, 19:20] = part_ref[c, x, 16:17] * has_u
        return 0

    lax.fori_loop(0, OX, own, 0)
    for c in range(3):
        b0[c, 12, mid] = part_ref[c, OX, 0:16] * has_r
        b0[c, 12, 19:20] = part_ref[c, OX, 16:17] * (has_r * has_u)
    for i in range(3):
        for f in range(NEL):
            els_ref[f, i, mid] = left_ref[3 * f + i]
            els_ref[f, i, low] = cl_ref[i, 3 * f : 3 * f + 3]
            els_ref[f, i, high] = cl_ref[i, 56 + 2 * f : 58 + 2 * f]
    for i in range(2):
        for f in range(NEL):
            els_ref[f, 12 + i, mid] = right_ref[2 * f + i]
            els_ref[f, 12 + i, low] = cr_ref[i, 3 * f : 3 * f + 3]
            els_ref[f, 12 + i, high] = cr_ref[i, 56 + 2 * f : 58 + 2 * f]

    def zz(x, _):
        for row in (0, 8, 16):
            els_ref[ZZ_AT, x, row : row + 8] = -(els_ref[8, x, row : row + 8] + els_ref[9, x, row : row + 8])
        return 0

    lax.fori_loop(0, WE, zz, 0)

    for c in range(3):
        for i in range(4):
            b0[c, i, mid] += left_ref[42 + 4 * c + i] * has_l
            b0[c, i, 19:20] += left_ref[54, 4 * c + i : 4 * c + i + 1] * (has_l * has_u)
            b0[c, i, 0:4] += cl_ref[i, 42 + 4 * c : 46 + 4 * c] * (has_l * has_d)
            b0[c, i, 19:22] += cl_ref[i, 84 + 3 * c : 87 + 3 * c] * (has_l * has_u)
        for i in range(3):
            b0[c, 12 + i, mid] += right_ref[28 + 3 * c + i] * has_r
            b0[c, 12 + i, 19:20] += right_ref[37, 3 * c + i : 3 * c + i + 1] * (has_r * has_u)
            b0[c, 12 + i, 0:4] += cr_ref[i, 42 + 4 * c : 46 + 4 * c] * (has_r * has_d)
            b0[c, 12 + i, 19:22] += cr_ref[i, 84 + 3 * c : 87 + 3 * c] * (has_r * has_u)

    def edges(x, _):
        inside = jnp.where(x == OX, has_r, 1.0)
        for c in range(3):
            b0[c, x + HALO, 0:4] += down_ref[x, 42 + 4 * c : 46 + 4 * c] * (inside * has_d)
            b0[c, x + HALO, 19:22] += up_ref[x, 28 + 3 * c : 31 + 3 * c] * (inside * has_u)
        return 0

    lax.fori_loop(0, OX + 1, edges, 0)

    basis = (b0, b1, b2, b3)
    three_steps(els_ref, basis, z_ref, lower_ref, upper_ref)

    def collect(x, sums):
        sums = list(sums)
        for row in (0, 8):
            for c in range(3):
                v = [b[c, x + HALO, row + HALO : row + HALO + 8] for b in basis]
                for k in range(4):
                    own_ref[k, c, x, row : row + 8] = v[k]
                for k in range(7):
                    sums[k] = sums[k] + v[k // 2] * v[k - k // 2]
        return tuple(sums)

    sums = lax.fori_loop(0, OX, collect, (zero,) * 7)
    dots_ref[...] = zero
    for k in range(7):
        dots_ref[k : k + 1] = sum_rows(sums[k])

    for c in range(3):
        for i in range(3):
            right_out[3 * c + i] = b3[c, 9 + i, mid]
            left_out[3 * c + i] = b3[c, 3 + i, mid]

    def slabs(x, _):
        for c in range(3):
            up_out[x, 3 * c : 3 * c + 3] = b3[c, x + HALO, 16:19]
            down_out[x, 3 * c : 3 * c + 3] = b3[c, x + HALO, 3:6]
        return 0

    lax.fori_loop(0, OX, slabs, 0)


def second_kernel(els_ref, own_ref, left_ref, right_ref, down_ref, up_ref, cl_ref, cr_ref,
                  tail_ref, dots_ref, b0, b1, b2, b3, z_ref, lower_ref, upper_ref):
    _, at_last_x, _, at_last_y = place()
    has_r, has_u = ask(at_last_x), ask(at_last_y)
    zero = jnp.zeros((8, DZ), F32)
    mid = slice(HALO, HALO + OY)

    def own(x, _):
        w = x + HALO
        for c in range(3):
            b0[c, w, 16:24] = zero
            b0[c, w, mid] = own_ref[3, c, x]
            b0[c, w, 0:3] = down_ref[x, 3 * c : 3 * c + 3]
            b0[c, w, 19:22] = up_ref[x, 3 * c : 3 * c + 3] * has_u
        return 0

    lax.fori_loop(0, OX, own, 0)
    for c in range(3):
        for i in range(3):
            b0[c, i, 16:24] = zero
            b0[c, i, mid] = left_ref[3 * c + i]
            b0[c, i, 0:3] = cl_ref[i, 3 * c : 3 * c + 3]
            b0[c, i, 19:22] = cl_ref[i, 16 + 3 * c : 19 + 3 * c] * has_u
            b0[c, 12 + i, 16:24] = zero
            b0[c, 12 + i, mid] = right_ref[3 * c + i] * has_r
            b0[c, 12 + i, 0:3] = cr_ref[i, 3 * c : 3 * c + 3] * has_r
            b0[c, 12 + i, 19:22] = cr_ref[i, 16 + 3 * c : 19 + 3 * c] * (has_r * has_u)

    basis = (b0, b1, b2, b3)
    three_steps(els_ref, basis, z_ref, lower_ref, upper_ref)

    def collect(x, sums):
        sums = list(sums)
        for row in (0, 8):
            for c in range(3):
                v = [own_ref[3, c, x, row : row + 8]]
                for k in range(1, 4):
                    w = b_at(basis[k], c, x, row)
                    v.append((w + w) - own_ref[3 - k, c, x, row : row + 8])
                    tail_ref[k - 1, c, x, row : row + 8] = v[k]
                for k in range(1, 6):
                    sums[k - 1] = sums[k - 1] + v[k // 2] * v[k - k // 2]
        return tuple(sums)

    sums = lax.fori_loop(0, OX, collect, (zero,) * 5)
    dots_ref[...] = zero
    for k in range(5):
        dots_ref[k : k + 1] = sum_rows(sums[k])


def b_at(ref, c, x, row):
    return ref[c, x + HALO, row + HALO : row + HALO + 8]


def times_matrix(p):
    out = [None] * (len(p) + 1)

    def add(k, value):
        out[k] = value if out[k] is None else out[k] + value

    for k, value in enumerate(p):
        add(k, value * (SPAN / 2))
        if k == 0:
            add(1, value * (SPAN / 2))
        else:
            add(k + 1, value * (SPAN / 4))
            add(k - 1, value * (SPAN / 4))
    return out


def tree_sum(values):
    while len(values) > 1:
        values = [a + b for a, b in zip(values[::2], values[1::2])] + ([values[-1]] if len(values) % 2 else [])
    return values[0]


def combine(p, a, q):
    out = []
    for k in range(max(len(p), len(q))):
        term = a * q[k] if k < len(q) else None
        if k < len(p):
            term = p[k] if term is None else p[k] + term
        out.append(term)
    return out


def coefficients(mu):
    gram = [[0.5 * (mu[i + j] + mu[abs(i - j)]) if i + j < len(mu) else None for j in range(7)] for i in range(7)]

    def inner(p, q):
        return tree_sum([p[i] * tree_sum([gram[i][j] * q[j] for j in range(len(q))]) for i in range(len(p))])

    remain = [jnp.ones_like(mu[0])]
    total = []
    for newton in range(NEWTON):
        direction = remain
        norm = inner(remain, remain)
        for step in range(CG_STEPS):
            image = times_matrix(direction)
            alpha = norm / inner(direction, image)
            total = combine(total, alpha, direction)
            remain = combine(remain, -alpha, image)
            if step + 1 < CG_STEPS:
                norm_next = inner(remain, remain)
                direction = combine(remain, norm_next / norm, direction)
                norm = norm_next
    return total, remain


def last_kernel(dots_ref, own_ref, tail_ref, displacement_ref, residual_ref):
    sums = jnp.broadcast_to(jnp.sum(dots_ref[...], axis=1, keepdims=True), (16, DZ))
    dots = [sums[k : k + 1] for k in range(7)] + [sums[8 + k : 9 + k] for k in range(5)]
    mu = dots[:2]
    for k in range(2, 12):
        mu.append((dots[k] + dots[k]) - mu[k % 2])
    total, remain = coefficients(mu)
    total = [jnp.broadcast_to(value, (8, DZ)) for value in total]
    remain = [jnp.broadcast_to(value, (8, DZ)) for value in remain]

    def write(x, _):
        for row in (0, 8):
            for c in range(3):
                v = [own_ref[k, c, x, row : row + 8] for k in range(4)]
                v += [tail_ref[k, c, x, row : row + 8] for k in range(3)]
                displacement_ref[c, x, row : row + 8] = tree_sum([a * b for a, b in zip(total, v)])
                residual_ref[c, x, row : row + 8] = tree_sum([a * b for a, b in zip(remain, v)])
        return 0

    lax.fori_loop(0, OX, write, 0)


def shape(*dims):
    return jax.ShapeDtypeStruct(dims, F32)


def call(kernel, outs, scratch=()):
    return pl.pallas_call(
        kernel,
        out_shape=outs,
        scratch_shapes=[pltpu.VMEM(dims, F32) for dims in scratch],
        compiler_params=pltpu.CompilerParams(vmem_limit_bytes=48 * 1024 * 1024),
    )


STEP_SCRATCH = [(3, WX, WY, DZ)] * 4 + [(6, WX, WY + 8, DZ)] * 3


def rotate(value, axis, steps):
    count = lax.axis_size(axis)
    return lax.ppermute(value, axis, [(i, (i + steps) % count) for i in range(count)])


def exchange(right, left, up, down, top):
    from_left = rotate(right, "gx", 1)
    from_right = rotate(left, "gx", -1)
    from_down = rotate(up, "gy", 1)
    from_up = rotate(down, "gy", -1)
    corners = jnp.concatenate([from_down, from_up], axis=1)
    corner_left = rotate(corners[6:top], "gx", 1)
    corner_right = rotate(corners[0:3], "gx", -1)
    return from_left, from_right, from_down, from_up, corner_left, corner_right


def sum_everywhere(value):
    ring = [i ^ 1 for i in range(4)], [3 - i for i in range(4)]
    if (lax.axis_size("gx"), lax.axis_size("gy")) != (8, 16):
        return lax.psum(value, ("gx", "gy"))
    value = value + lax.ppermute(value, "gx", [(i, i ^ 1) for i in range(8)])
    for pairs in ring:
        value = value + lax.ppermute(value, "gx", [(2 * y + k, 2 * pairs[y] + k) for y in range(4) for k in range(2)])
    for pairs in ring:
        value = value + lax.ppermute(value, "gy", [(4 * x + z, 4 * x + pairs[z]) for x in range(4) for z in range(4)])
    for pairs in ring:
        value = value + lax.ppermute(value, "gy", [(4 * x + z, 4 * pairs[x] + z) for x in range(4) for z in range(4)])
    return value


def body(load, plastic_flags, flow_dir, contact_flags, die_depth):
    stiff = CONTACT_STIFF * contact_flags.astype(F32)
    at_top = lax.broadcasted_iota(jnp.int32, (OX, OY, DZ), 2) == DZ - 1
    contact = jnp.where(at_top, stiff[:, :, None], 0.0)
    die = jnp.where(at_top, (stiff * die_depth)[:, :, None], 0.0)

    part, right, left, up, down = call(
        offset_kernel,
        [shape(3, OX + 1, WY, DZ), shape(55, OY, DZ), shape(38, OY, DZ), shape(OX + 1, 56, DZ), shape(OX + 1, 40, DZ)],
        [(6, OX + 1, WY + 8, DZ)] * 2,
    )(load, plastic_flags, flow_dir, contact, die)
    halos = exchange(right, left, up, down, 10)
    els, own, dots, right, left, up, down = call(
        first_kernel,
        [shape(NEL + 1, WE, WY, DZ), shape(4, 3, OX, OY, DZ), shape(8, DZ), shape(9, OY, DZ), shape(9, OY, DZ),
         shape(OX, 16, DZ), shape(OX, 16, DZ)],
        STEP_SCRATCH,
    )(plastic_flags, flow_dir, contact, part, *halos)
    halos = exchange(right, left, up, down, 9)
    tail, dots_tail = call(
        second_kernel, [shape(3, 3, OX, OY, DZ), shape(8, DZ)], STEP_SCRATCH
    )(els, own, *halos)
    dots = sum_everywhere(jnp.concatenate([dots, dots_tail], axis=0))
    return tuple(call(last_kernel, [shape(3, OX, OY, DZ)] * 2)(dots, own, tail))


def solution(mesh):
    in_specs = (
        P(None, "gx", "gy", None),
        P(None, "gx", "gy", None),
        P(None, "gx", "gy", None),
        P("gx", "gy"),
        P("gx", "gy"),
    )
    out_specs = (P(None, "gx", "gy", None), P(None, "gx", "gy", None))
    return jax.shard_map(body, mesh=mesh, in_specs=in_specs, out_specs=out_specs, check_vma=False)
```

time: 952 us -> 93.8 us (0.10)
  the two profiles are of different devices: /device:TPU:1 before, /device:TPU:6 now
where the time goes in v1:
time: 93.8 us; the launch traced here: 93.5 us
  waiting for transfers between devices  33 us (35%)
  starting transfers between devices  28.5 us (30%)
  Pallas kernels  25.5 us (27%)
  local copies, waits for them, and re-layouts  4.83 us (5%)
    ppermute x12, starting transfers between devices, rotate(): lax.ppermute(value, axis, [(i, (i + steps) % count) for i in range(count)])  18 us
    ppermute x12, waiting for transfers between devices, rotate(): lax.ppermute(value, axis, [(i, (i + steps) % count) for i in range(count)])  13.3 us
    pallas_call x1, Pallas kernels, body(): call(first_kernel, [shape(NEL + 1, WE, WY, DZ), shape(4, 3, OX, OY, DZ),...  12.4 us
    pallas_call x1, Pallas kernels, body(): call(second_kernel, [shape(3, 3, OX, OY, DZ), shape(8, DZ)], STEP_SCRATCH)  10.2 us
    ppermute x2, waiting for transfers between devices, sum_everywhere(): lax.ppermute(value, 'gy', [(4 * x + z, 4 * pairs[x] + z) for x in range(4...  8.29 us
    ppermute x2, starting transfers between devices, sum_everywhere(): lax.ppermute(value, 'gy', [(4 * x + z, 4 * x + pairs[z]) for x in range(4...  7.35 us
    ppermute x2, waiting for transfers between devices, sum_everywhere(): lax.ppermute(value, 'gx', [(2 * y + k, 2 * pairs[y] + k) for y in range(4...  5.7 us
    unnamed x15, local copies, waits for them, and re-layouts  4.77 us
  transfers between devices with their start and end apart: 19, of which 13 were waited for; matrix products, arithmetic and copies ran while one was open for 0% of the time, Pallas kernels for 0%

profile of v1, /device:TPU:6, one launch (start us, length us, event | category | flops | bytes accessed | tf_op | source)
XLA Modules:
  0.0 93.5 jit_solution(1465291121433855585)
XLA Ops:
  0.6 0.7 fusion
  1.5 1.1 %copy-done.1 = s32[8,9,16,128]{3,2,1,0:T(8,128)S(1)} copy-done((s32[8,9,16,128]{3,2,1,0:T(8,128)S(1)}, s32[8,9,16,128]{3,2,1,0:T(8,128)}, u32[]{:S(2)}) %copy-start.1) | copy-done | bytes 589848
  2.5 1.0 %copy-done.3 = f32[6,9,16,128]{3,2,1,0:T(8,128)S(1)} copy-done((f32[6,9,16,128]{3,2,1,0:T(8,128)S(1)}, f32[6,9,16,128]{3,2,1,0:T(8,128)}, u32[]{:S(2)}) %copy-start.3) | copy-done | bytes 442392
  3.6 0.9 copy-done.5
  4.5 1.7 %shard_map.68 = (f32[3,10,24,128]{3,2,1,0:T(8,128)S(1)}, f32[55,16,128]{2,1,0:T(8,128)S(1)}, f32[38,16,128]{2,1,0:T(8,128)S(1)}, f32[10,56,128]{2,1,0:T(8,128)S(1)}, f32[10,40,128]{2,1,0:T(8,128)S(1)}) custom-call(f32[3,9,16,128]{3,2,1,0:T(8,128)S(1)} %copy-done.5, s32[8,9,16,128]{3,2,1,0:T(8,128)S(1)} %copy-done.1, f32[6,9,16,128]{3,2,1,0:T(8,128)S(1)} %copy-done.3, ...), custom_call_target="tpu_custom_call" | custom-call | tf_op jit(solution)/shard_map/pallas_call | solution.py:642
  6.2 2.0 %collective-permute-start.2 = (f32[10,56,128]{2,1,0:T(8,128)S(1)}, f32[10,56,128]{2,1,0:T(8,128)S(1)}, u32[]{:S(2)}, u32[]{:S(2)}) collective-permute-start(f32[10,56,128]{2,1,0:T(8,128)S(1)} %get-tuple-element.19), channel_id=1, source_target_pairs={{0,1},{1,2},{2,3},{3,4},{4,5},{5,6},{6,7},{7,8},{8,9},{9,10},{10,1... | collective-permute-start | bytes 860168 | tf_op jit(solution)/shard_map/ppermute | solution.py:608
  8.2 2.5 %collective-permute-start.3 = (f32[10,40,128]{2,1,0:T(8,128)S(1)}, f32[10,40,128]{2,1,0:T(8,128)S(1)}, u32[]{:S(2)}, u32[]{:S(2)}) collective-permute-start(f32[10,40,128]{2,1,0:T(8,128)S(1)} %get-tuple-element.20), channel_id=1, source_target_pairs={{0,15},{1,0},{2,1},{3,2},{4,3},{5,4},{6,5},{7,6},{8,7},{9,8},{10,9... | collective-permute-start | bytes 614408 | tf_op jit(solution)/shard_map/ppermute | solution.py:608
  10.7 3.0 %collective-permute-start.1 = (f32[38,16,128]{2,1,0:T(8,128)S(1)}, f32[38,16,128]{2,1,0:T(8,128)S(1)}, u32[]{:S(2)}, u32[]{:S(2)}) collective-permute-start(f32[38,16,128]{2,1,0:T(8,128)S(1)} %get-tuple-element.18), channel_id=1, source_target_pairs={{0,112},{16,0},{32,16},{48,32},{64,48},{80,64},{96,80},{112,96},{1... | collective-permute-start | bytes 933896 | tf_op jit(solution)/shard_map/ppermute | solution.py:608
  13.6 3.8 %collective-permute-done.2.down_ref = f32[10,56,128]{2,1,0:T(8,128)S(1)} collective-permute-done((f32[10,56,128]{2,1,0:T(8,128)S(1)}, f32[10,56,128]{2,1,0:T(8,128)S(1)}, u32[]{:S(2)}, u32[]{:S(2)}) %collective-permute-start.2) | collective-permute-done | bytes 286752 | tf_op jit(solution)/shard_map/ppermute | solution.py:608
  17.5 2.9 %collective-permute-start.5 = (f32[3,96,128]{2,1,0:T(8,128)S(1)}, f32[3,96,128]{2,1,0:T(8,128)S(1)}, u32[]{:S(2)}, u32[]{:S(2)}) collective-permute-start(f32[3,96,128]{2,1,0:T(8,128)S(1)} %slice.17), channel_id=1, source_target_pairs={{0,112},{16,0},{32,16},{48,32},{64,48},{80,64},{96,80},{112,96},{1... | collective-permute-start | bytes 442376 | tf_op jit(solution)/shard_map/ppermute | solution.py:608
  20.5 2.7 %collective-permute-done.5.cr_ref = f32[3,96,128]{2,1,0:T(8,128)S(1)} collective-permute-done((f32[3,96,128]{2,1,0:T(8,128)S(1)}, f32[3,96,128]{2,1,0:T(8,128)S(1)}, u32[]{:S(2)}, u32[]{:S(2)}) %collective-permute-start.5) | collective-permute-done | bytes 147488 | tf_op jit(solution)/shard_map/ppermute | solution.py:608
  23.8 12.4 %shard_map.69 = (f32[15,14,24,128]{3,2,1,0:T(8,128)}, f32[4,3,9,16,128]{4,3,2,1,0:T(8,128)S(1)}, f32[8,128]{1,0:T(8,128)S(1)}, f32[9,16,128]{2,1,0:T(8,128)S(1)}...) custom-call(s32[8,9,16,128]{3,2,1,0:T(8,128)S(1)} %copy-done.2, ...), custom_call_target="tpu_custom_call" | custom-call | tf_op jit(solution)/shard_map/pallas_call | solution.py:648
  36.2 1.5 %collective-permute-start.6 = (f32[9,16,128]{2,1,0:T(8,128)S(1)}, f32[9,16,128]{2,1,0:T(8,128)S(1)}, u32[]{:S(2)}, u32[]{:S(2)}) collective-permute-start(f32[9,16,128]{2,1,0:T(8,128)S(1)} %get-tuple-element.24), channel_id=1, source_target_pairs={{0,16},{16,32},{32,48},{48,64},{64,80},{80,96},{96,112},{112,0},{1... | collective-permute-start | bytes 221192 | tf_op jit(solution)/shard_map/ppermute | solution.py:608
  37.7 1.4 %collective-permute-start.7 = (f32[9,16,128]{2,1,0:T(8,128)S(1)}, f32[9,16,128]{2,1,0:T(8,128)S(1)}, u32[]{:S(2)}, u32[]{:S(2)}) collective-permute-start(f32[9,16,128]{2,1,0:T(8,128)S(1)} %get-tuple-element.25), channel_id=1, source_target_pairs={{0,112},{16,0},{32,16},{48,32},{64,48},{80,64},{96,80},{112,96},{1... | collective-permute-start | bytes 221192 | tf_op jit(solution)/shard_map/ppermute | solution.py:608
  39.1 4.1 %collective-permute-start.9 = (f32[9,16,128]{2,1,0:T(8,128)S(1)}, f32[9,16,128]{2,1,0:T(8,128)S(1)}, u32[]{:S(2)}, u32[]{:S(2)}) collective-permute-start(f32[9,16,128]{2,1,0:T(8,128)S(1)} %get-tuple-element.27), channel_id=1, source_target_pairs={{0,15},{1,0},{2,1},{3,2},{4,3},{5,4},{6,5},{7,6},{8,7},{9,8},{10,9... | collective-permute-start | bytes 221192 | tf_op jit(solution)/shard_map/ppermute | solution.py:608
  43.3 2.0 %collective-permute-done.9.up_ref = f32[9,16,128]{2,1,0:T(8,128)S(1)} collective-permute-done((f32[9,16,128]{2,1,0:T(8,128)S(1)}, f32[9,16,128]{2,1,0:T(8,128)S(1)}, u32[]{:S(2)}, u32[]{:S(2)}) %collective-permute-start.9) | collective-permute-done | bytes 73760 | tf_op jit(solution)/shard_map/ppermute | solution.py:608
  45.8 1.2 %collective-permute-done.11.cr_ref = f32[3,32,128]{2,1,0:T(8,128)S(1)} collective-permute-done((f32[3,32,128]{2,1,0:T(8,128)S(1)}, f32[3,32,128]{2,1,0:T(8,128)S(1)}, u32[]{:S(2)}, u32[]{:S(2)}) %collective-permute-start.11) | collective-permute-done | bytes 49184 | tf_op jit(solution)/shard_map/ppermute | solution.py:608
  47.0 3.0 %collective-permute-done.10.cl_ref = f32[3,32,128]{2,1,0:T(8,128)S(1)} collective-permute-done((f32[3,32,128]{2,1,0:T(8,128)S(1)}, f32[3,32,128]{2,1,0:T(8,128)S(1)}, u32[]{:S(2)}, u32[]{:S(2)}) %collective-permute-start.10) | collective-permute-done | bytes 49184 | tf_op jit(solution)/shard_map/ppermute | solution.py:608
  50.0 1.7 %copy-done = f32[15,14,24,128]{3,2,1,0:T(8,128)S(1)} copy-done((f32[15,14,24,128]{3,2,1,0:T(8,128)S(1)}, f32[15,14,24,128]{3,2,1,0:T(8,128)}, u32[]{:S(2)}) %copy-start) | copy-done | bytes 2580504
  51.8 10.2 %shard_map.70 = (f32[3,3,9,16,128]{4,3,2,1,0:T(8,128)S(1)}, f32[8,128]{1,0:T(8,128)S(1)}) custom-call(f32[15,14,24,128]{3,2,1,0:T(8,128)S(1)} %copy-done, f32[4,3,9,16,128]{4,3,2,1,0:T(8,128)S(1)} %get-tuple-element.23.own_ref, f32[9,16,128]{2,1,0:T(8,128)S(1)} %collective-permute-done.6.left_ref, f32[9,16,128]{2,1,0:T(8,128)S(1)} %collective-permute-done.7.right_ref, ...), custom_call_target="tpu_custom_call" | custom-call | tf_op jit(solution)/shard_map/pallas_call | solution.py:655
  62.0 1.2 %collective-permute-done.12 = f32[16,128]{1,0:T(8,128)S(1)} collective-permute-done((f32[16,128]{1,0:T(8,128)S(1)}, f32[16,128]{1,0:T(8,128)S(1)}, u32[]{:S(2)}, u32[]{:S(2)}) %collective-permute-start.12) | collective-permute-done | bytes 8224 | tf_op jit(solution)/shard_map/ppermute | solution.py:626
  63.2 0.7 collective-permute-start.13
  63.9 3.0 %collective-permute-done.13 = f32[16,128]{1,0:T(8,128)S(1)} collective-permute-done((f32[16,128]{1,0:T(8,128)S(1)}, f32[16,128]{1,0:T(8,128)S(1)}, u32[]{:S(2)}, u32[]{:S(2)}) %collective-permute-start.13) | collective-permute-done | bytes 8224 | tf_op jit(solution)/shard_map/ppermute | solution.py:628
  66.9 2.1 %collective-permute-start.14 = (f32[16,128]{1,0:T(8,128)S(1)}, f32[16,128]{1,0:T(8,128)S(1)}, u32[]{:S(2)}, u32[]{:S(2)}) collective-permute-start(f32[16,128]{1,0:T(8,128)S(1)} %add.22), channel_id=1, source_target_pairs={{0,96},{16,112},{32,64},{48,80},{64,32},{80,48},{96,0},{112,16},{1... | collective-permute-start | bytes 24584 | tf_op jit(solution)/shard_map/ppermute | solution.py:628
  69.0 2.7 %collective-permute-done.14 = f32[16,128]{1,0:T(8,128)S(1)} collective-permute-done((f32[16,128]{1,0:T(8,128)S(1)}, f32[16,128]{1,0:T(8,128)S(1)}, u32[]{:S(2)}, u32[]{:S(2)}) %collective-permute-start.14) | collective-permute-done | bytes 8224 | tf_op jit(solution)/shard_map/ppermute | solution.py:628
  71.7 0.7 collective-permute-start.15
  72.4 2.9 %collective-permute-done.15 = f32[16,128]{1,0:T(8,128)S(1)} collective-permute-done((f32[16,128]{1,0:T(8,128)S(1)}, f32[16,128]{1,0:T(8,128)S(1)}, u32[]{:S(2)}, u32[]{:S(2)}) %collective-permute-start.15) | collective-permute-done | bytes 8224 | tf_op jit(solution)/shard_map/ppermute | solution.py:630
  75.4 6.6 %collective-permute-start.16 = (f32[16,128]{1,0:T(8,128)S(1)}, f32[16,128]{1,0:T(8,128)S(1)}, u32[]{:S(2)}, u32[]{:S(2)}) collective-permute-start(f32[16,128]{1,0:T(8,128)S(1)} %add.24), channel_id=1, source_target_pairs={{0,3},{1,2},{2,1},{3,0},{4,7},{5,6},{6,5},{7,4},{8,11},{9,10},{10,... | collective-permute-start | bytes 24584 | tf_op jit(solution)/shard_map/ppermute | solution.py:630
  82.0 1.6 %collective-permute-done.16 = f32[16,128]{1,0:T(8,128)S(1)} collective-permute-done((f32[16,128]{1,0:T(8,128)S(1)}, f32[16,128]{1,0:T(8,128)S(1)}, u32[]{:S(2)}, u32[]{:S(2)}) %collective-permute-start.16) | collective-permute-done | bytes 8224 | tf_op jit(solution)/shard_map/ppermute | solution.py:630
  83.7 3.6 %collective-permute-done.17 = f32[16,128]{1,0:T(8,128)S(1)} collective-permute-done((f32[16,128]{1,0:T(8,128)S(1)}, f32[16,128]{1,0:T(8,128)S(1)}, u32[]{:S(2)}, u32[]{:S(2)}) %collective-permute-start.17) | collective-permute-done | bytes 8224 | tf_op jit(solution)/shard_map/ppermute | solution.py:632
  87.5 4.6 %collective-permute-done.18 = f32[16,128]{1,0:T(8,128)S(1)} collective-permute-done((f32[16,128]{1,0:T(8,128)S(1)}, f32[16,128]{1,0:T(8,128)S(1)}, u32[]{:S(2)}, u32[]{:S(2)}) %collective-permute-start.18) | collective-permute-done | bytes 8224 | tf_op jit(solution)/shard_map/ppermute | solution.py:632
  92.2 1.3 %shard_map.71 = (f32[3,9,16,128]{3,2,1,0:T(8,128)}, f32[3,9,16,128]{3,2,1,0:T(8,128)}) custom-call(f32[16,128]{1,0:T(8,128)S(1)} %add.27.dots_ref, f32[4,3,9,16,128]{4,3,2,1,0:T(8,128)S(1)} %get-tuple-element.23.own_ref, f32[3,3,9,16,128]{4,3,2,1,0:T(8,128)S(1)} %get-tuple-element.29.tail_ref), custom_call_target="tpu_custom_call" | custom-call | tf_op jit(solution)/shard_map/pallas_call | solution.py:659
  (41 shorter events, 1.7 us)
Async XLA Ops:
  1.5 1.1 %copy-start.1 = (s32[8,9,16,128]{3,2,1,0:T(8,128)S(1)}, s32[8,9,16,128]{3,2,1,0:T(8,128)}, u32[]{:S(2)}) copy-start(s32[8,9,16,128]{3,2,1,0:T(8,128)} %flags_ref.3) | copy-start | bytes 1769476
  2.5 1.0 %copy-start.3 = (f32[6,9,16,128]{3,2,1,0:T(8,128)S(1)}, f32[6,9,16,128]{3,2,1,0:T(8,128)}, u32[]{:S(2)}) copy-start(f32[6,9,16,128]{3,2,1,0:T(8,128)} %flow_ref.3) | copy-start | bytes 1327108
  3.6 0.9 %copy-start.5 = (f32[3,9,16,128]{3,2,1,0:T(8,128)S(1)}, f32[3,9,16,128]{3,2,1,0:T(8,128)}, u32[]{:S(2)}) copy-start(f32[3,9,16,128]{3,2,1,0:T(8,128)} %load_ref.1) | copy-start | bytes 663556
  4.5 19.3 %copy-start.2 = (s32[8,9,16,128]{3,2,1,0:T(8,128)S(1)}, s32[8,9,16,128]{3,2,1,0:T(8,128)}, u32[]{:S(2)}) copy-start(s32[8,9,16,128]{3,2,1,0:T(8,128)} %flags_ref.3) | copy-start | bytes 1769476
  4.5 19.3 %copy-start.4 = (f32[6,9,16,128]{3,2,1,0:T(8,128)S(1)}, f32[6,9,16,128]{3,2,1,0:T(8,128)}, u32[]{:S(2)}) copy-start(f32[6,9,16,128]{3,2,1,0:T(8,128)} %flow_ref.3) | copy-start | bytes 1327108
  6.2 11.2 %collective-permute-start.2 = (f32[10,56,128]{2,1,0:T(8,128)S(1)}, f32[10,56,128]{2,1,0:T(8,128)S(1)}, u32[]{:S(2)}, u32[]{:S(2)}) collective-permute-start(f32[10,56,128]{2,1,0:T(8,128)S(1)} %get-tuple-element.19), channel_id=1, source_target_pairs={{0,1},{1,2},{2,3},{3,4},{4,5},{5,6},{6,7},{7,8},{8,9},{9,10},{10,1... | collective-permute-start | bytes 860168 | tf_op jit(solution)/shard_map/ppermute | solution.py:608
  8.2 9.2 %collective-permute-start.3 = (f32[10,40,128]{2,1,0:T(8,128)S(1)}, f32[10,40,128]{2,1,0:T(8,128)S(1)}, u32[]{:S(2)}, u32[]{:S(2)}) collective-permute-start(f32[10,40,128]{2,1,0:T(8,128)S(1)} %get-tuple-element.20), channel_id=1, source_target_pairs={{0,15},{1,0},{2,1},{3,2},{4,3},{5,4},{6,5},{7,6},{8,7},{9,8},{10,9... | collective-permute-start | bytes 614408 | tf_op jit(solution)/shard_map/ppermute | solution.py:608
  10.7 12.5 %collective-permute-start = (f32[55,16,128]{2,1,0:T(8,128)S(1)}, f32[55,16,128]{2,1,0:T(8,128)S(1)}, u32[]{:S(2)}, u32[]{:S(2)}) collective-permute-start(f32[55,16,128]{2,1,0:T(8,128)S(1)} %get-tuple-element.17), channel_id=1, source_target_pairs={{0,16},{16,32},{32,48},{48,64},{64,80},{80,96},{96,112},{112,0},{1... | collective-permute-start | bytes 1351688 | tf_op jit(solution)/shard_map/ppermute | solution.py:608
  10.7 9.8 %collective-permute-start.1 = (f32[38,16,128]{2,1,0:T(8,128)S(1)}, f32[38,16,128]{2,1,0:T(8,128)S(1)}, u32[]{:S(2)}, u32[]{:S(2)}) collective-permute-start(f32[38,16,128]{2,1,0:T(8,128)S(1)} %get-tuple-element.18), channel_id=1, source_target_pairs={{0,112},{16,0},{32,16},{48,32},{64,48},{80,64},{96,80},{112,96},{1... | collective-permute-start | bytes 933896 | tf_op jit(solution)/shard_map/ppermute | solution.py:608
  17.5 6.3 %collective-permute-start.4 = (f32[4,96,128]{2,1,0:T(8,128)S(1)}, f32[4,96,128]{2,1,0:T(8,128)S(1)}, u32[]{:S(2)}, u32[]{:S(2)}) collective-permute-start(f32[4,96,128]{2,1,0:T(8,128)S(1)} %slice.16), channel_id=1, source_target_pairs={{0,16},{16,32},{32,48},{48,64},{64,80},{80,96},{96,112},{112,0},{1... | collective-permute-start | bytes 589832 | tf_op jit(solution)/shard_map/ppermute | solution.py:608
  17.5 5.6 %collective-permute-start.5 = (f32[3,96,128]{2,1,0:T(8,128)S(1)}, f32[3,96,128]{2,1,0:T(8,128)S(1)}, u32[]{:S(2)}, u32[]{:S(2)}) collective-permute-start(f32[3,96,128]{2,1,0:T(8,128)S(1)} %slice.17), channel_id=1, source_target_pairs={{0,112},{16,0},{32,16},{48,32},{64,48},{80,64},{96,80},{112,96},{1... | collective-permute-start | bytes 442376 | tf_op jit(solution)/shard_map/ppermute | solution.py:608
  36.2 7.1 %collective-permute-start.8 = (f32[9,16,128]{2,1,0:T(8,128)S(1)}, f32[9,16,128]{2,1,0:T(8,128)S(1)}, u32[]{:S(2)}, u32[]{:S(2)}) collective-permute-start(f32[9,16,128]{2,1,0:T(8,128)S(1)} %get-tuple-element.26), channel_id=1, source_target_pairs={{0,1},{1,2},{2,3},{3,4},{4,5},{5,6},{6,7},{7,8},{8,9},{9,10},{10,1... | collective-permute-start | bytes 221192 | tf_op jit(solution)/shard_map/ppermute | solution.py:608
  36.2 9.6 %collective-permute-start.6 = (f32[9,16,128]{2,1,0:T(8,128)S(1)}, f32[9,16,128]{2,1,0:T(8,128)S(1)}, u32[]{:S(2)}, u32[]{:S(2)}) collective-permute-start(f32[9,16,128]{2,1,0:T(8,128)S(1)} %get-tuple-element.24), channel_id=1, source_target_pairs={{0,16},{16,32},{32,48},{48,64},{64,80},{80,96},{96,112},{112,0},{1... | collective-permute-start | bytes 221192 | tf_op jit(solution)/shard_map/ppermute | solution.py:608
  37.7 8.1 %collective-permute-start.7 = (f32[9,16,128]{2,1,0:T(8,128)S(1)}, f32[9,16,128]{2,1,0:T(8,128)S(1)}, u32[]{:S(2)}, u32[]{:S(2)}) collective-permute-start(f32[9,16,128]{2,1,0:T(8,128)S(1)} %get-tuple-element.25), channel_id=1, source_target_pairs={{0,112},{16,0},{32,16},{48,32},{64,48},{80,64},{96,80},{112,96},{1... | collective-permute-start | bytes 221192 | tf_op jit(solution)/shard_map/ppermute | solution.py:608
  39.1 6.1 %collective-permute-start.9 = (f32[9,16,128]{2,1,0:T(8,128)S(1)}, f32[9,16,128]{2,1,0:T(8,128)S(1)}, u32[]{:S(2)}, u32[]{:S(2)}) collective-permute-start(f32[9,16,128]{2,1,0:T(8,128)S(1)} %get-tuple-element.27), channel_id=1, source_target_pairs={{0,15},{1,0},{2,1},{3,2},{4,3},{5,4},{6,5},{7,6},{8,7},{9,8},{10,9... | collective-permute-start | bytes 221192 | tf_op jit(solution)/shard_map/ppermute | solution.py:608
  45.3 1.8 %collective-permute-start.11 = (f32[3,32,128]{2,1,0:T(8,128)S(1)}, f32[3,32,128]{2,1,0:T(8,128)S(1)}, u32[]{:S(2)}, u32[]{:S(2)}) collective-permute-start(f32[3,32,128]{2,1,0:T(8,128)S(1)} %get-tuple-element.30), channel_id=1, source_target_pairs={{0,112},{16,0},{32,16},{48,32},{64,48},{80,64},{96,80},{112,96},{1... | collective-permute-start | bytes 147464 | tf_op jit(solution)/shard_map/ppermute | solution.py:608
  45.3 4.7 %collective-permute-start.10 = (f32[3,32,128]{2,1,0:T(8,128)S(1)}, f32[3,32,128]{2,1,0:T(8,128)S(1)}, u32[]{:S(2)}, u32[]{:S(2)}) collective-permute-start(f32[3,32,128]{2,1,0:T(8,128)S(1)} %get-tuple-element.31), channel_id=1, source_target_pairs={{0,16},{16,32},{32,48},{48,64},{64,80},{80,96},{96,112},{112,0},{1... | collective-permute-start | bytes 147464 | tf_op jit(solution)/shard_map/ppermute | solution.py:608
  50.0 1.7 %copy-start = (f32[15,14,24,128]{3,2,1,0:T(8,128)S(1)}, f32[15,14,24,128]{3,2,1,0:T(8,128)}, u32[]{:S(2)}) copy-start(f32[15,14,24,128]{3,2,1,0:T(8,128)} %get-tuple-element.22.els_ref) | copy-start | bytes 7741444
  61.9 1.3 %collective-permute-start.12 = (f32[16,128]{1,0:T(8,128)S(1)}, f32[16,128]{1,0:T(8,128)S(1)}, u32[]{:S(2)}, u32[]{:S(2)}) collective-permute-start(f32[16,128]{1,0:T(8,128)S(1)} %constant_dynamic-update-slice_fusion.4), channel_id=1, source_target_pairs={{0,16},{16,0},{32,48},{48,32},{64,80},{80,64},{96,112},{112,96},{1... | collective-permute-start | bytes 24584 | tf_op jit(solution)/shard_map/ppermute | solution.py:626
  63.2 3.7 %collective-permute-start.13 = (f32[16,128]{1,0:T(8,128)S(1)}, f32[16,128]{1,0:T(8,128)S(1)}, u32[]{:S(2)}, u32[]{:S(2)}) collective-permute-start(f32[16,128]{1,0:T(8,128)S(1)} %add.21), channel_id=1, source_target_pairs={{0,32},{16,48},{32,0},{48,16},{64,96},{80,112},{96,64},{112,80},{1... | collective-permute-start | bytes 24584 | tf_op jit(solution)/shard_map/ppermute | solution.py:628
  66.9 4.9 %collective-permute-start.14 = (f32[16,128]{1,0:T(8,128)S(1)}, f32[16,128]{1,0:T(8,128)S(1)}, u32[]{:S(2)}, u32[]{:S(2)}) collective-permute-start(f32[16,128]{1,0:T(8,128)S(1)} %add.22), channel_id=1, source_target_pairs={{0,96},{16,112},{32,64},{48,80},{64,32},{80,48},{96,0},{112,16},{1... | collective-permute-start | bytes 24584 | tf_op jit(solution)/shard_map/ppermute | solution.py:628
  71.7 3.7 %collective-permute-start.15 = (f32[16,128]{1,0:T(8,128)S(1)}, f32[16,128]{1,0:T(8,128)S(1)}, u32[]{:S(2)}, u32[]{:S(2)}) collective-permute-start(f32[16,128]{1,0:T(8,128)S(1)} %add.23), channel_id=1, source_target_pairs={{0,1},{1,0},{2,3},{3,2},{4,5},{5,4},{6,7},{7,6},{8,9},{9,8},{10,11... | collective-permute-start | bytes 24584 | tf_op jit(solution)/shard_map/ppermute | solution.py:630
  75.4 8.3 %collective-permute-start.16 = (f32[16,128]{1,0:T(8,128)S(1)}, f32[16,128]{1,0:T(8,128)S(1)}, u32[]{:S(2)}, u32[]{:S(2)}) collective-permute-start(f32[16,128]{1,0:T(8,128)S(1)} %add.24), channel_id=1, source_target_pairs={{0,3},{1,2},{2,1},{3,0},{4,7},{5,6},{6,5},{7,4},{8,11},{9,10},{10,... | collective-permute-start | bytes 24584 | tf_op jit(solution)/shard_map/ppermute | solution.py:630
  83.6 3.7 %collective-permute-start.17 = (f32[16,128]{1,0:T(8,128)S(1)}, f32[16,128]{1,0:T(8,128)S(1)}, u32[]{:S(2)}, u32[]{:S(2)}) collective-permute-start(f32[16,128]{1,0:T(8,128)S(1)} %add.25), channel_id=1, source_target_pairs={{0,4},{1,5},{2,6},{3,7},{4,0},{5,1},{6,2},{7,3},{8,12},{9,13},{10,... | collective-permute-start | bytes 24584 | tf_op jit(solution)/shard_map/ppermute | solution.py:632
  87.3 4.9 %collective-permute-start.18 = (f32[16,128]{1,0:T(8,128)S(1)}, f32[16,128]{1,0:T(8,128)S(1)}, u32[]{:S(2)}, u32[]{:S(2)}) collective-permute-start(f32[16,128]{1,0:T(8,128)S(1)} %add.26), channel_id=1, source_target_pairs={{0,12},{1,13},{2,14},{3,15},{4,8},{5,9},{6,10},{7,11},{8,4},{9,5},... | collective-permute-start | bytes 24584 | tf_op jit(solution)/shard_map/ppermute | solution.py:632

commit v2 on v1

--- a/solution.py
+++ b/solution.py
@@ -169,11 +169,31 @@
     return jnp.where(flag, 0.0, 1.0).astype(F32)
 
 
-def offset_kernel(load_ref, flags_ref, flow_ref, contact_ref, die_ref,
-                  part_ref, right_ref, left_ref, up_ref, down_ref, lower_ref, upper_ref):
+def offset_kernel(load_hbm, flags_hbm, flow_hbm, active_ref, die_ref,
+                  part_ref, right_ref, left_ref, up_ref, down_ref, contact_ref,
+                  lower_ref, upper_ref, load_ref, flags_ref, flow_ref, load_sem, flags_sem, flow_sem):
+    copies = [
+        [pltpu.make_async_copy(source.at[m], target.at[m], sem.at[m]) for m in range(source.shape[0])]
+        for source, target, sem in (
+            (flags_hbm, flags_ref, flags_sem), (flow_hbm, flow_ref, flow_sem), (load_hbm, load_ref, load_sem))
+    ]
+    for group in copies:
+        for copy in group:
+            copy.start()
     lane = lanes()
     last_lane = lane == DZ - 1
     zero = jnp.zeros((8, DZ), F32)
+    last = lax.broadcasted_iota(jnp.int32, (OY, DZ), 1) == DZ - 1
+    same = lax.broadcasted_iota(jnp.int32, (OY, OY), 0) == lax.broadcasted_iota(jnp.int32, (OY, OY), 1)
+
+    def on_rows(row):
+        return jnp.sum(jnp.where(same, jnp.broadcast_to(row, (OY, OY)), 0.0), axis=1, keepdims=True)
+
+    die_rows = []
+    for x in range(OX):
+        stiff = CONTACT_STIFF * active_ref[x : x + 1].astype(F32)
+        contact_ref[x] = jnp.where(last, on_rows(stiff), 0.0)
+        die_rows.append(jnp.where(last, on_rows(stiff * die_ref[x : x + 1]), 0.0))
 
     def clear(x, _):
         for m in range(6):
@@ -182,6 +202,9 @@
         return 0
 
     lax.fori_loop(0, OX + 1, clear, 0)
+    for group in copies[:2]:
+        for copy in group:
+            copy.wait()
     for row in (0, 8):
 
         def element(x, behind):
@@ -200,18 +223,13 @@
                 part_ref[c, x, row : row + 8] = merge_yz(lower_ref, upper_ref, c, x, row, last_lane) * (-1.0 / 16.0)
         return 0
 
-    lax.fori_loop(0, OX + 1, finish, 0)
-
-    def add_load(x, _):
-        for c in range(3):
-            for row in (0, 8):
-                value = part_ref[c, x, row : row + 8] + load_ref[c, x, row : row + 8]
-                if c == 2:
-                    value = value + die_ref[x, row : row + 8]
-                part_ref[c, x, row : row + 8] = value
-        return 0
-
-    lax.fori_loop(0, OX, add_load, 0)
+    lax.fori_loop(0, OX + 1, finish, 0, unroll=2)
+    for copy in copies[2]:
+        copy.wait()
+    for x in range(OX):
+        for c in range(3):
+            value = part_ref[c, x, 0:OY] + load_ref[c, x]
+            part_ref[c, x, 0:OY] = value + die_rows[x] if c == 2 else value
 
     def field(f, x, rows):
         if f < 8:
@@ -276,11 +294,11 @@
                 )
         return 0
 
-    lax.fori_loop(0, WX, first, 0)
+    lax.fori_loop(0, WX, first, 0, unroll=5)
 
     for step in range(1, HALO + 1):
-        start = jnp.where(at_first_x, HALO, step - 1)
-        end = jnp.where(at_last_x, HALO + OX - 1, WX - 1 - step)
+        start, end = step - 1, WX - 1 - step
+        scale = (2.0 if step == 1 else 4.0) / SPAN
         for row in (0, 8, 16):
 
             def plane(x):
@@ -309,12 +327,21 @@
                 store_y(node, lower_ref, upper_ref, x, row, keep_upper if row == 0 else None)
                 return after, ahead
 
-            lax.fori_loop(start, end + 1, element, (plane(start), [zero] * 12))
-
-        node_start = jnp.where(at_first_x, HALO, step)
-        scale = (2.0 if step == 1 else 4.0) / SPAN
-
-        def finish(x, _):
+            carry = (plane(start), [zero] * 12)
+            for x in range(start, HALO):
+                carry = element(x, carry)
+            carry = (carry[0], [jnp.where(at_first_x, 0.0, value) for value in carry[1]])
+            first_pair = HALO + (end + 1 - HALO) % 2
+            if first_pair > HALO:
+                carry = element(HALO, carry)
+
+            def pair(k, carry):
+                x = first_pair + 2 * k
+                return element(x + 1, element(x, carry))
+
+            lax.fori_loop(0, (end + 1 - first_pair) // 2, pair, carry)
+
+        for x in range(step, end + 1):
             for row in (0, 8, 16):
                 for c in range(3):
                     here = basis[step - 1][c, x, row : row + 8]
@@ -325,14 +352,13 @@
                         value = value - here
                     else:
                         value = value - (here + here) - basis[step - 2][c, x, row : row + 8]
+                    if x >= HALO + OX:
+                        value = jnp.where(at_last_x, 0.0, value)
                     if row == 16:
                         value = jnp.where(keep_node, value, 0.0)
                     basis[step][c, x, row : row + 8] = value
                     if step < HALO:
                         z_ref[2 * c, x, row : row + 8], z_ref[2 * c + 1, x, row : row + 8] = z_pair(value, first_lane)
-            return 0
-
-        lax.fori_loop(node_start, end + 1, finish, 0)
 
 
 def sum_rows(values):
@@ -442,10 +468,12 @@
     for k in range(7):
         dots_ref[k : k + 1] = sum_rows(sums[k])
 
-    for c in range(3):
-        for i in range(3):
-            right_out[3 * c + i] = b3[c, 9 + i, mid]
-            left_out[3 * c + i] = b3[c, 3 + i, mid]
+    for i in range(3):
+        for c in range(3):
+            for out, x in ((right_out, 9 + i), (left_out, 3 + i)):
+                out[3 * c + i] = b3[c, x, mid]
+                out[9 + i, 3 * c : 3 * c + 3] = b3[c, x, 16:19]
+                out[12 + i, 3 * c : 3 * c + 3] = b3[c, x, 3:6]
 
     def slabs(x, _):
         for c in range(3):
@@ -456,33 +484,32 @@
     lax.fori_loop(0, OX, slabs, 0)
 
 
-def second_kernel(els_ref, own_ref, left_ref, right_ref, down_ref, up_ref, cl_ref, cr_ref,
-                  tail_ref, dots_ref, b0, b1, b2, b3, z_ref, lower_ref, upper_ref):
+def second_kernel(els_ref, own_ref, dots_ref, left_ref, right_ref, down_ref, up_ref,
+                  tail_ref, row_ref, b0, b1, b2, b3, z_ref, lower_ref, upper_ref):
     _, at_last_x, _, at_last_y = place()
     has_r, has_u = ask(at_last_x), ask(at_last_y)
     zero = jnp.zeros((8, DZ), F32)
     mid = slice(HALO, HALO + OY)
 
     def own(x, _):
-        w = x + HALO
-        for c in range(3):
-            b0[c, w, 16:24] = zero
-            b0[c, w, mid] = own_ref[3, c, x]
-            b0[c, w, 0:3] = down_ref[x, 3 * c : 3 * c + 3]
-            b0[c, w, 19:22] = up_ref[x, 3 * c : 3 * c + 3] * has_u
-        return 0
-
+        for c in range(3):
+            b0[c, x + HALO, mid] = own_ref[3, c, x]
+        return 0
+
+    def edges(x, _):
+        inside = jnp.where(x >= HALO + OX, has_r, 1.0)
+        for c in range(3):
+            b0[c, x, 16:24] = zero
+            b0[c, x, 0:3] = down_ref[x, 3 * c : 3 * c + 3] * inside
+            b0[c, x, 19:22] = up_ref[x, 3 * c : 3 * c + 3] * (inside * has_u)
+        return 0
+
+    lax.fori_loop(0, WX, edges, 0)
     lax.fori_loop(0, OX, own, 0)
     for c in range(3):
         for i in range(3):
-            b0[c, i, 16:24] = zero
             b0[c, i, mid] = left_ref[3 * c + i]
-            b0[c, i, 0:3] = cl_ref[i, 3 * c : 3 * c + 3]
-            b0[c, i, 19:22] = cl_ref[i, 16 + 3 * c : 19 + 3 * c] * has_u
-            b0[c, 12 + i, 16:24] = zero
             b0[c, 12 + i, mid] = right_ref[3 * c + i] * has_r
-            b0[c, 12 + i, 0:3] = cr_ref[i, 3 * c : 3 * c + 3] * has_r
-            b0[c, 12 + i, 19:22] = cr_ref[i, 16 + 3 * c : 19 + 3 * c] * (has_r * has_u)
 
     basis = (b0, b1, b2, b3)
     three_steps(els_ref, basis, z_ref, lower_ref, upper_ref)
@@ -501,9 +528,12 @@
         return tuple(sums)
 
     sums = lax.fori_loop(0, OX, collect, (zero,) * 5)
-    dots_ref[...] = zero
-    for k in range(5):
-        dots_ref[k : k + 1] = sum_rows(sums[k])
+    lane = lax.broadcasted_iota(jnp.int32, (1, DZ), 1)
+    line = jnp.zeros((1, DZ), F32)
+    for k in range(12):
+        dot = dots_ref[k : k + 1] if k < 7 else sum_rows(sums[k - 7])
+        line = jnp.where(lane == k, jnp.sum(dot, axis=1, keepdims=True), line)
+    row_ref[...] = jnp.broadcast_to(line, row_ref.shape)
 
 
 def b_at(ref, c, x, row):
@@ -566,8 +596,8 @@
 
 
 def last_kernel(dots_ref, own_ref, tail_ref, displacement_ref, residual_ref):
-    sums = jnp.broadcast_to(jnp.sum(dots_ref[...], axis=1, keepdims=True), (16, DZ))
-    dots = [sums[k : k + 1] for k in range(7)] + [sums[8 + k : 9 + k] for k in range(5)]
+    sums = jnp.sum(dots_ref[...], axis=0, keepdims=True)
+    dots = [jnp.broadcast_to(sums[:, k : k + 1], (1, DZ)) for k in range(12)]
     mu = dots[:2]
     for k in range(2, 12):
         mu.append((dots[k] + dots[k]) - mu[k % 2])
@@ -591,12 +621,13 @@
     return jax.ShapeDtypeStruct(dims, F32)
 
 
-def call(kernel, outs, scratch=()):
+def call(kernel, outs, scratch=(), mebibytes=24, **more):
     return pl.pallas_call(
         kernel,
         out_shape=outs,
-        scratch_shapes=[pltpu.VMEM(dims, F32) for dims in scratch],
-        compiler_params=pltpu.CompilerParams(vmem_limit_bytes=48 * 1024 * 1024),
+        scratch_shapes=[pltpu.VMEM(dims, F32) if isinstance(dims, tuple) else dims for dims in scratch],
+        compiler_params=pltpu.CompilerParams(vmem_limit_bytes=mebibytes * 1024 * 1024),
+        **more,
     )
 
 
@@ -619,44 +650,39 @@
     return from_left, from_right, from_down, from_up, corner_left, corner_right
 
 
-def sum_everywhere(value):
-    ring = [i ^ 1 for i in range(4)], [3 - i for i in range(4)]
-    if (lax.axis_size("gx"), lax.axis_size("gy")) != (8, 16):
-        return lax.psum(value, ("gx", "gy"))
-    value = value + lax.ppermute(value, "gx", [(i, i ^ 1) for i in range(8)])
-    for pairs in ring:
-        value = value + lax.ppermute(value, "gx", [(2 * y + k, 2 * pairs[y] + k) for y in range(4) for k in range(2)])
-    for pairs in ring:
-        value = value + lax.ppermute(value, "gy", [(4 * x + z, 4 * x + pairs[z]) for x in range(4) for z in range(4)])
-    for pairs in ring:
-        value = value + lax.ppermute(value, "gy", [(4 * x + z, 4 * pairs[x] + z) for x in range(4) for z in range(4)])
-    return value
+def exchange_in_turn(right, left, up, down):
+    from_left = rotate(right, "gx", 1)
+    from_right = rotate(left, "gx", -1)
+    up = jnp.concatenate([from_left[9:12], up, from_right[9:12]], axis=0)
+    down = jnp.concatenate([from_left[12:15], down, from_right[12:15]], axis=0)
+    return from_left, from_right, rotate(up, "gy", 1), rotate(down, "gy", -1)
 
 
 def body(load, plastic_flags, flow_dir, contact_flags, die_depth):
-    stiff = CONTACT_STIFF * contact_flags.astype(F32)
-    at_top = lax.broadcasted_iota(jnp.int32, (OX, OY, DZ), 2) == DZ - 1
-    contact = jnp.where(at_top, stiff[:, :, None], 0.0)
-    die = jnp.where(at_top, (stiff * die_depth)[:, :, None], 0.0)
-
-    part, right, left, up, down = call(
+    hbm, vmem = pl.BlockSpec(memory_space=pltpu.HBM), pl.BlockSpec(memory_space=pltpu.VMEM)
+    part, right, left, up, down, contact = call(
         offset_kernel,
-        [shape(3, OX + 1, WY, DZ), shape(55, OY, DZ), shape(38, OY, DZ), shape(OX + 1, 56, DZ), shape(OX + 1, 40, DZ)],
-        [(6, OX + 1, WY + 8, DZ)] * 2,
-    )(load, plastic_flags, flow_dir, contact, die)
+        [shape(3, OX + 1, WY, DZ), shape(55, OY, DZ), shape(38, OY, DZ), shape(OX + 1, 56, DZ),
+         shape(OX + 1, 40, DZ), shape(OX, OY, DZ)],
+        [(6, OX + 1, WY + 8, DZ)] * 2
+        + [(3, OX, OY, DZ), pltpu.VMEM((8, OX, OY, DZ), jnp.int32), (6, OX, OY, DZ)]
+        + [pltpu.SemaphoreType.DMA((count,)) for count in (3, 8, 6)],
+        in_specs=[hbm, hbm, hbm, vmem, vmem],
+    )(load, plastic_flags, flow_dir, contact_flags, die_depth)
     halos = exchange(right, left, up, down, 10)
     els, own, dots, right, left, up, down = call(
         first_kernel,
-        [shape(NEL + 1, WE, WY, DZ), shape(4, 3, OX, OY, DZ), shape(8, DZ), shape(9, OY, DZ), shape(9, OY, DZ),
+        [shape(NEL + 1, WE, WY, DZ), shape(4, 3, OX, OY, DZ), shape(8, DZ), shape(15, OY, DZ), shape(15, OY, DZ),
          shape(OX, 16, DZ), shape(OX, 16, DZ)],
         STEP_SCRATCH,
     )(plastic_flags, flow_dir, contact, part, *halos)
-    halos = exchange(right, left, up, down, 9)
-    tail, dots_tail = call(
-        second_kernel, [shape(3, 3, OX, OY, DZ), shape(8, DZ)], STEP_SCRATCH
-    )(els, own, *halos)
-    dots = sum_everywhere(jnp.concatenate([dots, dots_tail], axis=0))
-    return tuple(call(last_kernel, [shape(3, OX, OY, DZ)] * 2)(dots, own, tail))
+    halos = exchange_in_turn(right, left, up, down)
+    count = lax.axis_size("gx") * lax.axis_size("gy")
+    tail, line = call(
+        second_kernel, [shape(3, 3, OX, OY, DZ), shape(count, DZ)], STEP_SCRATCH
+    )(els, own, dots, *halos)
+    lines = lax.all_to_all(line, ("gx", "gy"), 0, 0, tiled=True)
+    return tuple(call(last_kernel, [shape(3, OX, OY, DZ)] * 2)(lines, own, tail))
 
 
 def solution(mesh):

time: 93.8 us -> 75.9 us (0.81)
  the two profiles are of different devices: /device:TPU:6 before, /device:TPU:1 now
where the time goes in v2:
time: 75.9 us; the launch traced here: 75.6 us
  blocking collectives  19.1 us (25%)
  Pallas kernels  18.7 us (25%)
  starting transfers between devices  16.9 us (22%)
  waiting for transfers between devices  15.6 us (21%)
  local copies, waits for them, and re-layouts  4.47 us (6%)
    all_to_all x1, blocking collectives, body(): lines = lax.all_to_all(line, ('gx', 'gy'), 0, 0, tiled=True)  19.1 us
    ppermute x10, starting transfers between devices, rotate(): lax.ppermute(value, axis, [(i, (i + steps) % count) for i in range(count)])  16.9 us
    ppermute x10, waiting for transfers between devices, rotate(): lax.ppermute(value, axis, [(i, (i + steps) % count) for i in range(count)])  15.6 us
    pallas_call x1, Pallas kernels, body(): call(first_kernel, [shape(NEL + 1, WE, WY, DZ), shape(4, 3, OX, OY, DZ),...  7.38 us
    pallas_call x1, Pallas kernels, body(): call(second_kernel, [shape(3, 3, OX, OY, DZ), shape(count, DZ)], STEP_SCR...  6.83 us
    unnamed x15, local copies, waits for them, and re-layouts  4.42 us
    pallas_call x1, Pallas kernels, body(): call(offset_kernel, [shape(3, OX + 1, WY, DZ), shape(55, OY, DZ), shape(3...  3.2 us
  transfers between devices with their start and end apart: 10, of which 5 were waited for; matrix products, arithmetic and copies ran while one was open for 0% of the time, Pallas kernels for 0%

profile of v2, /device:TPU:1, one launch (start us, length us, event | category | flops | bytes accessed | tf_op | source)
XLA Modules:
  0.0 75.6 jit_solution(13181293790584594892)
XLA Ops:
  0.6 0.0 copy-start
  0.6 1.1 %copy-done = s32[8,9,16,128]{3,2,1,0:T(8,128)S(1)} copy-done((s32[8,9,16,128]{3,2,1,0:T(8,128)S(1)}, s32[8,9,16,128]{3,2,1,0:T(8,128)}, u32[]{:S(2)}) %copy-start) | copy-done | bytes 589848
  1.7 1.0 %copy-done.2 = f32[6,9,16,128]{3,2,1,0:T(8,128)S(1)} copy-done((f32[6,9,16,128]{3,2,1,0:T(8,128)S(1)}, f32[6,9,16,128]{3,2,1,0:T(8,128)}, u32[]{:S(2)}) %copy-start.2) | copy-done | bytes 442392
  2.7 0.9 %copy-done.4 = f32[3,9,16,128]{3,2,1,0:T(8,128)S(1)} copy-done((f32[3,9,16,128]{3,2,1,0:T(8,128)S(1)}, f32[3,9,16,128]{3,2,1,0:T(8,128)}, u32[]{:S(2)}) %copy-start.4) | copy-done | bytes 221208
  3.6 0.7 copy-done.5
  4.3 0.7 copy-done.6
  5.0 3.2 %shard_map.68 = (f32[3,10,24,128]{3,2,1,0:T(8,128)S(1)}, f32[55,16,128]{2,1,0:T(8,128)S(1)}, f32[38,16,128]{2,1,0:T(8,128)S(1)}, f32[10,56,128]{2,1,0:T(8,128)S(...) custom-call(f32[3,9,16,128]{3,2,1,0:T(8,128)S(1)} %copy-done.4, s32[8,9,16,128]{3,2,1,0:T(8,128)S(1)} %copy-done, ...), custom_call_target="tpu_custom_call" | custom-call | tf_op jit(solution)/shard_map/pallas_call | solution.py:663
  8.3 2.5 %collective-permute-start.2 = (f32[10,56,128]{2,1,0:T(8,128)S(1)}, f32[10,56,128]{2,1,0:T(8,128)S(1)}, u32[]{:S(2)}, u32[]{:S(2)}) collective-permute-start(f32[10,56,128]{2,1,0:T(8,128)S(1)} %get-tuple-element.21), channel_id=1, source_target_pairs={{0,1},{1,2},{2,3},{3,4},{4,5},{5,6},{6,7},{7,8},{8,9},{9,10},{10,1... | collective-permute-start | bytes 860168 | tf_op jit(solution)/shard_map/ppermute | solution.py:639
  10.8 4.4 %collective-permute-start.3 = (f32[10,40,128]{2,1,0:T(8,128)S(1)}, f32[10,40,128]{2,1,0:T(8,128)S(1)}, u32[]{:S(2)}, u32[]{:S(2)}) collective-permute-start(f32[10,40,128]{2,1,0:T(8,128)S(1)} %get-tuple-element.22), channel_id=1, source_target_pairs={{0,15},{1,0},{2,1},{3,2},{4,3},{5,4},{6,5},{7,6},{8,7},{9,8},{10,9... | collective-permute-start | bytes 614408 | tf_op jit(solution)/shard_map/ppermute | solution.py:639
  15.2 2.1 %collective-permute-start = (f32[55,16,128]{2,1,0:T(8,128)S(1)}, f32[55,16,128]{2,1,0:T(8,128)S(1)}, u32[]{:S(2)}, u32[]{:S(2)}) collective-permute-start(f32[55,16,128]{2,1,0:T(8,128)S(1)} %get-tuple-element.19), channel_id=1, source_target_pairs={{0,16},{16,32},{32,48},{48,64},{64,80},{80,96},{96,112},{112,0},{1... | collective-permute-start | bytes 1351688 | tf_op jit(solution)/shard_map/ppermute | solution.py:639
  17.3 0.0 collective-permute-start.1
  17.3 4.3 %collective-permute-done.2.down_ref = f32[10,56,128]{2,1,0:T(8,128)S(1)} collective-permute-done((f32[10,56,128]{2,1,0:T(8,128)S(1)}, f32[10,56,128]{2,1,0:T(8,128)S(1)}, u32[]{:S(2)}, u32[]{:S(2)}) %collective-permute-start.2) | collective-permute-done | bytes 286752 | tf_op jit(solution)/shard_map/ppermute | solution.py:639
  21.7 0.0 collective-permute-done.3.up_ref
  21.7 2.4 %collective-permute-start.4 = (f32[4,96,128]{2,1,0:T(8,128)S(1)}, f32[4,96,128]{2,1,0:T(8,128)S(1)}, u32[]{:S(2)}, u32[]{:S(2)}) collective-permute-start(f32[4,96,128]{2,1,0:T(8,128)S(1)} %slice.24), channel_id=1, source_target_pairs={{0,16},{16,32},{32,48},{48,64},{64,80},{80,96},{96,112},{112,0},{1... | collective-permute-start | bytes 589832 | tf_op jit(solution)/shard_map/ppermute | solution.py:639
  24.2 0.0 collective-permute-start.5
  24.2 0.0 collective-permute-done.1.right_ref
  24.2 4.7 %collective-permute-done.5.cr_ref = f32[3,96,128]{2,1,0:T(8,128)S(1)} collective-permute-done((f32[3,96,128]{2,1,0:T(8,128)S(1)}, f32[3,96,128]{2,1,0:T(8,128)S(1)}, u32[]{:S(2)}, u32[]{:S(2)}) %collective-permute-start.5) | collective-permute-done | bytes 147488 | tf_op jit(solution)/shard_map/ppermute | solution.py:639
  28.9 0.0 collective-permute-done.left_ref
  28.9 0.0 collective-permute-done.4.cl_ref
  28.9 0.0 copy-done.1
  28.9 7.4 %shard_map.69 = (f32[15,14,24,128]{3,2,1,0:T(8,128)S(1)}, f32[4,3,9,16,128]{4,3,2,1,0:T(8,128)S(1)}, f32[8,128]{1,0:T(8,128)S(1)}, f32[15,16,128]{2,1,0:T(8,128)...) custom-call(s32[8,9,16,128]{3,2,1,0:T(8,128)S(1)} %copy-done.1, ...), custom_call_target="tpu_custom_call" | custom-call | tf_op jit(solution)/shard_map/pallas_call | solution.py:673
  36.3 0.3 collective-permute-start.6
  36.6 0.2 collective-permute-start.7
  36.8 1.7 %collective-permute-done.6.left_ref = f32[15,16,128]{2,1,0:T(8,128)S(1)} collective-permute-done((f32[15,16,128]{2,1,0:T(8,128)S(1)}, f32[15,16,128]{2,1,0:T(8,128)S(1)}, u32[]{:S(2)}, u32[]{:S(2)}) %collective-permute-start.6) | collective-permute-done | bytes 122912 | tf_op jit(solution)/shard_map/ppermute | solution.py:639
  38.5 2.7 %collective-permute-done.7.right_ref = f32[15,16,128]{2,1,0:T(8,128)S(1)} collective-permute-done((f32[15,16,128]{2,1,0:T(8,128)S(1)}, f32[15,16,128]{2,1,0:T(8,128)S(1)}, u32[]{:S(2)}, u32[]{:S(2)}) %collective-permute-start.7) | collective-permute-done | bytes 122912 | tf_op jit(solution)/shard_map/ppermute | solution.py:639
  41.3 0.1 collective-permute-start.8
  41.4 4.8 %collective-permute-start.9 = (f32[15,16,128]{2,1,0:T(8,128)S(1)}, f32[15,16,128]{2,1,0:T(8,128)S(1)}, u32[]{:S(2)}, u32[]{:S(2)}) collective-permute-start(f32[15,16,128]{2,1,0:T(8,128)S(1)} %pad_maximum_fusion.1), channel_id=1, source_target_pairs={{0,15},{1,0},{2,1},{3,2},{4,3},{5,4},{6,5},{7,6},{8,7},{9,8},{10,9... | collective-permute-start | bytes 368648 | tf_op jit(solution)/shard_map/ppermute | solution.py:639
  46.2 2.2 %collective-permute-done.8.down_ref = f32[15,16,128]{2,1,0:T(8,128)S(1)} collective-permute-done((f32[15,16,128]{2,1,0:T(8,128)S(1)}, f32[15,16,128]{2,1,0:T(8,128)S(1)}, u32[]{:S(2)}, u32[]{:S(2)}) %collective-permute-start.8) | collective-permute-done | bytes 122912 | tf_op jit(solution)/shard_map/ppermute | solution.py:639
  48.4 0.0 collective-permute-done.9.up_ref
  48.4 6.8 %shard_map.70 = (f32[3,3,9,16,128]{4,3,2,1,0:T(8,128)S(1)}, f32[128,128]{1,0:T(8,128)S(1)}) custom-call(f32[15,14,24,128]{3,2,1,0:T(8,128)S(1)} %get-tuple-element.23.els_ref, f32[4,3,9,16,128]{4,3,2,1,0:T(8,128)S(1)} %get-tuple-element.24.own_ref, f32[8,128]{1,0:T(8,128)S(1)} %get-tuple-element.25.dots_ref, ...), custom_call_target="tpu_custom_call" | custom-call | tf_op jit(solution)/shard_map/pallas_call | solution.py:681
  55.2 19.1 %all_to_all.11 = f32[128,1,128]{2,1,0:T(1,128)S(1)} all-to-all(f32[128,1,128]{2,1,0:T(1,128)S(1)} %bitcast.5), channel_id=1, replica_groups=mesh['gx'=8,'gy'=16] {'gx','gy'}, dimensions={0} | all-to-all | bytes 131072 | tf_op jit(solution)/shard_map/all_to_all | solution.py:684
  74.4 1.3 %shard_map.71 = (f32[3,9,16,128]{3,2,1,0:T(8,128)}, f32[3,9,16,128]{3,2,1,0:T(8,128)}) custom-call(f32[128,128]{1,0:T(8,128)S(1)} %bitcast.4, f32[4,3,9,16,128]{4,3,2,1,0:T(8,128)S(1)} %get-tuple-element.24.own_ref, f32[3,3,9,16,128]{4,3,2,1,0:T(8,128)S(1)} %get-tuple-element.31.tail_ref), custom_call_target="tpu_custom_call" | custom-call | tf_op jit(solution)/shard_map/pallas_call | solution.py:685
  (15 shorter events, 0.1 us)
Async XLA Ops:
  0.6 1.1 %copy-start = (s32[8,9,16,128]{3,2,1,0:T(8,128)S(1)}, s32[8,9,16,128]{3,2,1,0:T(8,128)}, u32[]{:S(2)}) copy-start(s32[8,9,16,128]{3,2,1,0:T(8,128)} %flags_ref.1) | copy-start | bytes 1769476
  1.7 1.0 %copy-start.2 = (f32[6,9,16,128]{3,2,1,0:T(8,128)S(1)}, f32[6,9,16,128]{3,2,1,0:T(8,128)}, u32[]{:S(2)}) copy-start(f32[6,9,16,128]{3,2,1,0:T(8,128)} %flow_ref.1) | copy-start | bytes 1327108
  2.7 0.9 %copy-start.4 = (f32[3,9,16,128]{3,2,1,0:T(8,128)S(1)}, f32[3,9,16,128]{3,2,1,0:T(8,128)}, u32[]{:S(2)}) copy-start(f32[3,9,16,128]{3,2,1,0:T(8,128)} %load_hbm.1) | copy-start | bytes 663556
  3.6 0.7 copy-start.5
  4.3 0.7 copy-start.6
  5.0 23.9 %copy-start.1 = (s32[8,9,16,128]{3,2,1,0:T(8,128)S(1)}, s32[8,9,16,128]{3,2,1,0:T(8,128)}, u32[]{:S(2)}) copy-start(s32[8,9,16,128]{3,2,1,0:T(8,128)} %flags_ref.1) | copy-start | bytes 1769476
  5.0 23.9 %copy-start.3 = (f32[6,9,16,128]{3,2,1,0:T(8,128)S(1)}, f32[6,9,16,128]{3,2,1,0:T(8,128)}, u32[]{:S(2)}) copy-start(f32[6,9,16,128]{3,2,1,0:T(8,128)} %flow_ref.1) | copy-start | bytes 1327108
  8.3 13.4 %collective-permute-start.2 = (f32[10,56,128]{2,1,0:T(8,128)S(1)}, f32[10,56,128]{2,1,0:T(8,128)S(1)}, u32[]{:S(2)}, u32[]{:S(2)}) collective-permute-start(f32[10,56,128]{2,1,0:T(8,128)S(1)} %get-tuple-element.21), channel_id=1, source_target_pairs={{0,1},{1,2},{2,3},{3,4},{4,5},{5,6},{6,7},{7,8},{8,9},{9,10},{10,1... | collective-permute-start | bytes 860168 | tf_op jit(solution)/shard_map/ppermute | solution.py:639
  10.8 10.9 %collective-permute-start.3 = (f32[10,40,128]{2,1,0:T(8,128)S(1)}, f32[10,40,128]{2,1,0:T(8,128)S(1)}, u32[]{:S(2)}, u32[]{:S(2)}) collective-permute-start(f32[10,40,128]{2,1,0:T(8,128)S(1)} %get-tuple-element.22), channel_id=1, source_target_pairs={{0,15},{1,0},{2,1},{3,2},{4,3},{5,4},{6,5},{7,6},{8,7},{9,8},{10,9... | collective-permute-start | bytes 614408 | tf_op jit(solution)/shard_map/ppermute | solution.py:639
  15.2 13.7 %collective-permute-start = (f32[55,16,128]{2,1,0:T(8,128)S(1)}, f32[55,16,128]{2,1,0:T(8,128)S(1)}, u32[]{:S(2)}, u32[]{:S(2)}) collective-permute-start(f32[55,16,128]{2,1,0:T(8,128)S(1)} %get-tuple-element.19), channel_id=1, source_target_pairs={{0,16},{16,32},{32,48},{48,64},{64,80},{80,96},{96,112},{112,0},{1... | collective-permute-start | bytes 1351688 | tf_op jit(solution)/shard_map/ppermute | solution.py:639
  17.3 6.9 %collective-permute-start.1 = (f32[38,16,128]{2,1,0:T(8,128)S(1)}, f32[38,16,128]{2,1,0:T(8,128)S(1)}, u32[]{:S(2)}, u32[]{:S(2)}) collective-permute-start(f32[38,16,128]{2,1,0:T(8,128)S(1)} %get-tuple-element.20), channel_id=1, source_target_pairs={{0,112},{16,0},{32,16},{48,32},{64,48},{80,64},{96,80},{112,96},{1... | collective-permute-start | bytes 933896 | tf_op jit(solution)/shard_map/ppermute | solution.py:639
  21.7 7.2 %collective-permute-start.4 = (f32[4,96,128]{2,1,0:T(8,128)S(1)}, f32[4,96,128]{2,1,0:T(8,128)S(1)}, u32[]{:S(2)}, u32[]{:S(2)}) collective-permute-start(f32[4,96,128]{2,1,0:T(8,128)S(1)} %slice.24), channel_id=1, source_target_pairs={{0,16},{16,32},{32,48},{48,64},{64,80},{80,96},{96,112},{112,0},{1... | collective-permute-start | bytes 589832 | tf_op jit(solution)/shard_map/ppermute | solution.py:639
  24.2 4.7 %collective-permute-start.5 = (f32[3,96,128]{2,1,0:T(8,128)S(1)}, f32[3,96,128]{2,1,0:T(8,128)S(1)}, u32[]{:S(2)}, u32[]{:S(2)}) collective-permute-start(f32[3,96,128]{2,1,0:T(8,128)S(1)} %slice.25), channel_id=1, source_target_pairs={{0,112},{16,0},{32,16},{48,32},{64,48},{80,64},{96,80},{112,96},{1... | collective-permute-start | bytes 442376 | tf_op jit(solution)/shard_map/ppermute | solution.py:639
  36.3 2.2 %collective-permute-start.6 = (f32[15,16,128]{2,1,0:T(8,128)S(1)}, f32[15,16,128]{2,1,0:T(8,128)S(1)}, u32[]{:S(2)}, u32[]{:S(2)}) collective-permute-start(f32[15,16,128]{2,1,0:T(8,128)S(1)} %get-tuple-element.26), channel_id=1, source_target_pairs={{0,16},{16,32},{32,48},{48,64},{64,80},{80,96},{96,112},{112,0},{1... | collective-permute-start | bytes 368648 | tf_op jit(solution)/shard_map/ppermute | solution.py:639
  36.6 4.6 %collective-permute-start.7 = (f32[15,16,128]{2,1,0:T(8,128)S(1)}, f32[15,16,128]{2,1,0:T(8,128)S(1)}, u32[]{:S(2)}, u32[]{:S(2)}) collective-permute-start(f32[15,16,128]{2,1,0:T(8,128)S(1)} %get-tuple-element.27), channel_id=1, source_target_pairs={{0,112},{16,0},{32,16},{48,32},{64,48},{80,64},{96,80},{112,96},{1... | collective-permute-start | bytes 368648 | tf_op jit(solution)/shard_map/ppermute | solution.py:639
  41.3 7.1 %collective-permute-start.8 = (f32[15,16,128]{2,1,0:T(8,128)S(1)}, f32[15,16,128]{2,1,0:T(8,128)S(1)}, u32[]{:S(2)}, u32[]{:S(2)}) collective-permute-start(f32[15,16,128]{2,1,0:T(8,128)S(1)} %pad_maximum_fusion), channel_id=1, source_target_pairs={{0,1},{1,2},{2,3},{3,4},{4,5},{5,6},{6,7},{7,8},{8,9},{9,10},{10,1... | collective-permute-start | bytes 368648 | tf_op jit(solution)/shard_map/ppermute | solution.py:639
  41.4 7.0 %collective-permute-start.9 = (f32[15,16,128]{2,1,0:T(8,128)S(1)}, f32[15,16,128]{2,1,0:T(8,128)S(1)}, u32[]{:S(2)}, u32[]{:S(2)}) collective-permute-start(f32[15,16,128]{2,1,0:T(8,128)S(1)} %pad_maximum_fusion.1), channel_id=1, source_target_pairs={{0,15},{1,0},{2,1},{3,2},{4,3},{5,4},{6,5},{7,6},{8,7},{9,8},{10,9... | collective-permute-start | bytes 368648 | tf_op jit(solution)/shard_map/ppermute | solution.py:639

commit v3 on v2

--- a/solution.py
+++ b/solution.py
@@ -165,35 +165,33 @@
     )
 
 
+def odd():
+    return lax.rem(lax.axis_index("gx"), 2)
+
+
 def ask(flag):
     return jnp.where(flag, 0.0, 1.0).astype(F32)
 
 
-def offset_kernel(load_hbm, flags_hbm, flow_hbm, active_ref, die_ref,
-                  part_ref, right_ref, left_ref, up_ref, down_ref, contact_ref,
-                  lower_ref, upper_ref, load_ref, flags_ref, flow_ref, load_sem, flags_sem, flow_sem):
-    copies = [
-        [pltpu.make_async_copy(source.at[m], target.at[m], sem.at[m]) for m in range(source.shape[0])]
-        for source, target, sem in (
-            (flags_hbm, flags_ref, flags_sem), (flow_hbm, flow_ref, flow_sem), (load_hbm, load_ref, load_sem))
-    ]
-    for group in copies:
-        for copy in group:
-            copy.start()
-    lane = lanes()
-    last_lane = lane == DZ - 1
-    zero = jnp.zeros((8, DZ), F32)
+def top_fields(active_ref, die_ref):
     last = lax.broadcasted_iota(jnp.int32, (OY, DZ), 1) == DZ - 1
     same = lax.broadcasted_iota(jnp.int32, (OY, OY), 0) == lax.broadcasted_iota(jnp.int32, (OY, OY), 1)
 
     def on_rows(row):
-        return jnp.sum(jnp.where(same, jnp.broadcast_to(row, (OY, OY)), 0.0), axis=1, keepdims=True)
-
-    die_rows = []
+        turned = jnp.sum(jnp.where(same, jnp.broadcast_to(row, (OY, OY)), 0.0), axis=1, keepdims=True)
+        return jnp.where(last, turned, 0.0)
+
+    contact, die = [], []
     for x in range(OX):
         stiff = CONTACT_STIFF * active_ref[x : x + 1].astype(F32)
-        contact_ref[x] = jnp.where(last, on_rows(stiff), 0.0)
-        die_rows.append(jnp.where(last, on_rows(stiff * die_ref[x : x + 1]), 0.0))
+        contact.append(on_rows(stiff))
+        die.append(on_rows(stiff * die_ref[x : x + 1]))
+    return contact, die
+
+
+def own_part(flags_ref, flow_ref, part_ref, lower_ref, upper_ref):
+    last_lane = lanes() == DZ - 1
+    zero = jnp.zeros((8, DZ), F32)
 
     def clear(x, _):
         for m in range(6):
@@ -202,9 +200,6 @@
         return 0
 
     lax.fori_loop(0, OX + 1, clear, 0)
-    for group in copies[:2]:
-        for copy in group:
-            copy.wait()
     for row in (0, 8):
 
         def element(x, behind):
@@ -216,20 +211,50 @@
 
         behind = lax.fori_loop(0, OX, element, [zero] * 12)
         store_y(behind, lower_ref, upper_ref, OX, row)
-
-    def finish(x, _):
+    for x in range(OX + 1):
         for c in range(3):
             for row in (0, 8, 16):
                 part_ref[c, x, row : row + 8] = merge_yz(lower_ref, upper_ref, c, x, row, last_lane) * (-1.0 / 16.0)
-        return 0
-
-    lax.fori_loop(0, OX + 1, finish, 0, unroll=2)
-    for copy in copies[2]:
+
+
+def add_load(part_ref, load_ref, die):
+    for x in range(OX):
+        for c in range(3):
+            value = part_ref[c, x, 0:OY] + load_ref[c, x]
+            part_ref[c, x, 0:OY] = value + die[x] if c == 2 else value
+
+
+def part_kernel(load_ref, flags_ref, flow_ref, active_ref, die_ref, part_ref, contact_ref, lower_ref, upper_ref):
+    contact, die = top_fields(active_ref, die_ref)
+    for x in range(OX):
+        contact_ref[x] = contact[x]
+    own_part(flags_ref, flow_ref, part_ref, lower_ref, upper_ref)
+    add_load(part_ref, load_ref, die)
+
+
+def slab_kernel(load_hbm, flags_hbm, flow_hbm, active_hbm, die_hbm, right_hbm, left_hbm, first_hbm, second_hbm,
+                right_ref, left_ref, rows_ref, part_ref, contact_ref, lower_ref, upper_ref,
+                load_ref, flags_ref, flow_ref, active_ref, die_ref, load_sem, flags_sem, flow_sem, top_sem, out_sem):
+    small = [
+        pltpu.make_async_copy(active_hbm, active_ref, top_sem.at[0]),
+        pltpu.make_async_copy(die_hbm, die_ref, top_sem.at[1]),
+    ]
+    large = [
+        [pltpu.make_async_copy(source.at[m], target.at[m], sem.at[m]) for m in range(source.shape[0])]
+        for source, target, sem in (
+            (flags_hbm, flags_ref, flags_sem), (flow_hbm, flow_ref, flow_sem), (load_hbm, load_ref, load_sem))
+    ]
+    for group in (small, *large):
+        for copy in group:
+            copy.start()
+    for copy in small:
         copy.wait()
+    contact, die = top_fields(active_ref, die_ref)
     for x in range(OX):
-        for c in range(3):
-            value = part_ref[c, x, 0:OY] + load_ref[c, x]
-            part_ref[c, x, 0:OY] = value + die_rows[x] if c == 2 else value
+        contact_ref[x] = contact[x]
+    for group in large[:2]:
+        for copy in group:
+            copy.wait()
 
     def field(f, x, rows):
         if f < 8:
@@ -244,6 +269,38 @@
             right_ref[3 * f + i] = field(f, 6 + i, whole)
         for i in range(2):
             left_ref[2 * f + i] = field(f, i, whole)
+    outs = [
+        pltpu.make_async_copy(right_ref.at[0:42], right_hbm.at[0:42], out_sem.at[0]),
+        pltpu.make_async_copy(left_ref.at[0:28], left_hbm.at[0:28], out_sem.at[1]),
+    ]
+    for copy in outs:
+        copy.start()
+
+    def slabs(x, _):
+        for f in range(NEL):
+            rows_ref[0, x, 3 * f : 3 * f + 3] = field(f, x, slice(13, 16))
+            rows_ref[1, x, 2 * f : 2 * f + 2] = field(f, x, slice(0, 2))
+        return 0
+
+    lax.fori_loop(0, OX, slabs, 0)
+    own_part(flags_ref, flow_ref, part_ref, lower_ref, upper_ref)
+    for copy in large[2]:
+        copy.wait()
+    add_load(part_ref, load_ref, die)
+
+    def part_slabs(x, _):
+        for c in range(3):
+            rows_ref[0, x, 42 + 4 * c : 46 + 4 * c] = part_ref[c, x, 13:17]
+            rows_ref[1, x, 28 + 3 * c : 31 + 3 * c] = part_ref[c, x, 0:3]
+        return 0
+
+    lax.fori_loop(0, OX + 1, part_slabs, 0)
+    outs += [
+        pltpu.make_async_copy(rows_ref.at[odd()], first_hbm, out_sem.at[2]),
+        pltpu.make_async_copy(rows_ref.at[1 - odd()], second_hbm, out_sem.at[3]),
+    ]
+    for copy in outs[2:]:
+        copy.start()
     for c in range(3):
         for i in range(4):
             right_ref[42 + 4 * c + i] = part_ref[c, 6 + i, 0:16]
@@ -251,22 +308,14 @@
         for i in range(3):
             left_ref[28 + 3 * c + i] = part_ref[c, i, 0:16]
             left_ref[37, 3 * c + i : 3 * c + i + 1] = part_ref[c, i, 16:17]
-
-    def slabs(x, _):
-        for f in range(NEL):
-            up_ref[x, 3 * f : 3 * f + 3] = field(f, x, slice(13, 16))
-            down_ref[x, 2 * f : 2 * f + 2] = field(f, x, slice(0, 2))
-        return 0
-
-    lax.fori_loop(0, OX, slabs, 0)
-
-    def part_slabs(x, _):
-        for c in range(3):
-            up_ref[x, 42 + 4 * c : 46 + 4 * c] = part_ref[c, x, 13:17]
-            down_ref[x, 28 + 3 * c : 31 + 3 * c] = part_ref[c, x, 0:3]
-        return 0
-
-    lax.fori_loop(0, OX + 1, part_slabs, 0)
+    outs += [
+        pltpu.make_async_copy(right_ref.at[42:55], right_hbm.at[42:55], out_sem.at[4]),
+        pltpu.make_async_copy(left_ref.at[28:38], left_hbm.at[28:38], out_sem.at[5]),
+    ]
+    for copy in outs[4:]:
+        copy.start()
+    for copy in outs:
+        copy.wait()
 
 
 def three_steps(els_ref, basis, z_ref, lower_ref, upper_ref):
@@ -365,11 +414,13 @@
     return jnp.sum(values, axis=0, keepdims=True)
 
 
-def first_kernel(flags_ref, flow_ref, contact_ref, part_ref, left_ref, right_ref, down_ref, up_ref, cl_ref, cr_ref,
-                 els_ref, own_ref, dots_ref, right_out, left_out, up_out, down_out,
+def first_kernel(flags_ref, flow_ref, contact_ref, part_ref, left_ref, right_ref, rows_ref, cl_ref, cr_ref,
+                 els_ref, own_ref, dots_ref, right_out, left_out, first_out, second_out,
                  b0, b1, b2, b3, z_ref, lower_ref, upper_ref):
     at_first_x, at_last_x, at_first_y, at_last_y = place()
     has_l, has_r, has_d, has_u = ask(at_first_x), ask(at_last_x), ask(at_first_y), ask(at_last_y)
+    below = odd()
+    above = 1 - below
     zero = jnp.zeros((8, DZ), F32)
     low, high = slice(0, 3), slice(19, 21)
     mid = slice(HALO, HALO + OY)
@@ -399,8 +450,8 @@
             else:
                 value = contact_ref[x]
             els_ref[f, w, mid] = value
-            els_ref[f, w, low] = down_ref[x, 3 * f : 3 * f + 3]
-            els_ref[f, w, high] = up_ref[x, 2 * f : 2 * f + 2]
+            els_ref[f, w, low] = rows_ref[x, below, 3 * f : 3 * f + 3]
+            els_ref[f, w, high] = rows_ref[x, above, 2 * f : 2 * f + 2]
         for c in range(3):
             b0[c, w, mid] = part_ref[c, x, 0:16]
             b0[c, w, 19:20] = part_ref[c, x, 16:17] * has_u
@@ -413,13 +464,13 @@
     for i in range(3):
         for f in range(NEL):
             els_ref[f, i, mid] = left_ref[3 * f + i]
-            els_ref[f, i, low] = cl_ref[i, 3 * f : 3 * f + 3]
-            els_ref[f, i, high] = cl_ref[i, 56 + 2 * f : 58 + 2 * f]
+            els_ref[f, i, low] = cl_ref[i, above, 3 * f : 3 * f + 3]
+            els_ref[f, i, high] = cl_ref[i, below, 2 * f : 2 * f + 2]
     for i in range(2):
         for f in range(NEL):
             els_ref[f, 12 + i, mid] = right_ref[2 * f + i]
-            els_ref[f, 12 + i, low] = cr_ref[i, 3 * f : 3 * f + 3]
-            els_ref[f, 12 + i, high] = cr_ref[i, 56 + 2 * f : 58 + 2 * f]
+            els_ref[f, 12 + i, low] = cr_ref[i, above, 3 * f : 3 * f + 3]
+            els_ref[f, 12 + i, high] = cr_ref[i, below, 2 * f : 2 * f + 2]
 
     def zz(x, _):
         for row in (0, 8, 16):
@@ -432,19 +483,19 @@
         for i in range(4):
             b0[c, i, mid] += left_ref[42 + 4 * c + i] * has_l
             b0[c, i, 19:20] += left_ref[54, 4 * c + i : 4 * c + i + 1] * (has_l * has_u)
-            b0[c, i, 0:4] += cl_ref[i, 42 + 4 * c : 46 + 4 * c] * (has_l * has_d)
-            b0[c, i, 19:22] += cl_ref[i, 84 + 3 * c : 87 + 3 * c] * (has_l * has_u)
+            b0[c, i, 0:4] += cl_ref[i, above, 42 + 4 * c : 46 + 4 * c] * (has_l * has_d)
+            b0[c, i, 19:22] += cl_ref[i, below, 28 + 3 * c : 31 + 3 * c] * (has_l * has_u)
         for i in range(3):
             b0[c, 12 + i, mid] += right_ref[28 + 3 * c + i] * has_r
             b0[c, 12 + i, 19:20] += right_ref[37, 3 * c + i : 3 * c + i + 1] * (has_r * has_u)
-            b0[c, 12 + i, 0:4] += cr_ref[i, 42 + 4 * c : 46 + 4 * c] * (has_r * has_d)
-            b0[c, 12 + i, 19:22] += cr_ref[i, 84 + 3 * c : 87 + 3 * c] * (has_r * has_u)
+            b0[c, 12 + i, 0:4] += cr_ref[i, above, 42 + 4 * c : 46 + 4 * c] * (has_r * has_d)
+            b0[c, 12 + i, 19:22] += cr_ref[i, below, 28 + 3 * c : 31 + 3 * c] * (has_r * has_u)
 
     def edges(x, _):
         inside = jnp.where(x == OX, has_r, 1.0)
         for c in range(3):
-            b0[c, x + HALO, 0:4] += down_ref[x, 42 + 4 * c : 46 + 4 * c] * (inside * has_d)
-            b0[c, x + HALO, 19:22] += up_ref[x, 28 + 3 * c : 31 + 3 * c] * (inside * has_u)
+            b0[c, x + HALO, 0:4] += rows_ref[x, below, 42 + 4 * c : 46 + 4 * c] * (inside * has_d)
+            b0[c, x + HALO, 19:22] += rows_ref[x, above, 28 + 3 * c : 31 + 3 * c] * (inside * has_u)
         return 0
 
     lax.fori_loop(0, OX + 1, edges, 0)
@@ -468,26 +519,33 @@
     for k in range(7):
         dots_ref[k : k + 1] = sum_rows(sums[k])
 
+    def edge_rows(c, x):
+        last, start = b3[c, x, 16:19], b3[c, x, 3:6]
+        return jnp.where(below == 0, last, start), jnp.where(below == 0, start, last)
+
     for i in range(3):
         for c in range(3):
             for out, x in ((right_out, 9 + i), (left_out, 3 + i)):
                 out[3 * c + i] = b3[c, x, mid]
-                out[9 + i, 3 * c : 3 * c + 3] = b3[c, x, 16:19]
-                out[12 + i, 3 * c : 3 * c + 3] = b3[c, x, 3:6]
+                first, second = edge_rows(c, x)
+                out[9 + i, 3 * c : 3 * c + 3] = second
+                out[12 + i, 3 * c : 3 * c + 3] = first
 
     def slabs(x, _):
         for c in range(3):
-            up_out[x, 3 * c : 3 * c + 3] = b3[c, x + HALO, 16:19]
-            down_out[x, 3 * c : 3 * c + 3] = b3[c, x + HALO, 3:6]
+            first, second = edge_rows(c, x + HALO)
+            first_out[x, 3 * c : 3 * c + 3] = first
+            second_out[x, 3 * c : 3 * c + 3] = second
         return 0
 
     lax.fori_loop(0, OX, slabs, 0)
 
 
-def second_kernel(els_ref, own_ref, dots_ref, left_ref, right_ref, down_ref, up_ref,
+def second_kernel(els_ref, own_ref, dots_ref, left_ref, right_ref, first_ref, second_ref,
                   tail_ref, row_ref, b0, b1, b2, b3, z_ref, lower_ref, upper_ref):
     _, at_last_x, _, at_last_y = place()
     has_r, has_u = ask(at_last_x), ask(at_last_y)
+    below = odd()
     zero = jnp.zeros((8, DZ), F32)
     mid = slice(HALO, HALO + OY)
 
@@ -500,8 +558,9 @@
         inside = jnp.where(x >= HALO + OX, has_r, 1.0)
         for c in range(3):
             b0[c, x, 16:24] = zero
-            b0[c, x, 0:3] = down_ref[x, 3 * c : 3 * c + 3] * inside
-            b0[c, x, 19:22] = up_ref[x, 3 * c : 3 * c + 3] * (inside * has_u)
+            one, two = first_ref[x, 3 * c : 3 * c + 3] * inside, second_ref[x, 3 * c : 3 * c + 3] * inside
+            b0[c, x, 0:3] = jnp.where(below == 0, one, two)
+            b0[c, x, 19:22] = jnp.where(below == 0, two, one) * has_u
         return 0
 
     lax.fori_loop(0, WX, edges, 0)
@@ -639,44 +698,62 @@
     return lax.ppermute(value, axis, [(i, (i + steps) % count) for i in range(count)])
 
 
-def exchange(right, left, up, down, top):
+def wind(value, forward):
+    count_x, count_y = lax.axis_size("gx"), lax.axis_size("gy")
+    pairs = []
+    for x in range(count_x):
+        for y in range(count_y):
+            ahead = y + 1 if (x % 2 == 0) == forward else y - 1
+            goal = (x, ahead) if 0 <= ahead < count_y else (x ^ 1, y)
+            pairs.append((x * count_y + y, goal[0] * count_y + goal[1]))
+    return lax.ppermute(value, ("gx", "gy"), pairs)
+
+
+def exchange(right, left, first, second):
     from_left = rotate(right, "gx", 1)
     from_right = rotate(left, "gx", -1)
-    from_down = rotate(up, "gy", 1)
-    from_up = rotate(down, "gy", -1)
-    corners = jnp.concatenate([from_down, from_up], axis=1)
-    corner_left = rotate(corners[6:top], "gx", 1)
-    corner_right = rotate(corners[0:3], "gx", -1)
-    return from_left, from_right, from_down, from_up, corner_left, corner_right
-
-
-def exchange_in_turn(right, left, up, down):
+    rows = jnp.stack([wind(first, True), wind(second, False)], axis=1)
+    corner_left = rotate(rows[6:10], "gx", 1)
+    corner_right = rotate(rows[0:3], "gx", -1)
+    return from_left, from_right, rows, corner_left, corner_right
+
+
+def exchange_in_turn(right, left, first, second):
     from_left = rotate(right, "gx", 1)
     from_right = rotate(left, "gx", -1)
-    up = jnp.concatenate([from_left[9:12], up, from_right[9:12]], axis=0)
-    down = jnp.concatenate([from_left[12:15], down, from_right[12:15]], axis=0)
-    return from_left, from_right, rotate(up, "gy", 1), rotate(down, "gy", -1)
+    first = jnp.concatenate([from_left[9:12], first, from_right[9:12]], axis=0)
+    second = jnp.concatenate([from_left[12:15], second, from_right[12:15]], axis=0)
+    return from_left, from_right, wind(first, True), wind(second, False)
 
 
 def body(load, plastic_flags, flow_dir, contact_flags, die_depth):
-    hbm, vmem = pl.BlockSpec(memory_space=pltpu.HBM), pl.BlockSpec(memory_space=pltpu.VMEM)
-    part, right, left, up, down, contact = call(
-        offset_kernel,
-        [shape(3, OX + 1, WY, DZ), shape(55, OY, DZ), shape(38, OY, DZ), shape(OX + 1, 56, DZ),
-         shape(OX + 1, 40, DZ), shape(OX, OY, DZ)],
-        [(6, OX + 1, WY + 8, DZ)] * 2
-        + [(3, OX, OY, DZ), pltpu.VMEM((8, OX, OY, DZ), jnp.int32), (6, OX, OY, DZ)]
-        + [pltpu.SemaphoreType.DMA((count,)) for count in (3, 8, 6)],
-        in_specs=[hbm, hbm, hbm, vmem, vmem],
-    )(load, plastic_flags, flow_dir, contact_flags, die_depth)
-    halos = exchange(right, left, up, down, 10)
-    els, own, dots, right, left, up, down = call(
+    slabs = [(55, OY, DZ), (38, OY, DZ), (OX + 1, 56, DZ), (OX + 1, 56, DZ)]
+    work = [(6, OX + 1, WY + 8, DZ)] * 2
+    outside = pl.BlockSpec(memory_space=pl.ANY)
+    inputs = (load, plastic_flags, flow_dir, contact_flags, die_depth)
+    right, left, first, second = call(
+        slab_kernel,
+        [shape(*dims) for dims in slabs],
+        slabs[:2] + [(2, OX + 1, 56, DZ), (3, OX + 1, WY, DZ), (OX, OY, DZ)] + work
+        + [(3, OX, OY, DZ), pltpu.VMEM((8, OX, OY, DZ), jnp.int32), (6, OX, OY, DZ),
+           pltpu.VMEM((OX, OY), jnp.int32), (OX, OY)]
+        + [pltpu.SemaphoreType.DMA((count,)) for count in (3, 8, 6, 2, 6)],
+        mebibytes=54,
+        in_specs=[outside] * 5,
+        out_specs=[outside] * 4,
+    )(*inputs)
+    part, contact = call(
+        part_kernel, [shape(3, OX + 1, WY, DZ), shape(OX, OY, DZ)], work,
+        cost_estimate=pl.CostEstimate(flops=4000000, bytes_accessed=2000000, transcendentals=0),
+    )(*inputs)
+    halos = exchange(right, left, first, second)
+    els, own, dots, right, left, first, second = call(
         first_kernel,
         [shape(NEL + 1, WE, WY, DZ), shape(4, 3, OX, OY, DZ), shape(8, DZ), shape(15, OY, DZ), shape(15, OY, DZ),
          shape(OX, 16, DZ), shape(OX, 16, DZ)],
         STEP_SCRATCH,
     )(plastic_flags, flow_dir, contact, part, *halos)
-    halos = exchange_in_turn(right, left, up, down)
+    halos = exchange_in_turn(right, left, first, second)
     count = lax.axis_size("gx") * lax.axis_size("gy")
     tail, line = call(
         second_kernel, [shape(3, 3, OX, OY, DZ), shape(count, DZ)], STEP_SCRATCH

time: 75.9 us -> 69.9 us (0.921)
  starting transfers between devices: 16.9 us -> 10.2 us
  blocking collectives: 19.1 us -> 24.3 us
  local copies, waits for them, and re-layouts: 4.47 us -> 0.03 us
  Pallas kernels: 18.7 us -> 19.8 us
  waiting for transfers between devices: 15.6 us -> 14.6 us
    ppermute x10 -> x6, starting transfers between devices: 16.9 us -> 5.81 us  [rotate(): lax.ppermute(value, axis, [(i, (i + steps) % count) for i in range(count)])]
    ppermute x10 -> x6, waiting for transfers between devices: 15.6 us -> 8.55 us  [rotate(): lax.ppermute(value, axis, [(i, (i + steps) % count) for i in range(count)])]
    ppermute x0 -> x4, waiting for transfers between devices: none -> 6.01 us  [wind(): return lax.ppermute(value, ('gx', 'gy'), pairs)]
    all_to_all x1, blocking collectives: 19.1 us -> 24.3 us  [body(): lines = lax.all_to_all(line, ('gx', 'gy'), 0, 0, tiled=True)]
    ppermute x0 -> x4, starting transfers between devices: none -> 4.41 us  [wind(): return lax.ppermute(value, ('gx', 'gy'), pairs)]
    unnamed x15 -> x10, local copies, waits for them, and re-layouts: 4.42 us -> 0.02 us
    pallas_call x1 -> x2, Pallas kernels: 3.2 us -> 4.33 us  [the longest x1 3.52 us: body(): call(slab_kernel, [shape(*dims) for dims in slabs], slabs[:2] + [(2, OX +...]
  transfers between devices with their start and end apart: 10 -> 10, of which waited for: 5 -> 6; matrix products, arithmetic and copies ran while one was open for 0% -> 0% of each run, Pallas kernels for 0% -> 1%
where the time goes in v3:
time: 69.9 us; the launch traced here: 69.8 us
  blocking collectives  24.3 us (35%)
  Pallas kernels  19.8 us (28%)
  waiting for transfers between devices  14.6 us (21%)
  starting transfers between devices  10.2 us (15%)
  between operations  0.79 us (1%)
    all_to_all x1, blocking collectives, body(): lines = lax.all_to_all(line, ('gx', 'gy'), 0, 0, tiled=True)  24.3 us
    ppermute x6, waiting for transfers between devices, rotate(): lax.ppermute(value, axis, [(i, (i + steps) % count) for i in range(count)])  8.55 us
    pallas_call x1, Pallas kernels, body(): call(first_kernel, [shape(NEL + 1, WE, WY, DZ), shape(4, 3, OX, OY, DZ),...  7.4 us
    pallas_call x1, Pallas kernels, body(): call(second_kernel, [shape(3, 3, OX, OY, DZ), shape(count, DZ)], STEP_SCR...  6.86 us
    ppermute x4, waiting for transfers between devices, wind(): return lax.ppermute(value, ('gx', 'gy'), pairs)  6.01 us
    ppermute x6, starting transfers between devices, rotate(): lax.ppermute(value, axis, [(i, (i + steps) % count) for i in range(count)])  5.81 us
    ppermute x4, starting transfers between devices, wind(): return lax.ppermute(value, ('gx', 'gy'), pairs)  4.41 us
    pallas_call x1, Pallas kernels, body(): call(slab_kernel, [shape(*dims) for dims in slabs], slabs[:2] + [(2, OX +...  3.52 us
  transfers between devices with their start and end apart: 10, of which 6 were waited for; matrix products, arithmetic and copies ran while one was open for 0% of the time, Pallas kernels for 1%

profile of v3, /device:TPU:1, one launch (start us, length us, event | category | flops | bytes accessed | tf_op | source)
XLA Modules:
  0.0 69.8 jit_solution(11478269906183334496)
XLA Ops:
  0.6 0.0 copy-start.1
  0.6 0.0 copy-start
  0.7 0.0 copy-start.4
  0.7 0.0 copy-start.3
  0.7 0.0 copy-start.2
  0.7 3.5 %shard_map.69 = (f32[55,16,128]{2,1,0:T(8,128)}, f32[38,16,128]{2,1,0:T(8,128)}, f32[10,56,128]{2,1,0:T(8,128)}, f32[10,56,128]{2,1,0:T(8,128)}) custom-call(f32[3,9,16,128]{3,2,1,0:T(8,128)} %load_hbm.1, s32[8,9,16,128]{3,2,1,0:T(8,128)} %flags_ref.3, f32[6,9,16,128]{3,2,1,0:T(8,128)} %flow_ref.3, s32[9,16]{1,0:T(8,128)} %active_hbm.1, f32[9,16]{1,0:T(8,128)} %die_hbm.1), custom_call_target="tpu_custom_call" | custom-call | tf_op jit(solution)/shard_map/pallas_call | solution.py:734
  4.2 1.5 %collective-permute-start.2 = (f32[10,56,128]{2,1,0:T(8,128)}, f32[10,56,128]{2,1,0:T(8,128)S(1)}, u32[]{:S(2)}, u32[]{:S(2)}) collective-permute-start(f32[10,56,128]{2,1,0:T(8,128)} %get-tuple-element.21), channel_id=1, source_target_pairs={{0,1},{1,2},{2,3},{3,4},{4,5},{5,6},{6,7},{7,8},{8,9},{9,10},{10,1... | collective-permute-start | bytes 860168 | tf_op jit(solution)/shard_map/ppermute | solution.py:709
  5.7 1.1 %collective-permute-start.3 = (f32[10,56,128]{2,1,0:T(8,128)}, f32[10,56,128]{2,1,0:T(8,128)S(1)}, u32[]{:S(2)}, u32[]{:S(2)}) collective-permute-start(f32[10,56,128]{2,1,0:T(8,128)} %get-tuple-element.22), channel_id=1, source_target_pairs={{0,16},{1,0},{2,1},{3,2},{4,3},{5,4},{6,5},{7,6},{8,7},{9,8},{10,9... | collective-permute-start | bytes 860168 | tf_op jit(solution)/shard_map/ppermute | solution.py:709
  6.8 2.1 %collective-permute-start = (f32[55,16,128]{2,1,0:T(8,128)}, f32[55,16,128]{2,1,0:T(8,128)S(1)}, u32[]{:S(2)}, u32[]{:S(2)}) collective-permute-start(f32[55,16,128]{2,1,0:T(8,128)} %get-tuple-element.19), channel_id=1, source_target_pairs={{0,16},{16,32},{32,48},{48,64},{64,80},{80,96},{96,112},{112,0},{1... | collective-permute-start | bytes 1351688 | tf_op jit(solution)/shard_map/ppermute | solution.py:698
  8.9 0.0 collective-permute-start.1
  8.9 2.5 %collective-permute-done.2 = f32[10,56,128]{2,1,0:T(8,128)S(1)} collective-permute-done((f32[10,56,128]{2,1,0:T(8,128)}, f32[10,56,128]{2,1,0:T(8,128)S(1)}, u32[]{:S(2)}, u32[]{:S(2)}) %collective-permute-start.2) | collective-permute-done | bytes 286752 | tf_op jit(solution)/shard_map/ppermute | solution.py:709
  11.4 1.3 %collective-permute-done.3 = f32[10,56,128]{2,1,0:T(8,128)S(1)} collective-permute-done((f32[10,56,128]{2,1,0:T(8,128)}, f32[10,56,128]{2,1,0:T(8,128)S(1)}, u32[]{:S(2)}, u32[]{:S(2)}) %collective-permute-start.3) | collective-permute-done | bytes 286752 | tf_op jit(solution)/shard_map/ppermute | solution.py:709
  12.7 3.2 %collective-permute-start.4 = (f32[4,2,56,128]{3,2,1,0:T(8,128)S(1)}, f32[4,2,56,128]{3,2,1,0:T(8,128)S(1)}, u32[]{:S(2)}, u32[]{:S(2)}) collective-permute-start(f32[4,2,56,128]{3,2,1,0:T(8,128)S(1)} %fusion), channel_id=1, source_target_pairs={{0,16},{16,32},{32,48},{48,64},{64,80},{80,96},{96,112},{112,0},{1... | collective-permute-start | bytes 688136 | tf_op jit(solution)/shard_map/ppermute | solution.py:698
  16.0 0.0 collective-permute-start.5
  16.0 0.0 copy-done.1
  16.0 0.8 %shard_map.68 = (f32[3,10,24,128]{3,2,1,0:T(8,128)S(1)}, f32[9,16,128]{2,1,0:T(8,128)S(1)}) custom-call(f32[3,9,16,128]{3,2,1,0:T(8,128)S(1)} %copy-done.2, s32[8,9,16,128]{3,2,1,0:T(8,128)S(1)} %copy-done, f32[6,9,16,128]{3,2,1,0:T(8,128)S(1)} %copy-done.1, s32[9,16]{1,0:T(8,128)S(1)} %copy-done.3, f32[9,16]{1,0:T(8,128)S(1)} %copy-done.4), custom_call_target="tpu_custom_call" | custom-call | flops 4000000 | bytes 2000000 | tf_op jit(solution)/shard_map/pallas_call | solution.py:745
  16.9 0.0 collective-permute-done.1.right_ref
  16.9 0.0 collective-permute-done.left_ref
  16.9 4.1 %collective-permute-done.5.cr_ref = f32[3,2,56,128]{3,2,1,0:T(8,128)S(1)} collective-permute-done((f32[3,2,56,128]{3,2,1,0:T(8,128)S(1)}, f32[3,2,56,128]{3,2,1,0:T(8,128)S(1)}, u32[]{:S(2)}, u32[]{:S(2)}) %collective-permute-start.5) | collective-permute-done | bytes 172064 | tf_op jit(solution)/shard_map/ppermute | solution.py:698
  21.0 0.0 collective-permute-done.4.cl_ref
  21.0 7.4 %shard_map.70 = (f32[15,14,24,128]{3,2,1,0:T(8,128)S(1)}, f32[4,3,9,16,128]{4,3,2,1,0:T(8,128)S(1)}, f32[8,128]{1,0:T(8,128)S(1)}, f32[15,16,128]{2,1,0:T(8,128)...) custom-call(s32[8,9,16,128]{3,2,1,0:T(8,128)S(1)} %copy-done, ...), custom_call_target="tpu_custom_call" | custom-call | tf_op jit(solution)/shard_map/pallas_call | solution.py:750
  28.4 0.4 collective-permute-start.6
  28.8 0.2 collective-permute-start.7
  29.0 1.7 %collective-permute-done.6.left_ref = f32[15,16,128]{2,1,0:T(8,128)S(1)} collective-permute-done((f32[15,16,128]{2,1,0:T(8,128)S(1)}, f32[15,16,128]{2,1,0:T(8,128)S(1)}, u32[]{:S(2)}, u32[]{:S(2)}) %collective-permute-start.6) | collective-permute-done | bytes 122912 | tf_op jit(solution)/shard_map/ppermute | solution.py:698
  30.7 2.7 %collective-permute-done.7.right_ref = f32[15,16,128]{2,1,0:T(8,128)S(1)} collective-permute-done((f32[15,16,128]{2,1,0:T(8,128)S(1)}, f32[15,16,128]{2,1,0:T(8,128)S(1)}, u32[]{:S(2)}, u32[]{:S(2)}) %collective-permute-start.7) | collective-permute-done | bytes 122912 | tf_op jit(solution)/shard_map/ppermute | solution.py:698
  33.4 1.0 %collective-permute-start.8 = (f32[15,16,128]{2,1,0:T(8,128)S(1)}, f32[15,16,128]{2,1,0:T(8,128)S(1)}, u32[]{:S(2)}, u32[]{:S(2)}) collective-permute-start(f32[15,16,128]{2,1,0:T(8,128)S(1)} %pad_maximum_fusion.1), channel_id=1, source_target_pairs={{0,1},{1,2},{2,3},{3,4},{4,5},{5,6},{6,7},{7,8},{8,9},{9,10},{10,1... | collective-permute-start | bytes 368648 | tf_op jit(solution)/shard_map/ppermute | solution.py:709
  34.5 0.8 %collective-permute-start.9 = (f32[15,16,128]{2,1,0:T(8,128)S(1)}, f32[15,16,128]{2,1,0:T(8,128)S(1)}, u32[]{:S(2)}, u32[]{:S(2)}) collective-permute-start(f32[15,16,128]{2,1,0:T(8,128)S(1)} %pad_maximum_fusion.2), channel_id=1, source_target_pairs={{0,16},{1,0},{2,1},{3,2},{4,3},{5,4},{6,5},{7,6},{8,7},{9,8},{10,9... | collective-permute-start | bytes 368648 | tf_op jit(solution)/shard_map/ppermute | solution.py:709
  35.2 2.2 %collective-permute-done.8.first_ref = f32[15,16,128]{2,1,0:T(8,128)S(1)} collective-permute-done((f32[15,16,128]{2,1,0:T(8,128)S(1)}, f32[15,16,128]{2,1,0:T(8,128)S(1)}, u32[]{:S(2)}, u32[]{:S(2)}) %collective-permute-start.8) | collective-permute-done | bytes 122912 | tf_op jit(solution)/shard_map/ppermute | solution.py:709
  37.4 0.0 collective-permute-done.9.second_ref
  37.4 6.9 %shard_map.71 = (f32[3,3,9,16,128]{4,3,2,1,0:T(8,128)S(1)}, f32[128,128]{1,0:T(8,128)S(1)}) custom-call(f32[15,14,24,128]{3,2,1,0:T(8,128)S(1)} %get-tuple-element.23.els_ref, f32[4,3,9,16,128]{4,3,2,1,0:T(8,128)S(1)} %get-tuple-element.24.own_ref, f32[8,128]{1,0:T(8,128)S(1)} %get-tuple-element.25.dots_ref, ...), custom_call_target="tpu_custom_call" | custom-call | tf_op jit(solution)/shard_map/pallas_call | solution.py:758
  44.3 24.3 %all_to_all.11 = f32[128,1,128]{2,1,0:T(1,128)S(1)} all-to-all(f32[128,1,128]{2,1,0:T(1,128)S(1)} %bitcast.7), channel_id=1, replica_groups=mesh['gx'=8,'gy'=16] {'gx','gy'}, dimensions={0} | all-to-all | bytes 131072 | tf_op jit(solution)/shard_map/all_to_all | solution.py:761
  68.5 1.3 %shard_map.72 = (f32[3,9,16,128]{3,2,1,0:T(8,128)}, f32[3,9,16,128]{3,2,1,0:T(8,128)}) custom-call(f32[128,128]{1,0:T(8,128)S(1)} %bitcast.6, f32[4,3,9,16,128]{4,3,2,1,0:T(8,128)S(1)} %get-tuple-element.24.own_ref, f32[3,3,9,16,128]{4,3,2,1,0:T(8,128)S(1)} %get-tuple-element.31.tail_ref), custom_call_target="tpu_custom_call" | custom-call | tf_op jit(solution)/shard_map/pallas_call | solution.py:762
  (11 shorter events, 0.1 us)
Async XLA Ops:
  0.6 15.4 %copy-start.1 = (f32[6,9,16,128]{3,2,1,0:T(8,128)S(1)}, f32[6,9,16,128]{3,2,1,0:T(8,128)}, u32[]{:S(2)}) copy-start(f32[6,9,16,128]{3,2,1,0:T(8,128)} %flow_ref.3) | copy-start | bytes 1327108
  0.6 15.4 %copy-start = (s32[8,9,16,128]{3,2,1,0:T(8,128)S(1)}, s32[8,9,16,128]{3,2,1,0:T(8,128)}, u32[]{:S(2)}) copy-start(s32[8,9,16,128]{3,2,1,0:T(8,128)} %flags_ref.3) | copy-start | bytes 1769476
  0.7 15.4 %copy-start.4 = (f32[9,16]{1,0:T(8,128)S(1)}, f32[9,16]{1,0:T(8,128)}, u32[]{:S(2)}) copy-start(f32[9,16]{1,0:T(8,128)} %die_hbm.1) | copy-start | bytes 1732
  0.7 15.4 %copy-start.3 = (s32[9,16]{1,0:T(8,128)S(1)}, s32[9,16]{1,0:T(8,128)}, u32[]{:S(2)}) copy-start(s32[9,16]{1,0:T(8,128)} %active_hbm.1) | copy-start | bytes 1732
  0.7 15.4 %copy-start.2 = (f32[3,9,16,128]{3,2,1,0:T(8,128)S(1)}, f32[3,9,16,128]{3,2,1,0:T(8,128)}, u32[]{:S(2)}) copy-start(f32[3,9,16,128]{3,2,1,0:T(8,128)} %load_hbm.1) | copy-start | bytes 663556
  4.2 7.2 %collective-permute-start.2 = (f32[10,56,128]{2,1,0:T(8,128)}, f32[10,56,128]{2,1,0:T(8,128)S(1)}, u32[]{:S(2)}, u32[]{:S(2)}) collective-permute-start(f32[10,56,128]{2,1,0:T(8,128)} %get-tuple-element.21), channel_id=1, source_target_pairs={{0,1},{1,2},{2,3},{3,4},{4,5},{5,6},{6,7},{7,8},{8,9},{9,10},{10,1... | collective-permute-start | bytes 860168 | tf_op jit(solution)/shard_map/ppermute | solution.py:709
  5.7 7.0 %collective-permute-start.3 = (f32[10,56,128]{2,1,0:T(8,128)}, f32[10,56,128]{2,1,0:T(8,128)S(1)}, u32[]{:S(2)}, u32[]{:S(2)}) collective-permute-start(f32[10,56,128]{2,1,0:T(8,128)} %get-tuple-element.22), channel_id=1, source_target_pairs={{0,16},{1,0},{2,1},{3,2},{4,3},{5,4},{6,5},{7,6},{8,7},{9,8},{10,9... | collective-permute-start | bytes 860168 | tf_op jit(solution)/shard_map/ppermute | solution.py:709
  6.8 10.1 %collective-permute-start = (f32[55,16,128]{2,1,0:T(8,128)}, f32[55,16,128]{2,1,0:T(8,128)S(1)}, u32[]{:S(2)}, u32[]{:S(2)}) collective-permute-start(f32[55,16,128]{2,1,0:T(8,128)} %get-tuple-element.19), channel_id=1, source_target_pairs={{0,16},{16,32},{32,48},{48,64},{64,80},{80,96},{96,112},{112,0},{1... | collective-permute-start | bytes 1351688 | tf_op jit(solution)/shard_map/ppermute | solution.py:698
  8.9 8.0 %collective-permute-start.1 = (f32[38,16,128]{2,1,0:T(8,128)}, f32[38,16,128]{2,1,0:T(8,128)S(1)}, u32[]{:S(2)}, u32[]{:S(2)}) collective-permute-start(f32[38,16,128]{2,1,0:T(8,128)} %get-tuple-element.20), channel_id=1, source_target_pairs={{0,112},{16,0},{32,16},{48,32},{64,48},{80,64},{96,80},{112,96},{1... | collective-permute-start | bytes 933896 | tf_op jit(solution)/shard_map/ppermute | solution.py:698
  12.7 8.3 %collective-permute-start.4 = (f32[4,2,56,128]{3,2,1,0:T(8,128)S(1)}, f32[4,2,56,128]{3,2,1,0:T(8,128)S(1)}, u32[]{:S(2)}, u32[]{:S(2)}) collective-permute-start(f32[4,2,56,128]{3,2,1,0:T(8,128)S(1)} %fusion), channel_id=1, source_target_pairs={{0,16},{16,32},{32,48},{48,64},{64,80},{80,96},{96,112},{112,0},{1... | collective-permute-start | bytes 688136 | tf_op jit(solution)/shard_map/ppermute | solution.py:698
  16.0 5.1 %collective-permute-start.5 = (f32[3,2,56,128]{3,2,1,0:T(8,128)S(1)}, f32[3,2,56,128]{3,2,1,0:T(8,128)S(1)}, u32[]{:S(2)}, u32[]{:S(2)}) collective-permute-start(f32[3,2,56,128]{3,2,1,0:T(8,128)S(1)} %fusion.1), channel_id=1, source_target_pairs={{0,112},{16,0},{32,16},{48,32},{64,48},{80,64},{96,80},{112,96},{1... | collective-permute-start | bytes 516104 | tf_op jit(solution)/shard_map/ppermute | solution.py:698
  28.4 2.2 %collective-permute-start.6 = (f32[15,16,128]{2,1,0:T(8,128)S(1)}, f32[15,16,128]{2,1,0:T(8,128)S(1)}, u32[]{:S(2)}, u32[]{:S(2)}) collective-permute-start(f32[15,16,128]{2,1,0:T(8,128)S(1)} %get-tuple-element.26), channel_id=1, source_target_pairs={{0,16},{16,32},{32,48},{48,64},{64,80},{80,96},{96,112},{112,0},{1... | collective-permute-start | bytes 368648 | tf_op jit(solution)/shard_map/ppermute | solution.py:698
  28.8 4.6 %collective-permute-start.7 = (f32[15,16,128]{2,1,0:T(8,128)S(1)}, f32[15,16,128]{2,1,0:T(8,128)S(1)}, u32[]{:S(2)}, u32[]{:S(2)}) collective-permute-start(f32[15,16,128]{2,1,0:T(8,128)S(1)} %get-tuple-element.27), channel_id=1, source_target_pairs={{0,112},{16,0},{32,16},{48,32},{64,48},{80,64},{96,80},{112,96},{1... | collective-permute-start | bytes 368648 | tf_op jit(solution)/shard_map/ppermute | solution.py:698
  33.4 4.0 %collective-permute-start.8 = (f32[15,16,128]{2,1,0:T(8,128)S(1)}, f32[15,16,128]{2,1,0:T(8,128)S(1)}, u32[]{:S(2)}, u32[]{:S(2)}) collective-permute-start(f32[15,16,128]{2,1,0:T(8,128)S(1)} %pad_maximum_fusion.1), channel_id=1, source_target_pairs={{0,1},{1,2},{2,3},{3,4},{4,5},{5,6},{6,7},{7,8},{8,9},{9,10},{10,1... | collective-permute-start | bytes 368648 | tf_op jit(solution)/shard_map/ppermute | solution.py:709
  34.5 2.9 %collective-permute-start.9 = (f32[15,16,128]{2,1,0:T(8,128)S(1)}, f32[15,16,128]{2,1,0:T(8,128)S(1)}, u32[]{:S(2)}, u32[]{:S(2)}) collective-permute-start(f32[15,16,128]{2,1,0:T(8,128)S(1)} %pad_maximum_fusion.2), channel_id=1, source_target_pairs={{0,16},{1,0},{2,1},{3,2},{4,3},{5,4},{6,5},{7,6},{8,7},{9,8},{10,9... | collective-permute-start | bytes 368648 | tf_op jit(solution)/shard_map/ppermute | solution.py:709

commit v4 on v3

--- a/solution.py
+++ b/solution.py
@@ -27,6 +27,25 @@
 NEL = 14
 CONTACT_AT = 13
 ZZ_AT = 14
+
+
+ROW_AT = (0, 54, 108, 168, 222, 276, 336, 390, 444, 498)
+SLAB_ROWS = 512
+LOW_PART, HIGH_PART = slice(0, 168), slice(336, 512)
+
+
+def up_rows(x, c):
+    at = ROW_AT[x] + (42 if x < OX else 0) + 4 * c
+    return slice(at, at + 4)
+
+
+def down_rows(x, c):
+    at = ROW_AT[x] + (28 if x < OX else 0) + 3 * c
+    return slice(at, at + 3)
+
+
+def moved(rows, by):
+    return slice(rows.start - by, rows.stop - by)
 
 
 def lanes():
@@ -240,9 +259,10 @@
         pltpu.make_async_copy(die_hbm, die_ref, top_sem.at[1]),
     ]
     large = [
-        [pltpu.make_async_copy(source.at[m], target.at[m], sem.at[m]) for m in range(source.shape[0])]
-        for source, target, sem in (
-            (flags_hbm, flags_ref, flags_sem), (flow_hbm, flow_ref, flow_sem), (load_hbm, load_ref, load_sem))
+        [pltpu.make_async_copy(source.at[m : m + step], target.at[m : m + step], sem.at[m])
+         for m in range(0, source.shape[0], step)]
+        for source, target, sem, step in (
+            (flags_hbm, flags_ref, flags_sem, 4), (flow_hbm, flow_ref, flow_sem, 3), (load_hbm, load_ref, load_sem, 3))
     ]
     for group in (small, *large):
         for copy in group:
@@ -276,25 +296,19 @@
     for copy in outs:
         copy.start()
 
-    def slabs(x, _):
+    for x in range(OX):
         for f in range(NEL):
-            rows_ref[0, x, 3 * f : 3 * f + 3] = field(f, x, slice(13, 16))
-            rows_ref[1, x, 2 * f : 2 * f + 2] = field(f, x, slice(0, 2))
-        return 0
-
-    lax.fori_loop(0, OX, slabs, 0)
+            rows_ref[0, ROW_AT[x] + 3 * f : ROW_AT[x] + 3 * f + 3] = field(f, x, slice(13, 16))
+            rows_ref[1, ROW_AT[x] + 2 * f : ROW_AT[x] + 2 * f + 2] = field(f, x, slice(0, 2))
     own_part(flags_ref, flow_ref, part_ref, lower_ref, upper_ref)
     for copy in large[2]:
         copy.wait()
     add_load(part_ref, load_ref, die)
 
-    def part_slabs(x, _):
-        for c in range(3):
-            rows_ref[0, x, 42 + 4 * c : 46 + 4 * c] = part_ref[c, x, 13:17]
-            rows_ref[1, x, 28 + 3 * c : 31 + 3 * c] = part_ref[c, x, 0:3]
-        return 0
-
-    lax.fori_loop(0, OX + 1, part_slabs, 0)
+    for x in range(OX + 1):
+        for c in range(3):
+            rows_ref[0, up_rows(x, c)] = part_ref[c, x, 13:17]
+            rows_ref[1, down_rows(x, c)] = part_ref[c, x, 0:3]
     outs += [
         pltpu.make_async_copy(rows_ref.at[odd()], first_hbm, out_sem.at[2]),
         pltpu.make_async_copy(rows_ref.at[1 - odd()], second_hbm, out_sem.at[3]),
@@ -391,7 +405,7 @@
             lax.fori_loop(0, (end + 1 - first_pair) // 2, pair, carry)
 
         for x in range(step, end + 1):
-            for row in (0, 8, 16):
+            for row in (0, 8, 16) if step < HALO else (HALO, HALO + 8):
                 for c in range(3):
                     here = basis[step - 1][c, x, row : row + 8]
                     value = merge_yz(lower_ref, upper_ref, c, x, row, last_lane) * (scale / 16.0)
@@ -418,7 +432,7 @@
                  els_ref, own_ref, dots_ref, right_out, left_out, first_out, second_out,
                  b0, b1, b2, b3, z_ref, lower_ref, upper_ref):
     at_first_x, at_last_x, at_first_y, at_last_y = place()
-    has_l, has_r, has_d, has_u = ask(at_first_x), ask(at_last_x), ask(at_first_y), ask(at_last_y)
+    has_l, has_r, has_u = ask(at_first_x), ask(at_last_x), ask(at_last_y)
     below = odd()
     above = 1 - below
     zero = jnp.zeros((8, DZ), F32)
@@ -450,27 +464,29 @@
             else:
                 value = contact_ref[x]
             els_ref[f, w, mid] = value
-            els_ref[f, w, low] = rows_ref[x, below, 3 * f : 3 * f + 3]
-            els_ref[f, w, high] = rows_ref[x, above, 2 * f : 2 * f + 2]
         for c in range(3):
             b0[c, w, mid] = part_ref[c, x, 0:16]
             b0[c, w, 19:20] = part_ref[c, x, 16:17] * has_u
         return 0
 
     lax.fori_loop(0, OX, own, 0)
+    for x in range(OX):
+        for f in range(NEL):
+            els_ref[f, x + HALO, low] = rows_ref[below, ROW_AT[x] + 3 * f : ROW_AT[x] + 3 * f + 3]
+            els_ref[f, x + HALO, high] = rows_ref[above, ROW_AT[x] + 2 * f : ROW_AT[x] + 2 * f + 2]
     for c in range(3):
         b0[c, 12, mid] = part_ref[c, OX, 0:16] * has_r
         b0[c, 12, 19:20] = part_ref[c, OX, 16:17] * (has_r * has_u)
     for i in range(3):
         for f in range(NEL):
             els_ref[f, i, mid] = left_ref[3 * f + i]
-            els_ref[f, i, low] = cl_ref[i, above, 3 * f : 3 * f + 3]
-            els_ref[f, i, high] = cl_ref[i, below, 2 * f : 2 * f + 2]
+            els_ref[f, i, low] = cl_ref[above, ROW_AT[i] + 3 * f : ROW_AT[i] + 3 * f + 3]
+            els_ref[f, i, high] = cl_ref[below, ROW_AT[i] + 2 * f : ROW_AT[i] + 2 * f + 2]
     for i in range(2):
         for f in range(NEL):
             els_ref[f, 12 + i, mid] = right_ref[2 * f + i]
-            els_ref[f, 12 + i, low] = cr_ref[i, above, 3 * f : 3 * f + 3]
-            els_ref[f, 12 + i, high] = cr_ref[i, below, 2 * f : 2 * f + 2]
+            els_ref[f, 12 + i, low] = cr_ref[above, ROW_AT[i] + 3 * f : ROW_AT[i] + 3 * f + 3]
+            els_ref[f, 12 + i, high] = cr_ref[below, ROW_AT[i] + 2 * f : ROW_AT[i] + 2 * f + 2]
 
     def zz(x, _):
         for row in (0, 8, 16):
@@ -478,27 +494,27 @@
         return 0
 
     lax.fori_loop(0, WE, zz, 0)
+
+    def from_below(piece):
+        return jnp.where(at_first_y, 0.0, piece)
 
     for c in range(3):
         for i in range(4):
             b0[c, i, mid] += left_ref[42 + 4 * c + i] * has_l
             b0[c, i, 19:20] += left_ref[54, 4 * c + i : 4 * c + i + 1] * (has_l * has_u)
-            b0[c, i, 0:4] += cl_ref[i, above, 42 + 4 * c : 46 + 4 * c] * (has_l * has_d)
-            b0[c, i, 19:22] += cl_ref[i, below, 28 + 3 * c : 31 + 3 * c] * (has_l * has_u)
+            b0[c, i, 0:4] += from_below(cl_ref[above, moved(up_rows(6 + i, c), HIGH_PART.start)]) * has_l
+            b0[c, i, 19:22] += cl_ref[below, moved(down_rows(6 + i, c), HIGH_PART.start)] * (has_l * has_u)
         for i in range(3):
             b0[c, 12 + i, mid] += right_ref[28 + 3 * c + i] * has_r
             b0[c, 12 + i, 19:20] += right_ref[37, 3 * c + i : 3 * c + i + 1] * (has_r * has_u)
-            b0[c, 12 + i, 0:4] += cr_ref[i, above, 42 + 4 * c : 46 + 4 * c] * (has_r * has_d)
-            b0[c, 12 + i, 19:22] += cr_ref[i, below, 28 + 3 * c : 31 + 3 * c] * (has_r * has_u)
-
-    def edges(x, _):
-        inside = jnp.where(x == OX, has_r, 1.0)
-        for c in range(3):
-            b0[c, x + HALO, 0:4] += rows_ref[x, below, 42 + 4 * c : 46 + 4 * c] * (inside * has_d)
-            b0[c, x + HALO, 19:22] += rows_ref[x, above, 28 + 3 * c : 31 + 3 * c] * (inside * has_u)
-        return 0
-
-    lax.fori_loop(0, OX + 1, edges, 0)
+            b0[c, 12 + i, 0:4] += from_below(cr_ref[above, up_rows(i, c)]) * has_r
+            b0[c, 12 + i, 19:22] += cr_ref[below, down_rows(i, c)] * (has_r * has_u)
+
+    for x in range(OX + 1):
+        inside = has_r if x == OX else 1.0
+        for c in range(3):
+            b0[c, x + HALO, 0:4] += from_below(rows_ref[below, up_rows(x, c)]) * inside
+            b0[c, x + HALO, 19:22] += rows_ref[above, down_rows(x, c)] * (inside * has_u)
 
     basis = (b0, b1, b2, b3)
     three_steps(els_ref, basis, z_ref, lower_ref, upper_ref)
@@ -526,19 +542,17 @@
     for i in range(3):
         for c in range(3):
             for out, x in ((right_out, 9 + i), (left_out, 3 + i)):
-                out[3 * c + i] = b3[c, x, mid]
+                out[16 * (3 * c + i) : 16 * (3 * c + i) + 16] = b3[c, x, mid]
                 first, second = edge_rows(c, x)
-                out[9 + i, 3 * c : 3 * c + 3] = second
-                out[12 + i, 3 * c : 3 * c + 3] = first
-
-    def slabs(x, _):
+                at = 9 * i + 3 * c
+                out[144 + at : 147 + at] = second
+                out[176 + at : 179 + at] = first
+    for x in range(OX):
         for c in range(3):
             first, second = edge_rows(c, x + HALO)
-            first_out[x, 3 * c : 3 * c + 3] = first
-            second_out[x, 3 * c : 3 * c + 3] = second
-        return 0
-
-    lax.fori_loop(0, OX, slabs, 0)
+            at = 9 * x + 3 * c
+            first_out[at : at + 3] = first
+            second_out[at : at + 3] = second
 
 
 def second_kernel(els_ref, own_ref, dots_ref, left_ref, right_ref, first_ref, second_ref,
@@ -554,21 +568,21 @@
             b0[c, x + HALO, mid] = own_ref[3, c, x]
         return 0
 
-    def edges(x, _):
-        inside = jnp.where(x >= HALO + OX, has_r, 1.0)
+    for x in range(WX):
+        inside = has_r if x >= HALO + OX else 1.0
         for c in range(3):
             b0[c, x, 16:24] = zero
-            one, two = first_ref[x, 3 * c : 3 * c + 3] * inside, second_ref[x, 3 * c : 3 * c + 3] * inside
+            at = 88 + 9 * x if x < HALO else 9 * (x - HALO) if x < HALO + OX else 120 + 9 * (x - HALO - OX)
+            rows = slice(at + 3 * c, at + 3 * c + 3)
+            one, two = first_ref[rows] * inside, second_ref[rows] * inside
             b0[c, x, 0:3] = jnp.where(below == 0, one, two)
             b0[c, x, 19:22] = jnp.where(below == 0, two, one) * has_u
-        return 0
-
-    lax.fori_loop(0, WX, edges, 0)
     lax.fori_loop(0, OX, own, 0)
     for c in range(3):
         for i in range(3):
-            b0[c, i, mid] = left_ref[3 * c + i]
-            b0[c, 12 + i, mid] = right_ref[3 * c + i] * has_r
+            block = slice(16 * (3 * c + i), 16 * (3 * c + i) + 16)
+            b0[c, i, mid] = left_ref[block]
+            b0[c, 12 + i, mid] = right_ref[block] * has_r
 
     basis = (b0, b1, b2, b3)
     three_steps(els_ref, basis, z_ref, lower_ref, upper_ref)
@@ -712,29 +726,29 @@
 def exchange(right, left, first, second):
     from_left = rotate(right, "gx", 1)
     from_right = rotate(left, "gx", -1)
-    rows = jnp.stack([wind(first, True), wind(second, False)], axis=1)
-    corner_left = rotate(rows[6:10], "gx", 1)
-    corner_right = rotate(rows[0:3], "gx", -1)
+    rows = jnp.stack([wind(first, True), wind(second, False)])
+    corner_left = rotate(rows[:, HIGH_PART], "gx", 1)
+    corner_right = rotate(rows[:, LOW_PART], "gx", -1)
     return from_left, from_right, rows, corner_left, corner_right
 
 
 def exchange_in_turn(right, left, first, second):
     from_left = rotate(right, "gx", 1)
     from_right = rotate(left, "gx", -1)
-    first = jnp.concatenate([from_left[9:12], first, from_right[9:12]], axis=0)
-    second = jnp.concatenate([from_left[12:15], second, from_right[12:15]], axis=0)
+    first = jnp.concatenate([first, from_left[144:176], from_right[144:176]], axis=0)
+    second = jnp.concatenate([second, from_left[176:208], from_right[176:208]], axis=0)
     return from_left, from_right, wind(first, True), wind(second, False)
 
 
 def body(load, plastic_flags, flow_dir, contact_flags, die_depth):
-    slabs = [(55, OY, DZ), (38, OY, DZ), (OX + 1, 56, DZ), (OX + 1, 56, DZ)]
+    slabs = [(55, OY, DZ), (38, OY, DZ), (SLAB_ROWS, DZ), (SLAB_ROWS, DZ)]
     work = [(6, OX + 1, WY + 8, DZ)] * 2
     outside = pl.BlockSpec(memory_space=pl.ANY)
     inputs = (load, plastic_flags, flow_dir, contact_flags, die_depth)
     right, left, first, second = call(
         slab_kernel,
         [shape(*dims) for dims in slabs],
-        slabs[:2] + [(2, OX + 1, 56, DZ), (3, OX + 1, WY, DZ), (OX, OY, DZ)] + work
+        slabs[:2] + [(2, SLAB_ROWS, DZ), (3, OX + 1, WY, DZ), (OX, OY, DZ)] + work
         + [(3, OX, OY, DZ), pltpu.VMEM((8, OX, OY, DZ), jnp.int32), (6, OX, OY, DZ),
            pltpu.VMEM((OX, OY), jnp.int32), (OX, OY)]
         + [pltpu.SemaphoreType.DMA((count,)) for count in (3, 8, 6, 2, 6)],
@@ -749,8 +763,7 @@
     halos = exchange(right, left, first, second)
     els, own, dots, right, left, first, second = call(
         first_kernel,
-        [shape(NEL + 1, WE, WY, DZ), shape(4, 3, OX, OY, DZ), shape(8, DZ), shape(15, OY, DZ), shape(15, OY, DZ),
-         shape(OX, 16, DZ), shape(OX, 16, DZ)],
+        [shape(NEL + 1, WE, WY, DZ), shape(4, 3, OX, OY, DZ), shape(8, DZ), shape(208, DZ), shape(208, DZ), shape(88, DZ), shape(88, DZ)],
         STEP_SCRATCH,
     )(plastic_flags, flow_dir, contact, part, *halos)
     halos = exchange_in_turn(right, left, first, second)

time: 69.9 us -> 67.6 us (0.967)
  waiting for transfers between devices: 14.6 us -> 13.1 us
    ppermute x4, waiting for transfers between devices: 6.01 us -> 5.23 us  [wind(): return lax.ppermute(value, ('gx', 'gy'), pairs)]
  transfers between devices with their start and end apart: 10 -> 10, of which waited for: 6 -> 7; matrix products, arithmetic and copies ran while one was open for 0% -> 0% of each run, Pallas kernels for 1% -> 1%
where the time goes in v4:
time: 67.6 us; the launch traced here: 67.5 us
  blocking collectives  23.9 us (35%)
  Pallas kernels  19.3 us (29%)
  waiting for transfers between devices  13.1 us (19%)
  starting transfers between devices  10.3 us (15%)
  between operations  0.78 us (1%)
    all_to_all x1, blocking collectives, body(): lines = lax.all_to_all(line, ('gx', 'gy'), 0, 0, tiled=True)  23.9 us
    ppermute x6, waiting for transfers between devices, rotate(): lax.ppermute(value, axis, [(i, (i + steps) % count) for i in range(count)])  7.87 us
    pallas_call x1, Pallas kernels, body(): call(first_kernel, [shape(NEL + 1, WE, WY, DZ), shape(4, 3, OX, OY, DZ),...  7.2 us
    pallas_call x1, Pallas kernels, body(): call(second_kernel, [shape(3, 3, OX, OY, DZ), shape(count, DZ)], STEP_SCR...  6.73 us
    ppermute x6, starting transfers between devices, rotate(): lax.ppermute(value, axis, [(i, (i + steps) % count) for i in range(count)])  5.87 us
    ppermute x4, waiting for transfers between devices, wind(): return lax.ppermute(value, ('gx', 'gy'), pairs)  5.23 us
    ppermute x4, starting transfers between devices, wind(): return lax.ppermute(value, ('gx', 'gy'), pairs)  4.41 us
    pallas_call x1, Pallas kernels, body(): call(slab_kernel, [shape(*dims) for dims in slabs], slabs[:2] + [(2, SLAB...  3.32 us
  transfers between devices with their start and end apart: 10, of which 7 were waited for; matrix products, arithmetic and copies ran while one was open for 0% of the time, Pallas kernels for 1%

profile of v4, /device:TPU:1, one launch (start us, length us, event | category | flops | bytes accessed | tf_op | source)
XLA Modules:
  0.0 67.5 jit_solution(17056302215597480362)
XLA Ops:
  0.6 0.0 copy-start.1
  0.6 0.0 copy-start
  0.7 0.0 copy-start.4
  0.7 0.0 copy-start.3
  0.7 0.0 copy-start.2
  0.7 3.3 %shard_map.69 = (f32[55,16,128]{2,1,0:T(8,128)}, f32[38,16,128]{2,1,0:T(8,128)}, f32[512,128]{1,0:T(8,128)}, f32[512,128]{1,0:T(8,128)}) custom-call(f32[3,9,16,128]{3,2,1,0:T(8,128)} %load_hbm.1, s32[8,9,16,128]{3,2,1,0:T(8,128)} %flags_ref.3, f32[6,9,16,128]{3,2,1,0:T(8,128)} %flow_ref.3, s32[9,16]{1,0:T(8,128)} %active_hbm.1, f32[9,16]{1,0:T(8,128)} %die_hbm.1), custom_call_target="tpu_custom_call" | custom-call | tf_op jit(solution)/shard_map/pallas_call | solution.py:748
  4.0 1.5 %collective-permute-start.2 = (f32[512,128]{1,0:T(8,128)}, f32[512,128]{1,0:T(8,128)S(1)}, u32[]{:S(2)}, u32[]{:S(2)}) collective-permute-start(f32[512,128]{1,0:T(8,128)} %get-tuple-element.21), channel_id=1, source_target_pairs={{0,1},{1,2},{2,3},{3,4},{4,5},{5,6},{6,7},{7,8},{8,9},{9,10},{10,1... | collective-permute-start | bytes 786440 | tf_op jit(solution)/shard_map/ppermute | solution.py:723
  5.5 1.1 %collective-permute-start.3 = (f32[512,128]{1,0:T(8,128)}, f32[512,128]{1,0:T(8,128)S(1)}, u32[]{:S(2)}, u32[]{:S(2)}) collective-permute-start(f32[512,128]{1,0:T(8,128)} %get-tuple-element.22), channel_id=1, source_target_pairs={{0,16},{1,0},{2,1},{3,2},{4,3},{5,4},{6,5},{7,6},{8,7},{9,8},{10,9... | collective-permute-start | bytes 786440 | tf_op jit(solution)/shard_map/ppermute | solution.py:723
  6.6 2.1 %collective-permute-start = (f32[55,16,128]{2,1,0:T(8,128)}, f32[55,16,128]{2,1,0:T(8,128)S(1)}, u32[]{:S(2)}, u32[]{:S(2)}) collective-permute-start(f32[55,16,128]{2,1,0:T(8,128)} %get-tuple-element.19), channel_id=1, source_target_pairs={{0,16},{16,32},{32,48},{48,64},{64,80},{80,96},{96,112},{112,0},{1... | collective-permute-start | bytes 1351688 | tf_op jit(solution)/shard_map/ppermute | solution.py:712
  8.7 0.0 collective-permute-start.1
  8.7 1.8 %collective-permute-done.2 = f32[512,128]{1,0:T(8,128)S(1)} collective-permute-done((f32[512,128]{1,0:T(8,128)}, f32[512,128]{1,0:T(8,128)S(1)}, u32[]{:S(2)}, u32[]{:S(2)}) %collective-permute-start.2) | collective-permute-done | bytes 262176 | tf_op jit(solution)/shard_map/ppermute | solution.py:723
  10.5 1.5 %collective-permute-done.3 = f32[512,128]{1,0:T(8,128)S(1)} collective-permute-done((f32[512,128]{1,0:T(8,128)}, f32[512,128]{1,0:T(8,128)S(1)}, u32[]{:S(2)}, u32[]{:S(2)}) %collective-permute-start.3) | collective-permute-done | bytes 262176 | tf_op jit(solution)/shard_map/ppermute | solution.py:723
  12.0 3.3 %collective-permute-start.4 = (f32[2,176,128]{2,1,0:T(8,128)S(1)}, f32[2,176,128]{2,1,0:T(8,128)S(1)}, u32[]{:S(2)}, u32[]{:S(2)}) collective-permute-start(f32[2,176,128]{2,1,0:T(8,128)S(1)} %fusion), channel_id=1, source_target_pairs={{0,16},{16,32},{32,48},{48,64},{64,80},{80,96},{96,112},{112,0},{1... | collective-permute-start | bytes 540680 | tf_op jit(solution)/shard_map/ppermute | solution.py:712
  15.3 0.0 collective-permute-start.5
  15.3 0.0 copy-done.1
  15.4 0.8 %shard_map.68 = (f32[3,10,24,128]{3,2,1,0:T(8,128)S(1)}, f32[9,16,128]{2,1,0:T(8,128)S(1)}) custom-call(f32[3,9,16,128]{3,2,1,0:T(8,128)S(1)} %copy-done.2, s32[8,9,16,128]{3,2,1,0:T(8,128)S(1)} %copy-done, f32[6,9,16,128]{3,2,1,0:T(8,128)S(1)} %copy-done.1, s32[9,16]{1,0:T(8,128)S(1)} %copy-done.3, f32[9,16]{1,0:T(8,128)S(1)} %copy-done.4), custom_call_target="tpu_custom_call" | custom-call | flops 4000000 | bytes 2000000 | tf_op jit(solution)/shard_map/pallas_call | solution.py:759
  16.2 0.0 collective-permute-done.1.right_ref
  16.2 3.9 %collective-permute-done.5.cr_ref = f32[2,168,128]{2,1,0:T(8,128)S(1)} collective-permute-done((f32[2,168,128]{2,1,0:T(8,128)S(1)}, f32[2,168,128]{2,1,0:T(8,128)S(1)}, u32[]{:S(2)}, u32[]{:S(2)}) %collective-permute-start.5) | collective-permute-done | bytes 172064 | tf_op jit(solution)/shard_map/ppermute | solution.py:712
  20.1 0.0 collective-permute-done.4.cl_ref
  20.2 0.0 collective-permute-done.left_ref
  20.2 7.2 %shard_map.70 = (f32[15,14,24,128]{3,2,1,0:T(8,128)S(1)}, f32[4,3,9,16,128]{4,3,2,1,0:T(8,128)S(1)}, f32[8,128]{1,0:T(8,128)S(1)}, f32[208,128]{1,0:T(8,128)S(1)...) custom-call(s32[8,9,16,128]{3,2,1,0:T(8,128)S(1)} %copy-done, ...), custom_call_target="tpu_custom_call" | custom-call | tf_op jit(solution)/shard_map/pallas_call | solution.py:764
  27.4 0.1 collective-permute-start.6
  27.4 0.5 collective-permute-start.7
  27.9 1.3 %collective-permute-done.6.left_ref = f32[208,128]{1,0:T(8,128)S(1)} collective-permute-done((f32[208,128]{1,0:T(8,128)S(1)}, f32[208,128]{1,0:T(8,128)S(1)}, u32[]{:S(2)}, u32[]{:S(2)}) %collective-permute-start.6) | collective-permute-done | bytes 106528 | tf_op jit(solution)/shard_map/ppermute | solution.py:712
  29.1 2.7 %collective-permute-done.7.right_ref = f32[208,128]{1,0:T(8,128)S(1)} collective-permute-done((f32[208,128]{1,0:T(8,128)S(1)}, f32[208,128]{1,0:T(8,128)S(1)}, u32[]{:S(2)}, u32[]{:S(2)}) %collective-permute-start.7) | collective-permute-done | bytes 106528 | tf_op jit(solution)/shard_map/ppermute | solution.py:712
  31.9 1.0 %collective-permute-start.8 = (f32[152,128]{1,0:T(8,128)S(1)}, f32[152,128]{1,0:T(8,128)S(1)}, u32[]{:S(2)}, u32[]{:S(2)}) collective-permute-start(f32[152,128]{1,0:T(8,128)S(1)} %pad_maximum_fusion.1), channel_id=1, source_target_pairs={{0,1},{1,2},{2,3},{3,4},{4,5},{5,6},{6,7},{7,8},{8,9},{9,10},{10,1... | collective-permute-start | bytes 233480 | tf_op jit(solution)/shard_map/ppermute | solution.py:723
  32.9 0.8 %collective-permute-start.9 = (f32[152,128]{1,0:T(8,128)S(1)}, f32[152,128]{1,0:T(8,128)S(1)}, u32[]{:S(2)}, u32[]{:S(2)}) collective-permute-start(f32[152,128]{1,0:T(8,128)S(1)} %pad_maximum_fusion.2), channel_id=1, source_target_pairs={{0,16},{1,0},{2,1},{3,2},{4,3},{5,4},{6,5},{7,6},{8,7},{9,8},{10,9... | collective-permute-start | bytes 233480 | tf_op jit(solution)/shard_map/ppermute | solution.py:723
  33.7 1.7 %collective-permute-done.8.first_ref = f32[152,128]{1,0:T(8,128)S(1)} collective-permute-done((f32[152,128]{1,0:T(8,128)S(1)}, f32[152,128]{1,0:T(8,128)S(1)}, u32[]{:S(2)}, u32[]{:S(2)}) %collective-permute-start.8) | collective-permute-done | bytes 77856 | tf_op jit(solution)/shard_map/ppermute | solution.py:723
  35.4 0.2 collective-permute-done.9.second_ref
  35.6 6.7 %shard_map.71 = (f32[3,3,9,16,128]{4,3,2,1,0:T(8,128)S(1)}, f32[128,128]{1,0:T(8,128)S(1)}) custom-call(f32[15,14,24,128]{3,2,1,0:T(8,128)S(1)} %get-tuple-element.23.els_ref, f32[4,3,9,16,128]{4,3,2,1,0:T(8,128)S(1)} %get-tuple-element.24.own_ref, f32[8,128]{1,0:T(8,128)S(1)} %get-tuple-element.25.dots_ref, f32[208,128]{1,0:T(8,128)S(1)} %collective-permute-done.6.left_ref, ...), custom_call_target="tpu_custom_call" | custom-call | tf_op jit(solution)/shard_map/pallas_call | solution.py:771
  42.3 23.9 %all_to_all.11 = f32[128,1,128]{2,1,0:T(1,128)S(1)} all-to-all(f32[128,1,128]{2,1,0:T(1,128)S(1)} %bitcast.7), channel_id=1, replica_groups=mesh['gx'=8,'gy'=16] {'gx','gy'}, dimensions={0} | all-to-all | bytes 131072 | tf_op jit(solution)/shard_map/all_to_all | solution.py:774
  66.2 1.3 %shard_map.72 = (f32[3,9,16,128]{3,2,1,0:T(8,128)}, f32[3,9,16,128]{3,2,1,0:T(8,128)}) custom-call(f32[128,128]{1,0:T(8,128)S(1)} %bitcast.6, f32[4,3,9,16,128]{4,3,2,1,0:T(8,128)S(1)} %get-tuple-element.24.own_ref, f32[3,3,9,16,128]{4,3,2,1,0:T(8,128)S(1)} %get-tuple-element.31.tail_ref), custom_call_target="tpu_custom_call" | custom-call | tf_op jit(solution)/shard_map/pallas_call | solution.py:775
  (11 shorter events, 0.1 us)
Async XLA Ops:
  0.6 14.7 %copy-start.1 = (f32[6,9,16,128]{3,2,1,0:T(8,128)S(1)}, f32[6,9,16,128]{3,2,1,0:T(8,128)}, u32[]{:S(2)}) copy-start(f32[6,9,16,128]{3,2,1,0:T(8,128)} %flow_ref.3) | copy-start | bytes 1327108
  0.6 14.7 %copy-start = (s32[8,9,16,128]{3,2,1,0:T(8,128)S(1)}, s32[8,9,16,128]{3,2,1,0:T(8,128)}, u32[]{:S(2)}) copy-start(s32[8,9,16,128]{3,2,1,0:T(8,128)} %flags_ref.3) | copy-start | bytes 1769476
  0.7 14.7 %copy-start.4 = (f32[9,16]{1,0:T(8,128)S(1)}, f32[9,16]{1,0:T(8,128)}, u32[]{:S(2)}) copy-start(f32[9,16]{1,0:T(8,128)} %die_hbm.1) | copy-start | bytes 1732
  0.7 14.7 %copy-start.3 = (s32[9,16]{1,0:T(8,128)S(1)}, s32[9,16]{1,0:T(8,128)}, u32[]{:S(2)}) copy-start(s32[9,16]{1,0:T(8,128)} %active_hbm.1) | copy-start | bytes 1732
  0.7 14.7 %copy-start.2 = (f32[3,9,16,128]{3,2,1,0:T(8,128)S(1)}, f32[3,9,16,128]{3,2,1,0:T(8,128)}, u32[]{:S(2)}) copy-start(f32[3,9,16,128]{3,2,1,0:T(8,128)} %load_hbm.1) | copy-start | bytes 663556
  4.0 6.5 %collective-permute-start.2 = (f32[512,128]{1,0:T(8,128)}, f32[512,128]{1,0:T(8,128)S(1)}, u32[]{:S(2)}, u32[]{:S(2)}) collective-permute-start(f32[512,128]{1,0:T(8,128)} %get-tuple-element.21), channel_id=1, source_target_pairs={{0,1},{1,2},{2,3},{3,4},{4,5},{5,6},{6,7},{7,8},{8,9},{9,10},{10,1... | collective-permute-start | bytes 786440 | tf_op jit(solution)/shard_map/ppermute | solution.py:723
  5.5 6.5 %collective-permute-start.3 = (f32[512,128]{1,0:T(8,128)}, f32[512,128]{1,0:T(8,128)S(1)}, u32[]{:S(2)}, u32[]{:S(2)}) collective-permute-start(f32[512,128]{1,0:T(8,128)} %get-tuple-element.22), channel_id=1, source_target_pairs={{0,16},{1,0},{2,1},{3,2},{4,3},{5,4},{6,5},{7,6},{8,7},{9,8},{10,9... | collective-permute-start | bytes 786440 | tf_op jit(solution)/shard_map/ppermute | solution.py:723
  6.6 13.5 %collective-permute-start = (f32[55,16,128]{2,1,0:T(8,128)}, f32[55,16,128]{2,1,0:T(8,128)S(1)}, u32[]{:S(2)}, u32[]{:S(2)}) collective-permute-start(f32[55,16,128]{2,1,0:T(8,128)} %get-tuple-element.19), channel_id=1, source_target_pairs={{0,16},{16,32},{32,48},{48,64},{64,80},{80,96},{96,112},{112,0},{1... | collective-permute-start | bytes 1351688 | tf_op jit(solution)/shard_map/ppermute | solution.py:712
  8.7 7.6 %collective-permute-start.1 = (f32[38,16,128]{2,1,0:T(8,128)}, f32[38,16,128]{2,1,0:T(8,128)S(1)}, u32[]{:S(2)}, u32[]{:S(2)}) collective-permute-start(f32[38,16,128]{2,1,0:T(8,128)} %get-tuple-element.20), channel_id=1, source_target_pairs={{0,112},{16,0},{32,16},{48,32},{64,48},{80,64},{96,80},{112,96},{1... | collective-permute-start | bytes 933896 | tf_op jit(solution)/shard_map/ppermute | solution.py:712
  12.0 8.1 %collective-permute-start.4 = (f32[2,176,128]{2,1,0:T(8,128)S(1)}, f32[2,176,128]{2,1,0:T(8,128)S(1)}, u32[]{:S(2)}, u32[]{:S(2)}) collective-permute-start(f32[2,176,128]{2,1,0:T(8,128)S(1)} %fusion), channel_id=1, source_target_pairs={{0,16},{16,32},{32,48},{48,64},{64,80},{80,96},{96,112},{112,0},{1... | collective-permute-start | bytes 540680 | tf_op jit(solution)/shard_map/ppermute | solution.py:712
  15.3 4.8 %collective-permute-start.5 = (f32[2,168,128]{2,1,0:T(8,128)S(1)}, f32[2,168,128]{2,1,0:T(8,128)S(1)}, u32[]{:S(2)}, u32[]{:S(2)}) collective-permute-start(f32[2,168,128]{2,1,0:T(8,128)S(1)} %fusion.1), channel_id=1, source_target_pairs={{0,112},{16,0},{32,16},{48,32},{64,48},{80,64},{96,80},{112,96},{1... | collective-permute-start | bytes 516104 | tf_op jit(solution)/shard_map/ppermute | solution.py:712
  27.4 1.8 %collective-permute-start.6 = (f32[208,128]{1,0:T(8,128)S(1)}, f32[208,128]{1,0:T(8,128)S(1)}, u32[]{:S(2)}, u32[]{:S(2)}) collective-permute-start(f32[208,128]{1,0:T(8,128)S(1)} %get-tuple-element.26), channel_id=1, source_target_pairs={{0,16},{16,32},{32,48},{48,64},{64,80},{80,96},{96,112},{112,0},{1... | collective-permute-start | bytes 319496 | tf_op jit(solution)/shard_map/ppermute | solution.py:712
  27.4 4.4 %collective-permute-start.7 = (f32[208,128]{1,0:T(8,128)S(1)}, f32[208,128]{1,0:T(8,128)S(1)}, u32[]{:S(2)}, u32[]{:S(2)}) collective-permute-start(f32[208,128]{1,0:T(8,128)S(1)} %get-tuple-element.27), channel_id=1, source_target_pairs={{0,112},{16,0},{32,16},{48,32},{64,48},{80,64},{96,80},{112,96},{1... | collective-permute-start | bytes 319496 | tf_op jit(solution)/shard_map/ppermute | solution.py:712
  31.9 3.5 %collective-permute-start.8 = (f32[152,128]{1,0:T(8,128)S(1)}, f32[152,128]{1,0:T(8,128)S(1)}, u32[]{:S(2)}, u32[]{:S(2)}) collective-permute-start(f32[152,128]{1,0:T(8,128)S(1)} %pad_maximum_fusion.1), channel_id=1, source_target_pairs={{0,1},{1,2},{2,3},{3,4},{4,5},{5,6},{6,7},{7,8},{8,9},{9,10},{10,1... | collective-permute-start | bytes 233480 | tf_op jit(solution)/shard_map/ppermute | solution.py:723
  32.9 2.7 %collective-permute-start.9 = (f32[152,128]{1,0:T(8,128)S(1)}, f32[152,128]{1,0:T(8,128)S(1)}, u32[]{:S(2)}, u32[]{:S(2)}) collective-permute-start(f32[152,128]{1,0:T(8,128)S(1)} %pad_maximum_fusion.2), channel_id=1, source_target_pairs={{0,16},{1,0},{2,1},{3,2},{4,3},{5,4},{6,5},{7,6},{8,7},{9,8},{10,9... | collective-permute-start | bytes 233480 | tf_op jit(solution)/shard_map/ppermute | solution.py:723

commit v5 on v4

--- a/solution.py
+++ b/solution.py
@@ -29,18 +29,20 @@
 ZZ_AT = 14
 
 
-ROW_AT = (0, 54, 108, 168, 222, 276, 336, 390, 444, 498)
-SLAB_ROWS = 512
-LOW_PART, HIGH_PART = slice(0, 168), slice(336, 512)
+UP_AT = (0, 54, 108, 168, 222, 276, 336, 390, 444, 498)
+DOWN_AT = (0, 37, 74, 112, 149, 186, 224, 261, 298, 335)
+UP_ROWS, DOWN_ROWS = 512, 344
+UP_LOW, UP_HIGH = slice(0, 168), slice(336, 512)
+DOWN_LOW, DOWN_HIGH = slice(0, 112), slice(224, 344)
 
 
 def up_rows(x, c):
-    at = ROW_AT[x] + (42 if x < OX else 0) + 4 * c
+    at = UP_AT[x] + (42 if x < OX else 0) + 4 * c
     return slice(at, at + 4)
 
 
 def down_rows(x, c):
-    at = ROW_AT[x] + (28 if x < OX else 0) + 3 * c
+    at = DOWN_AT[x] + (28 if x < OX else 0) + 3 * c
     return slice(at, at + 3)
 
 
@@ -251,8 +253,8 @@
     add_load(part_ref, load_ref, die)
 
 
-def slab_kernel(load_hbm, flags_hbm, flow_hbm, active_hbm, die_hbm, right_hbm, left_hbm, first_hbm, second_hbm,
-                right_ref, left_ref, rows_ref, part_ref, contact_ref, lower_ref, upper_ref,
+def slab_kernel(load_hbm, flags_hbm, flow_hbm, active_hbm, die_hbm, right_hbm, left_hbm, up_hbm, down_hbm,
+                right_ref, left_ref, up_ref, down_ref, part_ref, contact_ref, lower_ref, upper_ref,
                 load_ref, flags_ref, flow_ref, active_ref, die_ref, load_sem, flags_sem, flow_sem, top_sem, out_sem):
     small = [
         pltpu.make_async_copy(active_hbm, active_ref, top_sem.at[0]),
@@ -298,8 +300,8 @@
 
     for x in range(OX):
         for f in range(NEL):
-            rows_ref[0, ROW_AT[x] + 3 * f : ROW_AT[x] + 3 * f + 3] = field(f, x, slice(13, 16))
-            rows_ref[1, ROW_AT[x] + 2 * f : ROW_AT[x] + 2 * f + 2] = field(f, x, slice(0, 2))
+            up_ref[UP_AT[x] + 3 * f : UP_AT[x] + 3 * f + 3] = field(f, x, slice(13, 16))
+            down_ref[DOWN_AT[x] + 2 * f : DOWN_AT[x] + 2 * f + 2] = field(f, x, slice(0, 2))
     own_part(flags_ref, flow_ref, part_ref, lower_ref, upper_ref)
     for copy in large[2]:
         copy.wait()
@@ -307,11 +309,11 @@
 
     for x in range(OX + 1):
         for c in range(3):
-            rows_ref[0, up_rows(x, c)] = part_ref[c, x, 13:17]
-            rows_ref[1, down_rows(x, c)] = part_ref[c, x, 0:3]
+            up_ref[up_rows(x, c)] = part_ref[c, x, 13:17]
+            down_ref[down_rows(x, c)] = part_ref[c, x, 0:3]
     outs += [
-        pltpu.make_async_copy(rows_ref.at[odd()], first_hbm, out_sem.at[2]),
-        pltpu.make_async_copy(rows_ref.at[1 - odd()], second_hbm, out_sem.at[3]),
+        pltpu.make_async_copy(up_ref, up_hbm, out_sem.at[2]),
+        pltpu.make_async_copy(down_ref, down_hbm, out_sem.at[3]),
     ]
     for copy in outs[2:]:
         copy.start()
@@ -428,13 +430,11 @@
     return jnp.sum(values, axis=0, keepdims=True)
 
 
-def first_kernel(flags_ref, flow_ref, contact_ref, part_ref, left_ref, right_ref, rows_ref, cl_ref, cr_ref,
+def first_kernel(flags_ref, flow_ref, contact_ref, part_ref, left_ref, right_ref, up_ref, down_ref, cl_ref, cr_ref,
                  els_ref, own_ref, dots_ref, right_out, left_out, first_out, second_out,
                  b0, b1, b2, b3, z_ref, lower_ref, upper_ref):
     at_first_x, at_last_x, at_first_y, at_last_y = place()
     has_l, has_r, has_u = ask(at_first_x), ask(at_last_x), ask(at_last_y)
-    below = odd()
-    above = 1 - below
     zero = jnp.zeros((8, DZ), F32)
     low, high = slice(0, 3), slice(19, 21)
     mid = slice(HALO, HALO + OY)
@@ -472,21 +472,21 @@
     lax.fori_loop(0, OX, own, 0)
     for x in range(OX):
         for f in range(NEL):
-            els_ref[f, x + HALO, low] = rows_ref[below, ROW_AT[x] + 3 * f : ROW_AT[x] + 3 * f + 3]
-            els_ref[f, x + HALO, high] = rows_ref[above, ROW_AT[x] + 2 * f : ROW_AT[x] + 2 * f + 2]
+            els_ref[f, x + HALO, low] = up_ref[UP_AT[x] + 3 * f : UP_AT[x] + 3 * f + 3]
+            els_ref[f, x + HALO, high] = down_ref[DOWN_AT[x] + 2 * f : DOWN_AT[x] + 2 * f + 2]
     for c in range(3):
         b0[c, 12, mid] = part_ref[c, OX, 0:16] * has_r
         b0[c, 12, 19:20] = part_ref[c, OX, 16:17] * (has_r * has_u)
     for i in range(3):
         for f in range(NEL):
             els_ref[f, i, mid] = left_ref[3 * f + i]
-            els_ref[f, i, low] = cl_ref[above, ROW_AT[i] + 3 * f : ROW_AT[i] + 3 * f + 3]
-            els_ref[f, i, high] = cl_ref[below, ROW_AT[i] + 2 * f : ROW_AT[i] + 2 * f + 2]
+            els_ref[f, i, low] = cl_ref[UP_AT[i] + 3 * f : UP_AT[i] + 3 * f + 3]
+            els_ref[f, i, high] = cl_ref[176 + DOWN_AT[i] + 2 * f : 176 + DOWN_AT[i] + 2 * f + 2]
     for i in range(2):
         for f in range(NEL):
             els_ref[f, 12 + i, mid] = right_ref[2 * f + i]
-            els_ref[f, 12 + i, low] = cr_ref[above, ROW_AT[i] + 3 * f : ROW_AT[i] + 3 * f + 3]
-            els_ref[f, 12 + i, high] = cr_ref[below, ROW_AT[i] + 2 * f : ROW_AT[i] + 2 * f + 2]
+            els_ref[f, 12 + i, low] = cr_ref[UP_AT[i] + 3 * f : UP_AT[i] + 3 * f + 3]
+            els_ref[f, 12 + i, high] = cr_ref[168 + DOWN_AT[i] + 2 * f : 168 + DOWN_AT[i] + 2 * f + 2]
 
     def zz(x, _):
         for row in (0, 8, 16):
@@ -502,19 +502,19 @@
         for i in range(4):
             b0[c, i, mid] += left_ref[42 + 4 * c + i] * has_l
             b0[c, i, 19:20] += left_ref[54, 4 * c + i : 4 * c + i + 1] * (has_l * has_u)
-            b0[c, i, 0:4] += from_below(cl_ref[above, moved(up_rows(6 + i, c), HIGH_PART.start)]) * has_l
-            b0[c, i, 19:22] += cl_ref[below, moved(down_rows(6 + i, c), HIGH_PART.start)] * (has_l * has_u)
+            b0[c, i, 0:4] += from_below(cl_ref[moved(up_rows(6 + i, c), UP_HIGH.start)]) * has_l
+            b0[c, i, 19:22] += cl_ref[moved(down_rows(6 + i, c), DOWN_HIGH.start - 176)] * (has_l * has_u)
         for i in range(3):
             b0[c, 12 + i, mid] += right_ref[28 + 3 * c + i] * has_r
             b0[c, 12 + i, 19:20] += right_ref[37, 3 * c + i : 3 * c + i + 1] * (has_r * has_u)
-            b0[c, 12 + i, 0:4] += from_below(cr_ref[above, up_rows(i, c)]) * has_r
-            b0[c, 12 + i, 19:22] += cr_ref[below, down_rows(i, c)] * (has_r * has_u)
+            b0[c, 12 + i, 0:4] += from_below(cr_ref[up_rows(i, c)]) * has_r
+            b0[c, 12 + i, 19:22] += cr_ref[moved(down_rows(i, c), -168)] * (has_r * has_u)
 
     for x in range(OX + 1):
         inside = has_r if x == OX else 1.0
         for c in range(3):
-            b0[c, x + HALO, 0:4] += from_below(rows_ref[below, up_rows(x, c)]) * inside
-            b0[c, x + HALO, 19:22] += rows_ref[above, down_rows(x, c)] * (inside * has_u)
+            b0[c, x + HALO, 0:4] += from_below(up_ref[up_rows(x, c)]) * inside
+            b0[c, x + HALO, 19:22] += down_ref[down_rows(x, c)] * (inside * has_u)
 
     basis = (b0, b1, b2, b3)
     three_steps(els_ref, basis, z_ref, lower_ref, upper_ref)
@@ -530,14 +530,14 @@
                     sums[k] = sums[k] + v[k // 2] * v[k - k // 2]
         return tuple(sums)
 
-    sums = lax.fori_loop(0, OX, collect, (zero,) * 7)
+    sums = lax.fori_loop(0, OX, collect, (zero,) * 7, unroll=3)
     dots_ref[...] = zero
     for k in range(7):
         dots_ref[k : k + 1] = sum_rows(sums[k])
 
     def edge_rows(c, x):
-        last, start = b3[c, x, 16:19], b3[c, x, 3:6]
-        return jnp.where(below == 0, last, start), jnp.where(below == 0, start, last)
+        last, start, goes_up = b3[c, x, 16:19], b3[c, x, 3:6], odd() == 0
+        return jnp.where(goes_up, last, start), jnp.where(goes_up, start, last)
 
     for i in range(3):
         for c in range(3):
@@ -600,7 +600,7 @@
                     sums[k - 1] = sums[k - 1] + v[k // 2] * v[k - k // 2]
         return tuple(sums)
 
-    sums = lax.fori_loop(0, OX, collect, (zero,) * 5)
+    sums = lax.fori_loop(0, OX, collect, (zero,) * 5, unroll=3)
     lane = lax.broadcasted_iota(jnp.int32, (1, DZ), 1)
     line = jnp.zeros((1, DZ), F32)
     for k in range(12):
@@ -668,7 +668,7 @@
     return total, remain
 
 
-def last_kernel(dots_ref, own_ref, tail_ref, displacement_ref, residual_ref):
+def last_kernel(dots_ref, own_ref, tail_ref, displacement_hbm, residual_hbm, displacement_ref, residual_ref, sems):
     sums = jnp.sum(dots_ref[...], axis=0, keepdims=True)
     dots = [jnp.broadcast_to(sums[:, k : k + 1], (1, DZ)) for k in range(12)]
     mu = dots[:2]
@@ -677,17 +677,23 @@
     total, remain = coefficients(mu)
     total = [jnp.broadcast_to(value, (8, DZ)) for value in total]
     remain = [jnp.broadcast_to(value, (8, DZ)) for value in remain]
-
-    def write(x, _):
-        for row in (0, 8):
-            for c in range(3):
+    copies = []
+    for c in range(3):
+
+        def write(x, _):
+            for row in (0, 8):
                 v = [own_ref[k, c, x, row : row + 8] for k in range(4)]
                 v += [tail_ref[k, c, x, row : row + 8] for k in range(3)]
                 displacement_ref[c, x, row : row + 8] = tree_sum([a * b for a, b in zip(total, v)])
                 residual_ref[c, x, row : row + 8] = tree_sum([a * b for a, b in zip(remain, v)])
-        return 0
-
-    lax.fori_loop(0, OX, write, 0)
+            return 0
+
+        lax.fori_loop(0, OX, write, 0, unroll=3)
+        for m, (source, target) in enumerate(((displacement_ref, displacement_hbm), (residual_ref, residual_hbm))):
+            copies.append(pltpu.make_async_copy(source.at[c], target.at[c], sems.at[m, c]))
+            copies[-1].start()
+    for copy in copies:
+        copy.wait()
 
 
 def shape(*dims):
@@ -723,13 +729,14 @@
     return lax.ppermute(value, ("gx", "gy"), pairs)
 
 
-def exchange(right, left, first, second):
+def exchange(right, left, up, down):
     from_left = rotate(right, "gx", 1)
     from_right = rotate(left, "gx", -1)
-    rows = jnp.stack([wind(first, True), wind(second, False)])
-    corner_left = rotate(rows[:, HIGH_PART], "gx", 1)
-    corner_right = rotate(rows[:, LOW_PART], "gx", -1)
-    return from_left, from_right, rows, corner_left, corner_right
+    from_below = rotate(up, "gy", 1)
+    from_above = rotate(down, "gy", -1)
+    corner_left = rotate(jnp.concatenate([from_below[UP_HIGH], from_above[DOWN_HIGH]]), "gx", 1)
+    corner_right = rotate(jnp.concatenate([from_below[UP_LOW], from_above[DOWN_LOW]]), "gx", -1)
+    return from_left, from_right, from_below, from_above, corner_left, corner_right
 
 
 def exchange_in_turn(right, left, first, second):
@@ -741,14 +748,14 @@
 
 
 def body(load, plastic_flags, flow_dir, contact_flags, die_depth):
-    slabs = [(55, OY, DZ), (38, OY, DZ), (SLAB_ROWS, DZ), (SLAB_ROWS, DZ)]
+    slabs = [(55, OY, DZ), (38, OY, DZ), (UP_ROWS, DZ), (DOWN_ROWS, DZ)]
     work = [(6, OX + 1, WY + 8, DZ)] * 2
     outside = pl.BlockSpec(memory_space=pl.ANY)
     inputs = (load, plastic_flags, flow_dir, contact_flags, die_depth)
-    right, left, first, second = call(
+    right, left, up, down = call(
         slab_kernel,
         [shape(*dims) for dims in slabs],
-        slabs[:2] + [(2, SLAB_ROWS, DZ), (3, OX + 1, WY, DZ), (OX, OY, DZ)] + work
+        slabs + [(3, OX + 1, WY, DZ), (OX, OY, DZ)] + work
         + [(3, OX, OY, DZ), pltpu.VMEM((8, OX, OY, DZ), jnp.int32), (6, OX, OY, DZ),
            pltpu.VMEM((OX, OY), jnp.int32), (OX, OY)]
         + [pltpu.SemaphoreType.DMA((count,)) for count in (3, 8, 6, 2, 6)],
@@ -758,9 +765,9 @@
     )(*inputs)
     part, contact = call(
         part_kernel, [shape(3, OX + 1, WY, DZ), shape(OX, OY, DZ)], work,
-        cost_estimate=pl.CostEstimate(flops=4000000, bytes_accessed=2000000, transcendentals=0),
+        cost_estimate=pl.CostEstimate(flops=400000, bytes_accessed=1000, transcendentals=0),
     )(*inputs)
-    halos = exchange(right, left, first, second)
+    halos = exchange(right, left, up, down)
     els, own, dots, right, left, first, second = call(
         first_kernel,
         [shape(NEL + 1, WE, WY, DZ), shape(4, 3, OX, OY, DZ), shape(8, DZ), shape(208, DZ), shape(208, DZ), shape(88, DZ), shape(88, DZ)],
@@ -772,7 +779,14 @@
         second_kernel, [shape(3, 3, OX, OY, DZ), shape(count, DZ)], STEP_SCRATCH
     )(els, own, dots, *halos)
     lines = lax.all_to_all(line, ("gx", "gy"), 0, 0, tiled=True)
-    return tuple(call(last_kernel, [shape(3, OX, OY, DZ)] * 2)(lines, own, tail))
+    return tuple(
+        call(
+            last_kernel,
+            [shape(3, OX, OY, DZ)] * 2,
+            [(3, OX, OY, DZ)] * 2 + [pltpu.SemaphoreType.DMA((2, 3))],
+            out_specs=[outside] * 2,
+        )(lines, own, tail)
+    )
 
 
 def solution(mesh):

time: 67.6 us -> 66.7 us (0.987)
  blocking collectives: 23.9 us -> 19.4 us
  starting transfers between devices: 10.3 us -> 13.6 us
  local copies, waits for them, and re-layouts: 0.03 us -> 1.43 us
  waiting for transfers between devices: 13.1 us -> 12.1 us
    ppermute x6 -> x8, starting transfers between devices: 5.87 us -> 12 us  [rotate(): lax.ppermute(value, axis, [(i, (i + steps) % count) for i in range(count)])]
    all_to_all x1, blocking collectives: 23.9 us -> 19.4 us  [body(): lines = lax.all_to_all(line, ('gx', 'gy'), 0, 0, tiled=True)]
    ppermute x4 -> x2, waiting for transfers between devices: 5.23 us -> 1.85 us  [wind(): return lax.ppermute(value, ('gx', 'gy'), pairs)]
    ppermute x4 -> x2, starting transfers between devices: 4.41 us -> 1.54 us  [wind(): return lax.ppermute(value, ('gx', 'gy'), pairs)]
    ppermute x6 -> x8, waiting for transfers between devices: 7.87 us -> 10.2 us  [rotate(): lax.ppermute(value, axis, [(i, (i + steps) % count) for i in range(count)])]
    unnamed x10, local copies, waits for them, and re-layouts: 0.02 us -> 1.4 us
where the time goes in v5:
time: 66.7 us; the launch traced here: 66.4 us
  blocking collectives  19.4 us (29%)
  Pallas kernels  19.2 us (29%)
  starting transfers between devices  13.6 us (20%)
  waiting for transfers between devices  12.1 us (18%)
  local copies, waits for them, and re-layouts  1.43 us (2%)
  between operations  0.76 us (1%)
    all_to_all x1, blocking collectives, body(): lines = lax.all_to_all(line, ('gx', 'gy'), 0, 0, tiled=True)  19.4 us
    ppermute x8, starting transfers between devices, rotate(): lax.ppermute(value, axis, [(i, (i + steps) % count) for i in range(count)])  12 us
    ppermute x8, waiting for transfers between devices, rotate(): lax.ppermute(value, axis, [(i, (i + steps) % count) for i in range(count)])  10.2 us
    pallas_call x1, Pallas kernels, body(): call(first_kernel, [shape(NEL + 1, WE, WY, DZ), shape(4, 3, OX, OY, DZ),...  7.2 us
    pallas_call x1, Pallas kernels, body(): call(second_kernel, [shape(3, 3, OX, OY, DZ), shape(count, DZ)], STEP_SCR...  6.71 us
    pallas_call x1, Pallas kernels, body(): call(slab_kernel, [shape(*dims) for dims in slabs], slabs + [(3, OX + 1,...  3.27 us
    ppermute x2, waiting for transfers between devices, wind(): return lax.ppermute(value, ('gx', 'gy'), pairs)  1.85 us
    ppermute x2, starting transfers between devices, wind(): return lax.ppermute(value, ('gx', 'gy'), pairs)  1.54 us
  transfers between devices with their start and end apart: 10, of which 7 were waited for; matrix products, arithmetic and copies ran while one was open for 0% of the time, Pallas kernels for 1%

profile of v5, /device:TPU:1, one launch (start us, length us, event | category | flops | bytes accessed | tf_op | source)
XLA Modules:
  0.0 66.4 jit_solution(18020998843631376280)
XLA Ops:
  0.7 3.3 %shard_map.69 = (f32[55,16,128]{2,1,0:T(8,128)}, f32[38,16,128]{2,1,0:T(8,128)}, f32[512,128]{1,0:T(8,128)}, f32[344,128]{1,0:T(8,128)}) custom-call(f32[3,9,16,128]{3,2,1,0:T(8,128)} %load_hbm.1, s32[8,9,16,128]{3,2,1,0:T(8,128)} %flags_ref.3, f32[6,9,16,128]{3,2,1,0:T(8,128)} %flow_ref.3, s32[9,16]{1,0:T(8,128)} %active_hbm.1, f32[9,16]{1,0:T(8,128)} %die_hbm.1), custom_call_target="tpu_custom_call" | custom-call | tf_op jit(solution)/shard_map/pallas_call | solution.py:755
  3.9 2.5 %collective-permute-start.2 = (f32[512,128]{1,0:T(8,128)}, f32[512,128]{1,0:T(8,128)S(1)}, u32[]{:S(2)}, u32[]{:S(2)}) collective-permute-start(f32[512,128]{1,0:T(8,128)} %get-tuple-element.21), channel_id=1, source_target_pairs={{0,1},{1,2},{2,3},{3,4},{4,5},{5,6},{6,7},{7,8},{8,9},{9,10},{10,1... | collective-permute-start | bytes 786440 | tf_op jit(solution)/shard_map/ppermute | solution.py:718
  6.5 4.4 %collective-permute-start.3 = (f32[344,128]{1,0:T(8,128)}, f32[344,128]{1,0:T(8,128)S(1)}, u32[]{:S(2)}, u32[]{:S(2)}) collective-permute-start(f32[344,128]{1,0:T(8,128)} %get-tuple-element.22), channel_id=1, source_target_pairs={{0,15},{1,0},{2,1},{3,2},{4,3},{5,4},{6,5},{7,6},{8,7},{9,8},{10,9... | collective-permute-start | bytes 528392 | tf_op jit(solution)/shard_map/ppermute | solution.py:718
  10.9 2.1 %collective-permute-start = (f32[55,16,128]{2,1,0:T(8,128)}, f32[55,16,128]{2,1,0:T(8,128)S(1)}, u32[]{:S(2)}, u32[]{:S(2)}) collective-permute-start(f32[55,16,128]{2,1,0:T(8,128)} %get-tuple-element.19), channel_id=1, source_target_pairs={{0,16},{16,32},{32,48},{48,64},{64,80},{80,96},{96,112},{112,0},{1... | collective-permute-start | bytes 1351688 | tf_op jit(solution)/shard_map/ppermute | solution.py:718
  13.0 0.0 collective-permute-start.1
  13.0 1.3 %collective-permute-done.3.down_ref = f32[344,128]{1,0:T(8,128)S(1)} collective-permute-done((f32[344,128]{1,0:T(8,128)}, f32[344,128]{1,0:T(8,128)S(1)}, u32[]{:S(2)}, u32[]{:S(2)}) %collective-permute-start.3) | collective-permute-done | bytes 176160 | tf_op jit(solution)/shard_map/ppermute | solution.py:718
  14.3 2.7 %collective-permute-done.2.up_ref = f32[512,128]{1,0:T(8,128)S(1)} collective-permute-done((f32[512,128]{1,0:T(8,128)}, f32[512,128]{1,0:T(8,128)S(1)}, u32[]{:S(2)}, u32[]{:S(2)}) %collective-permute-start.2) | collective-permute-done | bytes 262176 | tf_op jit(solution)/shard_map/ppermute | solution.py:718
  17.1 2.4 %collective-permute-start.4 = (f32[296,128]{1,0:T(8,128)S(1)}, f32[296,128]{1,0:T(8,128)S(1)}, u32[]{:S(2)}, u32[]{:S(2)}) collective-permute-start(f32[296,128]{1,0:T(8,128)S(1)} %pad_maximum_fusion), channel_id=1, source_target_pairs={{0,16},{16,32},{32,48},{48,64},{64,80},{80,96},{96,112},{112,0},{1... | collective-permute-start | bytes 454664 | tf_op jit(solution)/shard_map/ppermute | solution.py:718
  19.5 0.0 collective-permute-start.5
  19.5 0.0 copy-done.1
  19.5 0.0 copy-done
  19.5 0.0 copy-done.2
  19.6 0.0 copy-start.3
  19.6 0.7 %copy-done.3 = s32[9,16]{1,0:T(8,128)S(1)} copy-done((s32[9,16]{1,0:T(8,128)S(1)}, s32[9,16]{1,0:T(8,128)}, u32[]{:S(2)}) %copy-start.3) | copy-done | bytes 600
  20.3 0.7 %copy-done.4 = f32[9,16]{1,0:T(8,128)S(1)} copy-done((f32[9,16]{1,0:T(8,128)S(1)}, f32[9,16]{1,0:T(8,128)}, u32[]{:S(2)}) %copy-start.4) | copy-done | bytes 600
  21.0 0.8 %shard_map.68 = (f32[3,10,24,128]{3,2,1,0:T(8,128)S(1)}, f32[9,16,128]{2,1,0:T(8,128)S(1)}) custom-call(f32[3,9,16,128]{3,2,1,0:T(8,128)S(1)} %copy-done.2, s32[8,9,16,128]{3,2,1,0:T(8,128)S(1)} %copy-done, f32[6,9,16,128]{3,2,1,0:T(8,128)S(1)} %copy-done.1, s32[9,16]{1,0:T(8,128)S(1)} %copy-done.3, f32[9,16]{1,0:T(8,128)S(1)} %copy-done.4), custom_call_target="tpu_custom_call" | custom-call | flops 400000 | bytes 1000 | tf_op jit(solution)/shard_map/pallas_call | solution.py:766
  21.8 0.0 collective-permute-done.1.right_ref
  21.8 2.3 %collective-permute-done.5.cr_ref = f32[280,128]{1,0:T(8,128)S(1)} collective-permute-done((f32[280,128]{1,0:T(8,128)S(1)}, f32[280,128]{1,0:T(8,128)S(1)}, u32[]{:S(2)}, u32[]{:S(2)}) %collective-permute-start.5) | collective-permute-done | bytes 143392 | tf_op jit(solution)/shard_map/ppermute | solution.py:718
  24.0 0.0 collective-permute-done.4.cl_ref
  24.0 0.0 collective-permute-done.left_ref
  24.0 7.2 %shard_map.70 = (f32[15,14,24,128]{3,2,1,0:T(8,128)S(1)}, f32[4,3,9,16,128]{4,3,2,1,0:T(8,128)S(1)}, f32[8,128]{1,0:T(8,128)S(1)}, f32[208,128]{1,0:T(8,128)S(1)...) custom-call(s32[8,9,16,128]{3,2,1,0:T(8,128)S(1)} %copy-done, ...), custom_call_target="tpu_custom_call" | custom-call | tf_op jit(solution)/shard_map/pallas_call | solution.py:771
  31.2 0.1 collective-permute-start.6
  31.3 0.5 collective-permute-start.7
  31.8 1.3 %collective-permute-done.6.left_ref = f32[208,128]{1,0:T(8,128)S(1)} collective-permute-done((f32[208,128]{1,0:T(8,128)S(1)}, f32[208,128]{1,0:T(8,128)S(1)}, u32[]{:S(2)}, u32[]{:S(2)}) %collective-permute-start.6) | collective-permute-done | bytes 106528 | tf_op jit(solution)/shard_map/ppermute | solution.py:718
  33.0 2.7 %collective-permute-done.7.right_ref = f32[208,128]{1,0:T(8,128)S(1)} collective-permute-done((f32[208,128]{1,0:T(8,128)S(1)}, f32[208,128]{1,0:T(8,128)S(1)}, u32[]{:S(2)}, u32[]{:S(2)}) %collective-permute-start.7) | collective-permute-done | bytes 106528 | tf_op jit(solution)/shard_map/ppermute | solution.py:718
  35.7 1.0 %collective-permute-start.8 = (f32[152,128]{1,0:T(8,128)S(1)}, f32[152,128]{1,0:T(8,128)S(1)}, u32[]{:S(2)}, u32[]{:S(2)}) collective-permute-start(f32[152,128]{1,0:T(8,128)S(1)} %pad_maximum_fusion.2), channel_id=1, source_target_pairs={{0,1},{1,2},{2,3},{3,4},{4,5},{5,6},{6,7},{7,8},{8,9},{9,10},{10,1... | collective-permute-start | bytes 233480 | tf_op jit(solution)/shard_map/ppermute | solution.py:729
  36.8 0.5 collective-permute-start.9
  37.3 1.8 %collective-permute-done.8.first_ref = f32[152,128]{1,0:T(8,128)S(1)} collective-permute-done((f32[152,128]{1,0:T(8,128)S(1)}, f32[152,128]{1,0:T(8,128)S(1)}, u32[]{:S(2)}, u32[]{:S(2)}) %collective-permute-start.8) | collective-permute-done | bytes 77856 | tf_op jit(solution)/shard_map/ppermute | solution.py:729
  39.1 0.1 collective-permute-done.9.second_ref
  39.1 6.7 %shard_map.71 = (f32[3,3,9,16,128]{4,3,2,1,0:T(8,128)S(1)}, f32[128,128]{1,0:T(8,128)S(1)}) custom-call(f32[15,14,24,128]{3,2,1,0:T(8,128)S(1)} %get-tuple-element.23.els_ref, f32[4,3,9,16,128]{4,3,2,1,0:T(8,128)S(1)} %get-tuple-element.24.own_ref, f32[8,128]{1,0:T(8,128)S(1)} %get-tuple-element.25.dots_ref, f32[208,128]{1,0:T(8,128)S(1)} %collective-permute-done.6.left_ref, ...), custom_call_target="tpu_custom_call" | custom-call | tf_op jit(solution)/shard_map/pallas_call | solution.py:778
  45.9 19.4 %all_to_all.11 = f32[128,1,128]{2,1,0:T(1,128)S(1)} all-to-all(f32[128,1,128]{2,1,0:T(1,128)S(1)} %bitcast.5), channel_id=1, replica_groups=mesh['gx'=8,'gy'=16] {'gx','gy'}, dimensions={0} | all-to-all | bytes 131072 | tf_op jit(solution)/shard_map/all_to_all | solution.py:781
  65.2 1.2 %shard_map.72 = (f32[3,9,16,128]{3,2,1,0:T(8,128)}, f32[3,9,16,128]{3,2,1,0:T(8,128)}) custom-call(f32[128,128]{1,0:T(8,128)S(1)} %bitcast.4, f32[4,3,9,16,128]{4,3,2,1,0:T(8,128)S(1)} %get-tuple-element.24.own_ref, f32[3,3,9,16,128]{4,3,2,1,0:T(8,128)S(1)} %get-tuple-element.31.tail_ref), custom_call_target="tpu_custom_call" | custom-call | tf_op jit(solution)/shard_map/pallas_call | solution.py:783
  (14 shorter events, 0.1 us)
Async XLA Ops:
  0.6 18.9 %copy-start.1 = (f32[6,9,16,128]{3,2,1,0:T(8,128)S(1)}, f32[6,9,16,128]{3,2,1,0:T(8,128)}, u32[]{:S(2)}) copy-start(f32[6,9,16,128]{3,2,1,0:T(8,128)} %flow_ref.3) | copy-start | bytes 1327108
  0.6 18.9 %copy-start = (s32[8,9,16,128]{3,2,1,0:T(8,128)S(1)}, s32[8,9,16,128]{3,2,1,0:T(8,128)}, u32[]{:S(2)}) copy-start(s32[8,9,16,128]{3,2,1,0:T(8,128)} %flags_ref.3) | copy-start | bytes 1769476
  0.6 18.9 %copy-start.2 = (f32[3,9,16,128]{3,2,1,0:T(8,128)S(1)}, f32[3,9,16,128]{3,2,1,0:T(8,128)}, u32[]{:S(2)}) copy-start(f32[3,9,16,128]{3,2,1,0:T(8,128)} %load_hbm.1) | copy-start | bytes 663556
  3.9 13.1 %collective-permute-start.2 = (f32[512,128]{1,0:T(8,128)}, f32[512,128]{1,0:T(8,128)S(1)}, u32[]{:S(2)}, u32[]{:S(2)}) collective-permute-start(f32[512,128]{1,0:T(8,128)} %get-tuple-element.21), channel_id=1, source_target_pairs={{0,1},{1,2},{2,3},{3,4},{4,5},{5,6},{6,7},{7,8},{8,9},{9,10},{10,1... | collective-permute-start | bytes 786440 | tf_op jit(solution)/shard_map/ppermute | solution.py:718
  6.5 7.8 %collective-permute-start.3 = (f32[344,128]{1,0:T(8,128)}, f32[344,128]{1,0:T(8,128)S(1)}, u32[]{:S(2)}, u32[]{:S(2)}) collective-permute-start(f32[344,128]{1,0:T(8,128)} %get-tuple-element.22), channel_id=1, source_target_pairs={{0,15},{1,0},{2,1},{3,2},{4,3},{5,4},{6,5},{7,6},{8,7},{9,8},{10,9... | collective-permute-start | bytes 528392 | tf_op jit(solution)/shard_map/ppermute | solution.py:718
  10.9 13.2 %collective-permute-start = (f32[55,16,128]{2,1,0:T(8,128)}, f32[55,16,128]{2,1,0:T(8,128)S(1)}, u32[]{:S(2)}, u32[]{:S(2)}) collective-permute-start(f32[55,16,128]{2,1,0:T(8,128)} %get-tuple-element.19), channel_id=1, source_target_pairs={{0,16},{16,32},{32,48},{48,64},{64,80},{80,96},{96,112},{112,0},{1... | collective-permute-start | bytes 1351688 | tf_op jit(solution)/shard_map/ppermute | solution.py:718
  13.0 8.8 %collective-permute-start.1 = (f32[38,16,128]{2,1,0:T(8,128)}, f32[38,16,128]{2,1,0:T(8,128)S(1)}, u32[]{:S(2)}, u32[]{:S(2)}) collective-permute-start(f32[38,16,128]{2,1,0:T(8,128)} %get-tuple-element.20), channel_id=1, source_target_pairs={{0,112},{16,0},{32,16},{48,32},{64,48},{80,64},{96,80},{112,96},{1... | collective-permute-start | bytes 933896 | tf_op jit(solution)/shard_map/ppermute | solution.py:718
  17.1 7.0 %collective-permute-start.4 = (f32[296,128]{1,0:T(8,128)S(1)}, f32[296,128]{1,0:T(8,128)S(1)}, u32[]{:S(2)}, u32[]{:S(2)}) collective-permute-start(f32[296,128]{1,0:T(8,128)S(1)} %pad_maximum_fusion), channel_id=1, source_target_pairs={{0,16},{16,32},{32,48},{48,64},{64,80},{80,96},{96,112},{112,0},{1... | collective-permute-start | bytes 454664 | tf_op jit(solution)/shard_map/ppermute | solution.py:718
  19.5 4.5 %collective-permute-start.5 = (f32[280,128]{1,0:T(8,128)S(1)}, f32[280,128]{1,0:T(8,128)S(1)}, u32[]{:S(2)}, u32[]{:S(2)}) collective-permute-start(f32[280,128]{1,0:T(8,128)S(1)} %pad_maximum_fusion.1), channel_id=1, source_target_pairs={{0,112},{16,0},{32,16},{48,32},{64,48},{80,64},{96,80},{112,96},{1... | collective-permute-start | bytes 430088 | tf_op jit(solution)/shard_map/ppermute | solution.py:718
  19.6 0.7 %copy-start.3 = (s32[9,16]{1,0:T(8,128)S(1)}, s32[9,16]{1,0:T(8,128)}, u32[]{:S(2)}) copy-start(s32[9,16]{1,0:T(8,128)} %active_hbm.1) | copy-start | bytes 1732
  20.3 0.7 %copy-start.4 = (f32[9,16]{1,0:T(8,128)S(1)}, f32[9,16]{1,0:T(8,128)}, u32[]{:S(2)}) copy-start(f32[9,16]{1,0:T(8,128)} %die_hbm.1) | copy-start | bytes 1732
  31.2 1.8 %collective-permute-start.6 = (f32[208,128]{1,0:T(8,128)S(1)}, f32[208,128]{1,0:T(8,128)S(1)}, u32[]{:S(2)}, u32[]{:S(2)}) collective-permute-start(f32[208,128]{1,0:T(8,128)S(1)} %get-tuple-element.26), channel_id=1, source_target_pairs={{0,16},{16,32},{32,48},{48,64},{64,80},{80,96},{96,112},{112,0},{1... | collective-permute-start | bytes 319496 | tf_op jit(solution)/shard_map/ppermute | solution.py:718
  31.3 4.4 %collective-permute-start.7 = (f32[208,128]{1,0:T(8,128)S(1)}, f32[208,128]{1,0:T(8,128)S(1)}, u32[]{:S(2)}, u32[]{:S(2)}) collective-permute-start(f32[208,128]{1,0:T(8,128)S(1)} %get-tuple-element.27), channel_id=1, source_target_pairs={{0,112},{16,0},{32,16},{48,32},{64,48},{80,64},{96,80},{112,96},{1... | collective-permute-start | bytes 319496 | tf_op jit(solution)/shard_map/ppermute | solution.py:718
  35.7 3.3 %collective-permute-start.8 = (f32[152,128]{1,0:T(8,128)S(1)}, f32[152,128]{1,0:T(8,128)S(1)}, u32[]{:S(2)}, u32[]{:S(2)}) collective-permute-start(f32[152,128]{1,0:T(8,128)S(1)} %pad_maximum_fusion.2), channel_id=1, source_target_pairs={{0,1},{1,2},{2,3},{3,4},{4,5},{5,6},{6,7},{7,8},{8,9},{9,10},{10,1... | collective-permute-start | bytes 233480 | tf_op jit(solution)/shard_map/ppermute | solution.py:729
  36.8 2.4 %collective-permute-start.9 = (f32[152,128]{1,0:T(8,128)S(1)}, f32[152,128]{1,0:T(8,128)S(1)}, u32[]{:S(2)}, u32[]{:S(2)}) collective-permute-start(f32[152,128]{1,0:T(8,128)S(1)} %pad_maximum_fusion.3), channel_id=1, source_target_pairs={{0,16},{1,0},{2,1},{3,2},{4,3},{5,4},{6,5},{7,6},{8,7},{9,8},{10,9... | collective-permute-start | bytes 233480 | tf_op jit(solution)/shard_map/ppermute | solution.py:729

commit v6 on v5

--- a/solution.py
+++ b/solution.py
@@ -230,7 +230,7 @@
             store_y(node, lower_ref, upper_ref, x, row)
             return ahead
 
-        behind = lax.fori_loop(0, OX, element, [zero] * 12)
+        behind = lax.fori_loop(0, OX, element, [zero] * 12, unroll=3)
         store_y(behind, lower_ref, upper_ref, OX, row)
     for x in range(OX + 1):
         for c in range(3):
@@ -274,9 +274,6 @@
     contact, die = top_fields(active_ref, die_ref)
     for x in range(OX):
         contact_ref[x] = contact[x]
-    for group in large[:2]:
-        for copy in group:
-            copy.wait()
 
     def field(f, x, rows):
         if f < 8:
@@ -286,22 +283,23 @@
         return contact_ref[x, rows]
 
     whole = slice(0, OY)
+    arrived = {0: large[0][0], 4: large[0][1], 8: large[1][0], 10: large[1][1]}
     for f in range(NEL):
+        if f in arrived:
+            arrived[f].wait()
         for i in range(3):
             right_ref[3 * f + i] = field(f, 6 + i, whole)
         for i in range(2):
             left_ref[2 * f + i] = field(f, i, whole)
+        for x in range(OX):
+            up_ref[UP_AT[x] + 3 * f : UP_AT[x] + 3 * f + 3] = field(f, x, slice(13, 16))
+            down_ref[DOWN_AT[x] + 2 * f : DOWN_AT[x] + 2 * f + 2] = field(f, x, slice(0, 2))
     outs = [
         pltpu.make_async_copy(right_ref.at[0:42], right_hbm.at[0:42], out_sem.at[0]),
         pltpu.make_async_copy(left_ref.at[0:28], left_hbm.at[0:28], out_sem.at[1]),
     ]
     for copy in outs:
         copy.start()
-
-    for x in range(OX):
-        for f in range(NEL):
-            up_ref[UP_AT[x] + 3 * f : UP_AT[x] + 3 * f + 3] = field(f, x, slice(13, 16))
-            down_ref[DOWN_AT[x] + 2 * f : DOWN_AT[x] + 2 * f + 2] = field(f, x, slice(0, 2))
     own_part(flags_ref, flow_ref, part_ref, lower_ref, upper_ref)
     for copy in large[2]:
         copy.wait()

time: 66.7 us -> 66.5 us (level)
  no operation moved by 1% of the time
where the time goes in v6:
time: 66.5 us; the launch traced here: 66.2 us
  blocking collectives  19.4 us (29%)
  Pallas kernels  18.9 us (28%)
  starting transfers between devices  13.6 us (20%)
  waiting for transfers between devices  12.2 us (18%)
  local copies, waits for them, and re-layouts  1.43 us (2%)
  between operations  0.76 us (1%)
    all_to_all x1, blocking collectives, body(): lines = lax.all_to_all(line, ('gx', 'gy'), 0, 0, tiled=True)  19.4 us
    ppermute x8, starting transfers between devices, rotate(): lax.ppermute(value, axis, [(i, (i + steps) % count) for i in range(count)])  12 us
    ppermute x8, waiting for transfers between devices, rotate(): lax.ppermute(value, axis, [(i, (i + steps) % count) for i in range(count)])  10.3 us
    pallas_call x1, Pallas kernels, body(): call(first_kernel, [shape(NEL + 1, WE, WY, DZ), shape(4, 3, OX, OY, DZ),...  7.2 us
    pallas_call x1, Pallas kernels, body(): call(second_kernel, [shape(3, 3, OX, OY, DZ), shape(count, DZ)], STEP_SCR...  6.71 us
    pallas_call x1, Pallas kernels, body(): call(slab_kernel, [shape(*dims) for dims in slabs], slabs + [(3, OX + 1,...  3.06 us
    ppermute x2, waiting for transfers between devices, wind(): return lax.ppermute(value, ('gx', 'gy'), pairs)  1.85 us
    ppermute x2, starting transfers between devices, wind(): return lax.ppermute(value, ('gx', 'gy'), pairs)  1.54 us
  transfers between devices with their start and end apart: 10, of which 7 were waited for; matrix products, arithmetic and copies ran while one was open for 0% of the time, Pallas kernels for 1%

profile of v6, /device:TPU:1, one launch (start us, length us, event | category | flops | bytes accessed | tf_op | source)
XLA Modules:
  0.0 66.2 jit_solution(16527568862095380625)
XLA Ops:
  0.6 0.0 copy-start.1
  0.6 0.0 copy-start
  0.6 0.0 copy-start.2
  0.7 3.1 %shard_map.69 = (f32[55,16,128]{2,1,0:T(8,128)}, f32[38,16,128]{2,1,0:T(8,128)}, f32[512,128]{1,0:T(8,128)}, f32[344,128]{1,0:T(8,128)}) custom-call(f32[3,9,16,128]{3,2,1,0:T(8,128)} %load_hbm.1, s32[8,9,16,128]{3,2,1,0:T(8,128)} %flags_ref.3, f32[6,9,16,128]{3,2,1,0:T(8,128)} %flow_ref.3, s32[9,16]{1,0:T(8,128)} %active_hbm.1, f32[9,16]{1,0:T(8,128)} %die_hbm.1), custom_call_target="tpu_custom_call" | custom-call | tf_op jit(solution)/shard_map/pallas_call | solution.py:753
  3.7 2.5 %collective-permute-start.2 = (f32[512,128]{1,0:T(8,128)}, f32[512,128]{1,0:T(8,128)S(1)}, u32[]{:S(2)}, u32[]{:S(2)}) collective-permute-start(f32[512,128]{1,0:T(8,128)} %get-tuple-element.21), channel_id=1, source_target_pairs={{0,1},{1,2},{2,3},{3,4},{4,5},{5,6},{6,7},{7,8},{8,9},{9,10},{10,1... | collective-permute-start | bytes 786440 | tf_op jit(solution)/shard_map/ppermute | solution.py:716
  6.3 4.4 %collective-permute-start.3 = (f32[344,128]{1,0:T(8,128)}, f32[344,128]{1,0:T(8,128)S(1)}, u32[]{:S(2)}, u32[]{:S(2)}) collective-permute-start(f32[344,128]{1,0:T(8,128)} %get-tuple-element.22), channel_id=1, source_target_pairs={{0,15},{1,0},{2,1},{3,2},{4,3},{5,4},{6,5},{7,6},{8,7},{9,8},{10,9... | collective-permute-start | bytes 528392 | tf_op jit(solution)/shard_map/ppermute | solution.py:716
  10.7 2.1 %collective-permute-start = (f32[55,16,128]{2,1,0:T(8,128)}, f32[55,16,128]{2,1,0:T(8,128)S(1)}, u32[]{:S(2)}, u32[]{:S(2)}) collective-permute-start(f32[55,16,128]{2,1,0:T(8,128)} %get-tuple-element.19), channel_id=1, source_target_pairs={{0,16},{16,32},{32,48},{48,64},{64,80},{80,96},{96,112},{112,0},{1... | collective-permute-start | bytes 1351688 | tf_op jit(solution)/shard_map/ppermute | solution.py:716
  12.8 0.0 collective-permute-start.1
  12.8 1.3 %collective-permute-done.3.down_ref = f32[344,128]{1,0:T(8,128)S(1)} collective-permute-done((f32[344,128]{1,0:T(8,128)}, f32[344,128]{1,0:T(8,128)S(1)}, u32[]{:S(2)}, u32[]{:S(2)}) %collective-permute-start.3) | collective-permute-done | bytes 176160 | tf_op jit(solution)/shard_map/ppermute | solution.py:716
  14.1 2.7 %collective-permute-done.2.up_ref = f32[512,128]{1,0:T(8,128)S(1)} collective-permute-done((f32[512,128]{1,0:T(8,128)}, f32[512,128]{1,0:T(8,128)S(1)}, u32[]{:S(2)}, u32[]{:S(2)}) %collective-permute-start.2) | collective-permute-done | bytes 262176 | tf_op jit(solution)/shard_map/ppermute | solution.py:716
  16.8 2.4 %collective-permute-start.4 = (f32[296,128]{1,0:T(8,128)S(1)}, f32[296,128]{1,0:T(8,128)S(1)}, u32[]{:S(2)}, u32[]{:S(2)}) collective-permute-start(f32[296,128]{1,0:T(8,128)S(1)} %pad_maximum_fusion), channel_id=1, source_target_pairs={{0,16},{16,32},{32,48},{48,64},{64,80},{80,96},{96,112},{112,0},{1... | collective-permute-start | bytes 454664 | tf_op jit(solution)/shard_map/ppermute | solution.py:716
  19.3 0.0 collective-permute-start.5
  19.3 0.0 copy-start.3
  19.4 0.7 %copy-done.3 = s32[9,16]{1,0:T(8,128)S(1)} copy-done((s32[9,16]{1,0:T(8,128)S(1)}, s32[9,16]{1,0:T(8,128)}, u32[]{:S(2)}) %copy-start.3) | copy-done | bytes 600
  20.0 0.7 %copy-done.4 = f32[9,16]{1,0:T(8,128)S(1)} copy-done((f32[9,16]{1,0:T(8,128)S(1)}, f32[9,16]{1,0:T(8,128)}, u32[]{:S(2)}) %copy-start.4) | copy-done | bytes 600
  20.7 0.7 %shard_map.68 = (f32[3,10,24,128]{3,2,1,0:T(8,128)S(1)}, f32[9,16,128]{2,1,0:T(8,128)S(1)}) custom-call(f32[3,9,16,128]{3,2,1,0:T(8,128)S(1)} %copy-done.2, s32[8,9,16,128]{3,2,1,0:T(8,128)S(1)} %copy-done, f32[6,9,16,128]{3,2,1,0:T(8,128)S(1)} %copy-done.1, s32[9,16]{1,0:T(8,128)S(1)} %copy-done.3, f32[9,16]{1,0:T(8,128)S(1)} %copy-done.4), custom_call_target="tpu_custom_call" | custom-call | flops 400000 | bytes 1000 | tf_op jit(solution)/shard_map/pallas_call | solution.py:764
  21.5 0.0 collective-permute-done.1.right_ref
  21.5 2.4 %collective-permute-done.5.cr_ref = f32[280,128]{1,0:T(8,128)S(1)} collective-permute-done((f32[280,128]{1,0:T(8,128)S(1)}, f32[280,128]{1,0:T(8,128)S(1)}, u32[]{:S(2)}, u32[]{:S(2)}) %collective-permute-start.5) | collective-permute-done | bytes 143392 | tf_op jit(solution)/shard_map/ppermute | solution.py:716
  23.8 0.0 collective-permute-done.4.cl_ref
  23.8 0.0 collective-permute-done.left_ref
  23.8 7.2 %shard_map.70 = (f32[15,14,24,128]{3,2,1,0:T(8,128)S(1)}, f32[4,3,9,16,128]{4,3,2,1,0:T(8,128)S(1)}, f32[8,128]{1,0:T(8,128)S(1)}, f32[208,128]{1,0:T(8,128)S(1)...) custom-call(s32[8,9,16,128]{3,2,1,0:T(8,128)S(1)} %copy-done, ...), custom_call_target="tpu_custom_call" | custom-call | tf_op jit(solution)/shard_map/pallas_call | solution.py:769
  31.0 0.1 collective-permute-start.6
  31.1 0.5 collective-permute-start.7
  31.6 1.3 %collective-permute-done.6.left_ref = f32[208,128]{1,0:T(8,128)S(1)} collective-permute-done((f32[208,128]{1,0:T(8,128)S(1)}, f32[208,128]{1,0:T(8,128)S(1)}, u32[]{:S(2)}, u32[]{:S(2)}) %collective-permute-start.6) | collective-permute-done | bytes 106528 | tf_op jit(solution)/shard_map/ppermute | solution.py:716
  32.8 2.7 %collective-permute-done.7.right_ref = f32[208,128]{1,0:T(8,128)S(1)} collective-permute-done((f32[208,128]{1,0:T(8,128)S(1)}, f32[208,128]{1,0:T(8,128)S(1)}, u32[]{:S(2)}, u32[]{:S(2)}) %collective-permute-start.7) | collective-permute-done | bytes 106528 | tf_op jit(solution)/shard_map/ppermute | solution.py:716
  35.5 1.0 %collective-permute-start.8 = (f32[152,128]{1,0:T(8,128)S(1)}, f32[152,128]{1,0:T(8,128)S(1)}, u32[]{:S(2)}, u32[]{:S(2)}) collective-permute-start(f32[152,128]{1,0:T(8,128)S(1)} %pad_maximum_fusion.2), channel_id=1, source_target_pairs={{0,1},{1,2},{2,3},{3,4},{4,5},{5,6},{6,7},{7,8},{8,9},{9,10},{10,1... | collective-permute-start | bytes 233480 | tf_op jit(solution)/shard_map/ppermute | solution.py:727
  36.6 0.5 collective-permute-start.9
  37.1 1.8 %collective-permute-done.8.first_ref = f32[152,128]{1,0:T(8,128)S(1)} collective-permute-done((f32[152,128]{1,0:T(8,128)S(1)}, f32[152,128]{1,0:T(8,128)S(1)}, u32[]{:S(2)}, u32[]{:S(2)}) %collective-permute-start.8) | collective-permute-done | bytes 77856 | tf_op jit(solution)/shard_map/ppermute | solution.py:727
  38.9 0.1 collective-permute-done.9.second_ref
  38.9 6.7 %shard_map.71 = (f32[3,3,9,16,128]{4,3,2,1,0:T(8,128)S(1)}, f32[128,128]{1,0:T(8,128)S(1)}) custom-call(f32[15,14,24,128]{3,2,1,0:T(8,128)S(1)} %get-tuple-element.23.els_ref, f32[4,3,9,16,128]{4,3,2,1,0:T(8,128)S(1)} %get-tuple-element.24.own_ref, f32[8,128]{1,0:T(8,128)S(1)} %get-tuple-element.25.dots_ref, f32[208,128]{1,0:T(8,128)S(1)} %collective-permute-done.6.left_ref, ...), custom_call_target="tpu_custom_call" | custom-call | tf_op jit(solution)/shard_map/pallas_call | solution.py:776
  45.7 19.4 %all_to_all.11 = f32[128,1,128]{2,1,0:T(1,128)S(1)} all-to-all(f32[128,1,128]{2,1,0:T(1,128)S(1)} %bitcast.5), channel_id=1, replica_groups=mesh['gx'=8,'gy'=16] {'gx','gy'}, dimensions={0} | all-to-all | bytes 131072 | tf_op jit(solution)/shard_map/all_to_all | solution.py:779
  65.0 1.2 %shard_map.72 = (f32[3,9,16,128]{3,2,1,0:T(8,128)}, f32[3,9,16,128]{3,2,1,0:T(8,128)}) custom-call(f32[128,128]{1,0:T(8,128)S(1)} %bitcast.4, f32[4,3,9,16,128]{4,3,2,1,0:T(8,128)S(1)} %get-tuple-element.24.own_ref, f32[3,3,9,16,128]{4,3,2,1,0:T(8,128)S(1)} %get-tuple-element.31.tail_ref), custom_call_target="tpu_custom_call" | custom-call | tf_op jit(solution)/shard_map/pallas_call | solution.py:781
  (14 shorter events, 0.1 us)
Async XLA Ops:
  0.6 18.7 %copy-start.1 = (f32[6,9,16,128]{3,2,1,0:T(8,128)S(1)}, f32[6,9,16,128]{3,2,1,0:T(8,128)}, u32[]{:S(2)}) copy-start(f32[6,9,16,128]{3,2,1,0:T(8,128)} %flow_ref.3) | copy-start | bytes 1327108
  0.6 18.7 %copy-start = (s32[8,9,16,128]{3,2,1,0:T(8,128)S(1)}, s32[8,9,16,128]{3,2,1,0:T(8,128)}, u32[]{:S(2)}) copy-start(s32[8,9,16,128]{3,2,1,0:T(8,128)} %flags_ref.3) | copy-start | bytes 1769476
  0.6 18.7 %copy-start.2 = (f32[3,9,16,128]{3,2,1,0:T(8,128)S(1)}, f32[3,9,16,128]{3,2,1,0:T(8,128)}, u32[]{:S(2)}) copy-start(f32[3,9,16,128]{3,2,1,0:T(8,128)} %load_hbm.1) | copy-start | bytes 663556
  3.7 13.1 %collective-permute-start.2 = (f32[512,128]{1,0:T(8,128)}, f32[512,128]{1,0:T(8,128)S(1)}, u32[]{:S(2)}, u32[]{:S(2)}) collective-permute-start(f32[512,128]{1,0:T(8,128)} %get-tuple-element.21), channel_id=1, source_target_pairs={{0,1},{1,2},{2,3},{3,4},{4,5},{5,6},{6,7},{7,8},{8,9},{9,10},{10,1... | collective-permute-start | bytes 786440 | tf_op jit(solution)/shard_map/ppermute | solution.py:716
  6.3 7.8 %collective-permute-start.3 = (f32[344,128]{1,0:T(8,128)}, f32[344,128]{1,0:T(8,128)S(1)}, u32[]{:S(2)}, u32[]{:S(2)}) collective-permute-start(f32[344,128]{1,0:T(8,128)} %get-tuple-element.22), channel_id=1, source_target_pairs={{0,15},{1,0},{2,1},{3,2},{4,3},{5,4},{6,5},{7,6},{8,7},{9,8},{10,9... | collective-permute-start | bytes 528392 | tf_op jit(solution)/shard_map/ppermute | solution.py:716
  10.7 13.2 %collective-permute-start = (f32[55,16,128]{2,1,0:T(8,128)}, f32[55,16,128]{2,1,0:T(8,128)S(1)}, u32[]{:S(2)}, u32[]{:S(2)}) collective-permute-start(f32[55,16,128]{2,1,0:T(8,128)} %get-tuple-element.19), channel_id=1, source_target_pairs={{0,16},{16,32},{32,48},{48,64},{64,80},{80,96},{96,112},{112,0},{1... | collective-permute-start | bytes 1351688 | tf_op jit(solution)/shard_map/ppermute | solution.py:716
  12.8 8.7 %collective-permute-start.1 = (f32[38,16,128]{2,1,0:T(8,128)}, f32[38,16,128]{2,1,0:T(8,128)S(1)}, u32[]{:S(2)}, u32[]{:S(2)}) collective-permute-start(f32[38,16,128]{2,1,0:T(8,128)} %get-tuple-element.20), channel_id=1, source_target_pairs={{0,112},{16,0},{32,16},{48,32},{64,48},{80,64},{96,80},{112,96},{1... | collective-permute-start | bytes 933896 | tf_op jit(solution)/shard_map/ppermute | solution.py:716
  16.8 7.0 %collective-permute-start.4 = (f32[296,128]{1,0:T(8,128)S(1)}, f32[296,128]{1,0:T(8,128)S(1)}, u32[]{:S(2)}, u32[]{:S(2)}) collective-permute-start(f32[296,128]{1,0:T(8,128)S(1)} %pad_maximum_fusion), channel_id=1, source_target_pairs={{0,16},{16,32},{32,48},{48,64},{64,80},{80,96},{96,112},{112,0},{1... | collective-permute-start | bytes 454664 | tf_op jit(solution)/shard_map/ppermute | solution.py:716
  19.3 4.5 %collective-permute-start.5 = (f32[280,128]{1,0:T(8,128)S(1)}, f32[280,128]{1,0:T(8,128)S(1)}, u32[]{:S(2)}, u32[]{:S(2)}) collective-permute-start(f32[280,128]{1,0:T(8,128)S(1)} %pad_maximum_fusion.1), channel_id=1, source_target_pairs={{0,112},{16,0},{32,16},{48,32},{64,48},{80,64},{96,80},{112,96},{1... | collective-permute-start | bytes 430088 | tf_op jit(solution)/shard_map/ppermute | solution.py:716
  19.3 0.7 %copy-start.3 = (s32[9,16]{1,0:T(8,128)S(1)}, s32[9,16]{1,0:T(8,128)}, u32[]{:S(2)}) copy-start(s32[9,16]{1,0:T(8,128)} %active_hbm.1) | copy-start | bytes 1732
  20.0 0.7 %copy-start.4 = (f32[9,16]{1,0:T(8,128)S(1)}, f32[9,16]{1,0:T(8,128)}, u32[]{:S(2)}) copy-start(f32[9,16]{1,0:T(8,128)} %die_hbm.1) | copy-start | bytes 1732
  31.0 1.8 %collective-permute-start.6 = (f32[208,128]{1,0:T(8,128)S(1)}, f32[208,128]{1,0:T(8,128)S(1)}, u32[]{:S(2)}, u32[]{:S(2)}) collective-permute-start(f32[208,128]{1,0:T(8,128)S(1)} %get-tuple-element.26), channel_id=1, source_target_pairs={{0,16},{16,32},{32,48},{48,64},{64,80},{80,96},{96,112},{112,0},{1... | collective-permute-start | bytes 319496 | tf_op jit(solution)/shard_map/ppermute | solution.py:716
  31.1 4.4 %collective-permute-start.7 = (f32[208,128]{1,0:T(8,128)S(1)}, f32[208,128]{1,0:T(8,128)S(1)}, u32[]{:S(2)}, u32[]{:S(2)}) collective-permute-start(f32[208,128]{1,0:T(8,128)S(1)} %get-tuple-element.27), channel_id=1, source_target_pairs={{0,112},{16,0},{32,16},{48,32},{64,48},{80,64},{96,80},{112,96},{1... | collective-permute-start | bytes 319496 | tf_op jit(solution)/shard_map/ppermute | solution.py:716
  35.5 3.3 %collective-permute-start.8 = (f32[152,128]{1,0:T(8,128)S(1)}, f32[152,128]{1,0:T(8,128)S(1)}, u32[]{:S(2)}, u32[]{:S(2)}) collective-permute-start(f32[152,128]{1,0:T(8,128)S(1)} %pad_maximum_fusion.2), channel_id=1, source_target_pairs={{0,1},{1,2},{2,3},{3,4},{4,5},{5,6},{6,7},{7,8},{8,9},{9,10},{10,1... | collective-permute-start | bytes 233480 | tf_op jit(solution)/shard_map/ppermute | solution.py:727
  36.6 2.4 %collective-permute-start.9 = (f32[152,128]{1,0:T(8,128)S(1)}, f32[152,128]{1,0:T(8,128)S(1)}, u32[]{:S(2)}, u32[]{:S(2)}) collective-permute-start(f32[152,128]{1,0:T(8,128)S(1)} %pad_maximum_fusion.3), channel_id=1, source_target_pairs={{0,16},{1,0},{2,1},{3,2},{4,3},{5,4},{6,5},{7,6},{8,7},{9,8},{10,9... | collective-permute-start | bytes 233480 | tf_op jit(solution)/shard_map/ppermute | solution.py:727

commit v7 on v6

--- a/solution.py
+++ b/solution.py
@@ -27,6 +27,8 @@
 NEL = 14
 CONTACT_AT = 13
 ZZ_AT = 14
+FOLD = 6
+FOLDED = -1
 
 
 UP_AT = (0, 54, 108, 168, 222, 276, 336, 390, 444, 498)
@@ -340,6 +342,7 @@
     keep_upper = jnp.logical_or(rows >= HALO, jnp.logical_not(at_first_y))
     keep_node = jnp.logical_or(rows < HALO, jnp.logical_not(at_last_y))
     zero = jnp.zeros((8, DZ), F32)
+    low_half = rows < 4
 
     def clear(x, _):
         for m in range(6):
@@ -362,12 +365,19 @@
     for step in range(1, HALO + 1):
         start, end = step - 1, WX - 1 - step
         scale = (2.0 if step == 1 else 4.0) / SPAN
-        for row in (0, 8, 16):
+        for row in (0, 8, 16) if step == 1 else (FOLDED, 0, 8):
+
+            def rows_of(ref, m, x, shift=0):
+                if row != FOLDED:
+                    return ref[m, x, row + shift : row + shift + 8]
+                return jnp.where(
+                    low_half, ref[m, x, 16 + shift : 24 + shift], ref[m, x + FOLD, 12 + shift : 20 + shift]
+                )
 
             def plane(x):
                 values = []
                 for m in range(6):
-                    low, high = z_ref[m, x, row : row + 8], z_ref[m, x, row + 1 : row + 9]
+                    low, high = rows_of(z_ref, m, x), rows_of(z_ref, m, x, 1)
                     values += [high + low, high - low]
                 return values
 
@@ -384,17 +394,23 @@
                     [q[4 * c + 3] + p[4 * c + 3] for c in range(3)],
                     [q[4 * c + 3] - p[4 * c + 3] for c in range(3)],
                 )
-                here = [els_ref[f, x, row : row + 8] for f in range(NEL + 1) if f != CONTACT_AT]
+                here = [rows_of(els_ref, f, x) for f in range(NEL + 1) if f != CONTACT_AT]
                 n = (here[8], here[9], here[13], here[10], here[11], here[12])
                 node, ahead = scatter_x(element_core(modes, n, here[:8]), behind)
-                store_y(node, lower_ref, upper_ref, x, row, keep_upper if row == 0 else None)
+                if row == FOLDED:
+                    store_y(node, lower_ref, upper_ref, x, 16)
+                    store_y(node, lower_ref, upper_ref, x + FOLD, 12)
+                else:
+                    store_y(node, lower_ref, upper_ref, x, row, keep_upper if row == 0 else None)
                 return after, ahead
 
-            carry = (plane(start), [zero] * 12)
-            for x in range(start, HALO):
+            first_x, last_x = (1, FOLD) if row == FOLDED else (start, end)
+            gone = jnp.logical_and(at_first_x, low_half) if row == FOLDED else at_first_x
+            carry = (plane(first_x), [zero] * 12)
+            for x in range(first_x, HALO):
                 carry = element(x, carry)
-            carry = (carry[0], [jnp.where(at_first_x, 0.0, value) for value in carry[1]])
-            first_pair = HALO + (end + 1 - HALO) % 2
+            carry = (carry[0], [jnp.where(gone, 0.0, value) for value in carry[1]])
+            first_pair = HALO + (last_x + 1 - HALO) % 2
             if first_pair > HALO:
                 carry = element(HALO, carry)
 
@@ -402,7 +418,14 @@
                 x = first_pair + 2 * k
                 return element(x + 1, element(x, carry))
 
-            lax.fori_loop(0, (end + 1 - first_pair) // 2, pair, carry)
+            carry = lax.fori_loop(0, (last_x + 1 - first_pair) // 2, pair, carry)
+            if row == FOLDED:
+                for c in range(3):
+                    ss, sd, ds, dd = carry[1][4 * c : 4 * c + 4]
+                    for m, value in ((2 * c, ss - sd), (2 * c + 1, ds - dd)):
+                        lower_ref[m, FOLD + 1, 16:24] += jnp.where(low_half, value, 0.0)
+                    for m, value in ((2 * c, ss + sd), (2 * c + 1, ds + dd)):
+                        upper_ref[m, FOLD + 1, 24:32] += jnp.where(low_half, value, 0.0)
 
         for x in range(step, end + 1):
             for row in (0, 8, 16) if step < HALO else (HALO, HALO + 8):

time: 66.5 us -> 66.2 us (level)
  no operation moved by 1% of the time
where the time goes in v7:
time: 66.2 us; the launch traced here: 65.9 us
  blocking collectives  19.4 us (29%)
  Pallas kernels  18.6 us (28%)
  starting transfers between devices  13.6 us (21%)
  waiting for transfers between devices  12.2 us (18%)
  local copies, waits for them, and re-layouts  1.43 us (2%)
  between operations  0.76 us (1%)
    all_to_all x1, blocking collectives, body(): lines = lax.all_to_all(line, ('gx', 'gy'), 0, 0, tiled=True)  19.4 us
    ppermute x8, starting transfers between devices, rotate(): lax.ppermute(value, axis, [(i, (i + steps) % count) for i in range(count)])  12 us
    ppermute x8, waiting for transfers between devices, rotate(): lax.ppermute(value, axis, [(i, (i + steps) % count) for i in range(count)])  10.3 us
    pallas_call x1, Pallas kernels, body(): call(first_kernel, [shape(NEL + 1, WE, WY, DZ), shape(4, 3, OX, OY, DZ),...  7.05 us
    pallas_call x1, Pallas kernels, body(): call(second_kernel, [shape(3, 3, OX, OY, DZ), shape(count, DZ)], STEP_SCR...  6.56 us
    pallas_call x1, Pallas kernels, body(): call(slab_kernel, [shape(*dims) for dims in slabs], slabs + [(3, OX + 1,...  3.06 us
    ppermute x2, waiting for transfers between devices, wind(): return lax.ppermute(value, ('gx', 'gy'), pairs)  1.85 us
    ppermute x2, starting transfers between devices, wind(): return lax.ppermute(value, ('gx', 'gy'), pairs)  1.54 us
  transfers between devices with their start and end apart: 10, of which 7 were waited for; matrix products, arithmetic and copies ran while one was open for 0% of the time, Pallas kernels for 1%

profile of v7, /device:TPU:1, one launch (start us, length us, event | category | flops | bytes accessed | tf_op | source)
XLA Modules:
  0.0 65.9 jit_solution(13388716139700859318)
XLA Ops:
  0.6 0.0 copy-start.1
  0.6 0.0 copy-start
  0.6 0.0 copy-start.2
  0.7 3.1 %shard_map.69 = (f32[55,16,128]{2,1,0:T(8,128)}, f32[38,16,128]{2,1,0:T(8,128)}, f32[512,128]{1,0:T(8,128)}, f32[344,128]{1,0:T(8,128)}) custom-call(f32[3,9,16,128]{3,2,1,0:T(8,128)} %load_hbm.1, s32[8,9,16,128]{3,2,1,0:T(8,128)} %flags_ref.3, f32[6,9,16,128]{3,2,1,0:T(8,128)} %flow_ref.3, s32[9,16]{1,0:T(8,128)} %active_hbm.1, f32[9,16]{1,0:T(8,128)} %die_hbm.1), custom_call_target="tpu_custom_call" | custom-call | tf_op jit(solution)/shard_map/pallas_call | solution.py:776
  3.7 2.5 %collective-permute-start.2 = (f32[512,128]{1,0:T(8,128)}, f32[512,128]{1,0:T(8,128)S(1)}, u32[]{:S(2)}, u32[]{:S(2)}) collective-permute-start(f32[512,128]{1,0:T(8,128)} %get-tuple-element.21), channel_id=1, source_target_pairs={{0,1},{1,2},{2,3},{3,4},{4,5},{5,6},{6,7},{7,8},{8,9},{9,10},{10,1... | collective-permute-start | bytes 786440 | tf_op jit(solution)/shard_map/ppermute | solution.py:739
  6.3 4.4 %collective-permute-start.3 = (f32[344,128]{1,0:T(8,128)}, f32[344,128]{1,0:T(8,128)S(1)}, u32[]{:S(2)}, u32[]{:S(2)}) collective-permute-start(f32[344,128]{1,0:T(8,128)} %get-tuple-element.22), channel_id=1, source_target_pairs={{0,15},{1,0},{2,1},{3,2},{4,3},{5,4},{6,5},{7,6},{8,7},{9,8},{10,9... | collective-permute-start | bytes 528392 | tf_op jit(solution)/shard_map/ppermute | solution.py:739
  10.7 2.1 %collective-permute-start = (f32[55,16,128]{2,1,0:T(8,128)}, f32[55,16,128]{2,1,0:T(8,128)S(1)}, u32[]{:S(2)}, u32[]{:S(2)}) collective-permute-start(f32[55,16,128]{2,1,0:T(8,128)} %get-tuple-element.19), channel_id=1, source_target_pairs={{0,16},{16,32},{32,48},{48,64},{64,80},{80,96},{96,112},{112,0},{1... | collective-permute-start | bytes 1351688 | tf_op jit(solution)/shard_map/ppermute | solution.py:739
  12.8 0.0 collective-permute-start.1
  12.8 1.3 %collective-permute-done.3.down_ref = f32[344,128]{1,0:T(8,128)S(1)} collective-permute-done((f32[344,128]{1,0:T(8,128)}, f32[344,128]{1,0:T(8,128)S(1)}, u32[]{:S(2)}, u32[]{:S(2)}) %collective-permute-start.3) | collective-permute-done | bytes 176160 | tf_op jit(solution)/shard_map/ppermute | solution.py:739
  14.1 2.7 %collective-permute-done.2.up_ref = f32[512,128]{1,0:T(8,128)S(1)} collective-permute-done((f32[512,128]{1,0:T(8,128)}, f32[512,128]{1,0:T(8,128)S(1)}, u32[]{:S(2)}, u32[]{:S(2)}) %collective-permute-start.2) | collective-permute-done | bytes 262176 | tf_op jit(solution)/shard_map/ppermute | solution.py:739
  16.8 2.4 %collective-permute-start.4 = (f32[296,128]{1,0:T(8,128)S(1)}, f32[296,128]{1,0:T(8,128)S(1)}, u32[]{:S(2)}, u32[]{:S(2)}) collective-permute-start(f32[296,128]{1,0:T(8,128)S(1)} %pad_maximum_fusion), channel_id=1, source_target_pairs={{0,16},{16,32},{32,48},{48,64},{64,80},{80,96},{96,112},{112,0},{1... | collective-permute-start | bytes 454664 | tf_op jit(solution)/shard_map/ppermute | solution.py:739
  19.3 0.0 collective-permute-start.5
  19.3 0.0 copy-start.3
  19.4 0.7 %copy-done.3 = s32[9,16]{1,0:T(8,128)S(1)} copy-done((s32[9,16]{1,0:T(8,128)S(1)}, s32[9,16]{1,0:T(8,128)}, u32[]{:S(2)}) %copy-start.3) | copy-done | bytes 600
  20.0 0.7 %copy-done.4 = f32[9,16]{1,0:T(8,128)S(1)} copy-done((f32[9,16]{1,0:T(8,128)S(1)}, f32[9,16]{1,0:T(8,128)}, u32[]{:S(2)}) %copy-start.4) | copy-done | bytes 600
  20.7 0.7 %shard_map.68 = (f32[3,10,24,128]{3,2,1,0:T(8,128)S(1)}, f32[9,16,128]{2,1,0:T(8,128)S(1)}) custom-call(f32[3,9,16,128]{3,2,1,0:T(8,128)S(1)} %copy-done.2, s32[8,9,16,128]{3,2,1,0:T(8,128)S(1)} %copy-done, f32[6,9,16,128]{3,2,1,0:T(8,128)S(1)} %copy-done.1, s32[9,16]{1,0:T(8,128)S(1)} %copy-done.3, f32[9,16]{1,0:T(8,128)S(1)} %copy-done.4), custom_call_target="tpu_custom_call" | custom-call | flops 400000 | bytes 1000 | tf_op jit(solution)/shard_map/pallas_call | solution.py:787
  21.5 0.0 collective-permute-done.1.right_ref
  21.5 2.4 %collective-permute-done.5.cr_ref = f32[280,128]{1,0:T(8,128)S(1)} collective-permute-done((f32[280,128]{1,0:T(8,128)S(1)}, f32[280,128]{1,0:T(8,128)S(1)}, u32[]{:S(2)}, u32[]{:S(2)}) %collective-permute-start.5) | collective-permute-done | bytes 143392 | tf_op jit(solution)/shard_map/ppermute | solution.py:739
  23.8 0.0 collective-permute-done.4.cl_ref
  23.8 0.0 collective-permute-done.left_ref
  23.8 7.0 %shard_map.70 = (f32[15,14,24,128]{3,2,1,0:T(8,128)S(1)}, f32[4,3,9,16,128]{4,3,2,1,0:T(8,128)S(1)}, f32[8,128]{1,0:T(8,128)S(1)}, f32[208,128]{1,0:T(8,128)S(1)...) custom-call(s32[8,9,16,128]{3,2,1,0:T(8,128)S(1)} %copy-done, ...), custom_call_target="tpu_custom_call" | custom-call | tf_op jit(solution)/shard_map/pallas_call | solution.py:792
  30.9 0.1 collective-permute-start.6
  30.9 0.5 collective-permute-start.7
  31.4 1.3 %collective-permute-done.6.left_ref = f32[208,128]{1,0:T(8,128)S(1)} collective-permute-done((f32[208,128]{1,0:T(8,128)S(1)}, f32[208,128]{1,0:T(8,128)S(1)}, u32[]{:S(2)}, u32[]{:S(2)}) %collective-permute-start.6) | collective-permute-done | bytes 106528 | tf_op jit(solution)/shard_map/ppermute | solution.py:739
  32.7 2.7 %collective-permute-done.7.right_ref = f32[208,128]{1,0:T(8,128)S(1)} collective-permute-done((f32[208,128]{1,0:T(8,128)S(1)}, f32[208,128]{1,0:T(8,128)S(1)}, u32[]{:S(2)}, u32[]{:S(2)}) %collective-permute-start.7) | collective-permute-done | bytes 106528 | tf_op jit(solution)/shard_map/ppermute | solution.py:739
  35.4 1.0 %collective-permute-start.8 = (f32[152,128]{1,0:T(8,128)S(1)}, f32[152,128]{1,0:T(8,128)S(1)}, u32[]{:S(2)}, u32[]{:S(2)}) collective-permute-start(f32[152,128]{1,0:T(8,128)S(1)} %pad_maximum_fusion.2), channel_id=1, source_target_pairs={{0,1},{1,2},{2,3},{3,4},{4,5},{5,6},{6,7},{7,8},{8,9},{9,10},{10,1... | collective-permute-start | bytes 233480 | tf_op jit(solution)/shard_map/ppermute | solution.py:750
  36.4 0.5 collective-permute-start.9
  36.9 1.8 %collective-permute-done.8.first_ref = f32[152,128]{1,0:T(8,128)S(1)} collective-permute-done((f32[152,128]{1,0:T(8,128)S(1)}, f32[152,128]{1,0:T(8,128)S(1)}, u32[]{:S(2)}, u32[]{:S(2)}) %collective-permute-start.8) | collective-permute-done | bytes 77856 | tf_op jit(solution)/shard_map/ppermute | solution.py:750
  38.7 0.1 collective-permute-done.9.second_ref
  38.8 6.6 %shard_map.71 = (f32[3,3,9,16,128]{4,3,2,1,0:T(8,128)S(1)}, f32[128,128]{1,0:T(8,128)S(1)}) custom-call(f32[15,14,24,128]{3,2,1,0:T(8,128)S(1)} %get-tuple-element.23.els_ref, f32[4,3,9,16,128]{4,3,2,1,0:T(8,128)S(1)} %get-tuple-element.24.own_ref, f32[8,128]{1,0:T(8,128)S(1)} %get-tuple-element.25.dots_ref, f32[208,128]{1,0:T(8,128)S(1)} %collective-permute-done.6.left_ref, ...), custom_call_target="tpu_custom_call" | custom-call | tf_op jit(solution)/shard_map/pallas_call | solution.py:799
  45.4 19.4 %all_to_all.11 = f32[128,1,128]{2,1,0:T(1,128)S(1)} all-to-all(f32[128,1,128]{2,1,0:T(1,128)S(1)} %bitcast.5), channel_id=1, replica_groups=mesh['gx'=8,'gy'=16] {'gx','gy'}, dimensions={0} | all-to-all | bytes 131072 | tf_op jit(solution)/shard_map/all_to_all | solution.py:802
  64.7 1.2 %shard_map.72 = (f32[3,9,16,128]{3,2,1,0:T(8,128)}, f32[3,9,16,128]{3,2,1,0:T(8,128)}) custom-call(f32[128,128]{1,0:T(8,128)S(1)} %bitcast.4, f32[4,3,9,16,128]{4,3,2,1,0:T(8,128)S(1)} %get-tuple-element.24.own_ref, f32[3,3,9,16,128]{4,3,2,1,0:T(8,128)S(1)} %get-tuple-element.31.tail_ref), custom_call_target="tpu_custom_call" | custom-call | tf_op jit(solution)/shard_map/pallas_call | solution.py:804
  (14 shorter events, 0.1 us)
Async XLA Ops:
  0.6 18.7 %copy-start.1 = (f32[6,9,16,128]{3,2,1,0:T(8,128)S(1)}, f32[6,9,16,128]{3,2,1,0:T(8,128)}, u32[]{:S(2)}) copy-start(f32[6,9,16,128]{3,2,1,0:T(8,128)} %flow_ref.3) | copy-start | bytes 1327108
  0.6 18.7 %copy-start = (s32[8,9,16,128]{3,2,1,0:T(8,128)S(1)}, s32[8,9,16,128]{3,2,1,0:T(8,128)}, u32[]{:S(2)}) copy-start(s32[8,9,16,128]{3,2,1,0:T(8,128)} %flags_ref.3) | copy-start | bytes 1769476
  0.6 18.7 %copy-start.2 = (f32[3,9,16,128]{3,2,1,0:T(8,128)S(1)}, f32[3,9,16,128]{3,2,1,0:T(8,128)}, u32[]{:S(2)}) copy-start(f32[3,9,16,128]{3,2,1,0:T(8,128)} %load_hbm.1) | copy-start | bytes 663556
  3.7 13.1 %collective-permute-start.2 = (f32[512,128]{1,0:T(8,128)}, f32[512,128]{1,0:T(8,128)S(1)}, u32[]{:S(2)}, u32[]{:S(2)}) collective-permute-start(f32[512,128]{1,0:T(8,128)} %get-tuple-element.21), channel_id=1, source_target_pairs={{0,1},{1,2},{2,3},{3,4},{4,5},{5,6},{6,7},{7,8},{8,9},{9,10},{10,1... | collective-permute-start | bytes 786440 | tf_op jit(solution)/shard_map/ppermute | solution.py:739
  6.3 7.8 %collective-permute-start.3 = (f32[344,128]{1,0:T(8,128)}, f32[344,128]{1,0:T(8,128)S(1)}, u32[]{:S(2)}, u32[]{:S(2)}) collective-permute-start(f32[344,128]{1,0:T(8,128)} %get-tuple-element.22), channel_id=1, source_target_pairs={{0,15},{1,0},{2,1},{3,2},{4,3},{5,4},{6,5},{7,6},{8,7},{9,8},{10,9... | collective-permute-start | bytes 528392 | tf_op jit(solution)/shard_map/ppermute | solution.py:739
  10.7 13.2 %collective-permute-start = (f32[55,16,128]{2,1,0:T(8,128)}, f32[55,16,128]{2,1,0:T(8,128)S(1)}, u32[]{:S(2)}, u32[]{:S(2)}) collective-permute-start(f32[55,16,128]{2,1,0:T(8,128)} %get-tuple-element.19), channel_id=1, source_target_pairs={{0,16},{16,32},{32,48},{48,64},{64,80},{80,96},{96,112},{112,0},{1... | collective-permute-start | bytes 1351688 | tf_op jit(solution)/shard_map/ppermute | solution.py:739
  12.8 8.7 %collective-permute-start.1 = (f32[38,16,128]{2,1,0:T(8,128)}, f32[38,16,128]{2,1,0:T(8,128)S(1)}, u32[]{:S(2)}, u32[]{:S(2)}) collective-permute-start(f32[38,16,128]{2,1,0:T(8,128)} %get-tuple-element.20), channel_id=1, source_target_pairs={{0,112},{16,0},{32,16},{48,32},{64,48},{80,64},{96,80},{112,96},{1... | collective-permute-start | bytes 933896 | tf_op jit(solution)/shard_map/ppermute | solution.py:739
  16.8 7.0 %collective-permute-start.4 = (f32[296,128]{1,0:T(8,128)S(1)}, f32[296,128]{1,0:T(8,128)S(1)}, u32[]{:S(2)}, u32[]{:S(2)}) collective-permute-start(f32[296,128]{1,0:T(8,128)S(1)} %pad_maximum_fusion), channel_id=1, source_target_pairs={{0,16},{16,32},{32,48},{48,64},{64,80},{80,96},{96,112},{112,0},{1... | collective-permute-start | bytes 454664 | tf_op jit(solution)/shard_map/ppermute | solution.py:739
  19.3 4.5 %collective-permute-start.5 = (f32[280,128]{1,0:T(8,128)S(1)}, f32[280,128]{1,0:T(8,128)S(1)}, u32[]{:S(2)}, u32[]{:S(2)}) collective-permute-start(f32[280,128]{1,0:T(8,128)S(1)} %pad_maximum_fusion.1), channel_id=1, source_target_pairs={{0,112},{16,0},{32,16},{48,32},{64,48},{80,64},{96,80},{112,96},{1... | collective-permute-start | bytes 430088 | tf_op jit(solution)/shard_map/ppermute | solution.py:739
  19.3 0.7 %copy-start.3 = (s32[9,16]{1,0:T(8,128)S(1)}, s32[9,16]{1,0:T(8,128)}, u32[]{:S(2)}) copy-start(s32[9,16]{1,0:T(8,128)} %active_hbm.1) | copy-start | bytes 1732
  20.0 0.7 %copy-start.4 = (f32[9,16]{1,0:T(8,128)S(1)}, f32[9,16]{1,0:T(8,128)}, u32[]{:S(2)}) copy-start(f32[9,16]{1,0:T(8,128)} %die_hbm.1) | copy-start | bytes 1732
  30.9 1.8 %collective-permute-start.6 = (f32[208,128]{1,0:T(8,128)S(1)}, f32[208,128]{1,0:T(8,128)S(1)}, u32[]{:S(2)}, u32[]{:S(2)}) collective-permute-start(f32[208,128]{1,0:T(8,128)S(1)} %get-tuple-element.26), channel_id=1, source_target_pairs={{0,16},{16,32},{32,48},{48,64},{64,80},{80,96},{96,112},{112,0},{1... | collective-permute-start | bytes 319496 | tf_op jit(solution)/shard_map/ppermute | solution.py:739
  30.9 4.4 %collective-permute-start.7 = (f32[208,128]{1,0:T(8,128)S(1)}, f32[208,128]{1,0:T(8,128)S(1)}, u32[]{:S(2)}, u32[]{:S(2)}) collective-permute-start(f32[208,128]{1,0:T(8,128)S(1)} %get-tuple-element.27), channel_id=1, source_target_pairs={{0,112},{16,0},{32,16},{48,32},{64,48},{80,64},{96,80},{112,96},{1... | collective-permute-start | bytes 319496 | tf_op jit(solution)/shard_map/ppermute | solution.py:739
  35.4 3.3 %collective-permute-start.8 = (f32[152,128]{1,0:T(8,128)S(1)}, f32[152,128]{1,0:T(8,128)S(1)}, u32[]{:S(2)}, u32[]{:S(2)}) collective-permute-start(f32[152,128]{1,0:T(8,128)S(1)} %pad_maximum_fusion.2), channel_id=1, source_target_pairs={{0,1},{1,2},{2,3},{3,4},{4,5},{5,6},{6,7},{7,8},{8,9},{9,10},{10,1... | collective-permute-start | bytes 233480 | tf_op jit(solution)/shard_map/ppermute | solution.py:750
  36.4 2.4 %collective-permute-start.9 = (f32[152,128]{1,0:T(8,128)S(1)}, f32[152,128]{1,0:T(8,128)S(1)}, u32[]{:S(2)}, u32[]{:S(2)}) collective-permute-start(f32[152,128]{1,0:T(8,128)S(1)} %pad_maximum_fusion.3), channel_id=1, source_target_pairs={{0,16},{1,0},{2,1},{3,2},{4,3},{5,4},{6,5},{7,6},{8,7},{9,8},{10,9... | collective-permute-start | bytes 233480 | tf_op jit(solution)/shard_map/ppermute | solution.py:750
